TPU v7x, 32 devices: a whole 2x2x4 slice. The times are simulated.
32 devices in a mesh: ctx: 4 (over y, x), head: 4 (over z), var: 2 (over core).
Axes of the slice: x: 2, y: 2, z: 4, core: 2. Of those that a mesh axis runs over, the one named last changes fastest.
Arguments:
- sequence: bfloat16 [2048, 1536], P('ctx', 'head'), may hold values from -8 to 8
- deletions: int32 [8, 2], P('var'), parts along dimension 0, may hold values from 0 to 2048, as said below
- conv_taps: float32 [3, 1536], P(None, 'head'), may hold values from -3 to 3
- conv_bias: float32 [1536], P('head'), may hold values from -3 to 3
- w_proj: bfloat16 [1536, 3584], P(None, 'head'), may hold values from -1 to 1
- w_out: bfloat16 [1536, 1536], P('head'), may hold values from -0.15625 to 0.15625
- w_pair: bfloat16 [1536, 256], P('head'), may hold values from -0.15625 to 0.15625
- dist_table: float32 [16, 128], replicated, may hold values from -3 to 3
Outputs:
- pair_map: bfloat16 [8, 512, 512, 128], P('var', 'ctx', 'head'), parts along dimension 0
There are 2 independent parts, one for each index of `var`. A program takes and returns all parts, laid end to end along the dimension named above; an argument that names none is the same for every part. Nothing has to cross between parts.
Inputs may be any that keep to these rules, and one draw needn't show every extreme that they name: `deletions`: each variant deletes 1 to 128 consecutive tokens, some variant deletes exactly 128, and some variant's deletion ends at the last token of the locus.
All inputs are finite; a program needn't handle non-finite values.
Results may differ from a plain program's by a relative error of at most 0.025.
Values may be sent and summed in bfloat16 or wider, within the bound.
No kernel may reach another device: no remote copies, remote signals or barrier semaphores. Data moves between devices by JAX's collectives and lax.ppermute only.
A program may use at most 128 MiB of HBM per device.

v0:
```python
import functools
import math

import jax
import jax.numpy as jnp
from jax import lax
from jax.experimental import pallas as pl
from jax.experimental.pallas import tpu as pltpu
from jax.sharding import PartitionSpec as P

HD = 128
VD = 192
VP = 256
C = 128
NB = 16
POOL = 4
WIN = 160
ALIGN = 32
CHUNK = 512
SHIFTS = 16
ROWS = 16
MIB = 1024 * 1024
QSCALE = math.log2(math.e) / math.sqrt(HD)
GELU_A = math.sqrt(2.0 / math.pi)
GELU_B = GELU_A * 0.044715


def trunk_of(taps, low, middle, high):
    convolved = taps[0:1] * low + taps[1:2] * middle + taps[2:3] * high + taps[3:4]
    half = 0.5 * convolved
    bent = jnp.tanh(convolved * (GELU_A + GELU_B * (convolved * convolved)))
    return middle + (half + half * bent)


def pool_matrix(count):
    wide = lax.broadcasted_iota(jnp.int32, (count // POOL, count), 1) // POOL
    tall = lax.broadcasted_iota(jnp.int32, (count // POOL, count), 0)
    return jnp.where(wide == tall, 1.0 / POOL, 0.0).astype(jnp.bfloat16)


def project_kernel(heads, n_var, n_head, count, scalars, w_proj, *refs):
    taps, pieces = refs[:n_head], refs[n_head : n_head + 2 * count]
    out, pooled_out, given, weights, rows, left, right, sems = refs[n_head + 2 * count :]
    step, width = pieces[0].shape[1:]
    tokens = rows.shape[1] - 2 * step
    size = step // POOL
    ours, core, first, last = (scalars[k] for k in range(4))

    given_copy = pltpu.make_async_copy(w_proj, given, sems.at[2 * count, 0])
    given_copy.start()
    copies = []
    for index, piece in enumerate(pieces):
        half = core if index < count else 1 - core
        at = pl.multiple_of((scalars[4 + index % count] * n_var + half + 1) * step, step)
        for s in range(n_head):
            copy = pltpu.make_async_copy(
                piece.at[s], rows.at[s, pl.ds(at, step)], sems.at[index, s]
            )
            copy.start()
            copies.append(copy)
    rows[:, 0:step] = jnp.zeros((n_head, step, width), jnp.bfloat16)
    rows[:, tokens + step :] = jnp.zeros((n_head, step, width), jnp.bfloat16)
    columns = weights.shape[1]
    given_copy.wait()
    for s, back in enumerate(head_order(n_head)):
        source = pl.ds(pl.multiple_of(lax.rem(ours + n_head - back, n_head) * width, ALIGN), width)
        into = slice(s * width, (s + 1) * width)
        for h in range(heads):
            low, key, value = h * (2 * HD + VD), h * HD, heads * HD + h * VP
            query = heads * (HD + VP) + h * HD
            weights[into, key : key + HD] = given[source, low + HD : low + 2 * HD]
            weights[into, value : value + VD] = given[source, low + 2 * HD : low + 2 * HD + VD]
            weights[into, value + VD : value + VP] = jnp.zeros((width, VP - VD), jnp.bfloat16)
            weights[into, query : query + HD] = given[source, low : low + HD]
    at = lax.broadcasted_iota(jnp.int32, (1, columns), 1)
    ones = jnp.zeros((1, columns), jnp.float32)
    scale = jnp.where(at >= heads * (HD + VP), QSCALE, 1.0)
    for h in range(heads):
        ones = jnp.where(at == heads * HD + h * VP + VD, 1.0, ones)
    low_taps = [tap[...].astype(jnp.bfloat16) for tap in taps]
    for copy in copies:
        copy.wait()

    def make(stage, into):
        for part in range(2):
            start = (stage * 2 + part) * step
            for s in range(n_head):
                into[part * step : (part + 1) * step, s * width : (s + 1) * width] = trunk_of(
                    low_taps[s],
                    *(
                        rows[s, pl.ds(pl.multiple_of(start + shift, step), step), :]
                        for shift in (0, step, 2 * step)
                    ),
                )

    def product_of(block):
        product = jnp.dot(block, weights[...], preferred_element_type=jnp.float32)
        return (product * scale + ones).astype(jnp.bfloat16)

    def project(stage, block):
        product = product_of(block[...])
        for part in range(2):
            at = stage * 2 + part
            rows_here = slice(part * step, (part + 1) * step)
            out[pl.ds(pl.multiple_of(at * step, step), step)] = product[rows_here]
            pooled_out[pl.ds(pl.multiple_of(at * size, size), size)] = jnp.dot(
                pool_matrix(step), block[rows_here, 0:width], preferred_element_type=jnp.float32
            )

    def window(index):
        start = (first // ALIGN) * ALIGN + (index - 1) * step
        return pl.multiple_of(jnp.clip(start, 0, tokens - WIN), ALIGN)

    def make_windows(into):
        for index in range(3):
            start = window(index)
            at = start + lax.broadcasted_iota(jnp.int32, (WIN, 1), 0)
            kept = [
                jnp.where(
                    jnp.logical_or(at + shift < first, at + shift >= last), 1.0, 0.0
                ).astype(jnp.bfloat16)
                for shift in (-step, 0, step)
            ]
            for s in range(n_head):
                into[index * WIN : (index + 1) * WIN, s * width : (s + 1) * width] = trunk_of(
                    low_taps[s],
                    *(
                        rows[s, pl.ds(pl.multiple_of(start + shift, ALIGN), WIN), :] * keep
                        for shift, keep in zip((0, step, 2 * step), kept)
                    ),
                )

    stages = tokens // (2 * step)
    make(0, left)

    def two_stages(n, carry):
        make(2 * n + 1, right)
        project(2 * n, left)
        make(2 * n + 2, left)
        project(2 * n + 1, right)
        return carry

    if stages > 2:
        lax.fori_loop(0, stages // 2 - 1, two_stages, 0)
    make(stages - 1, right)
    project(stages - 2, left)
    make_windows(left)
    project(stages - 1, right)
    product = product_of(left[0 : 3 * WIN])
    for index in range(3):
        rows_here = slice(index * WIN, (index + 1) * WIN)
        out[pl.ds(window(index), WIN)] = product[rows_here]
        small = pl.multiple_of(window(index) // POOL, ALIGN // POOL)
        pooled_out[pl.ds(small, WIN // POOL)] = jnp.dot(
            pool_matrix(WIN), left[rows_here, 0:width], preferred_element_type=jnp.float32
        )


def attend_kernel(
    heads, own, order, kvq, pooled, w_mix, w_pair,
    out, scores_a, scores_b, top_a, top_b, total,
):
    tokens = kvq.shape[0]
    chunk = scores_a.shape[2]
    steps = tokens // chunk
    key_cols, value_cols = heads * HD, heads * (HD + VP)
    pool = pool_matrix(own)
    scores, tops = (scores_a, scores_b), (top_a, top_b)
    chains = [(n, h) for n in range(out.shape[0]) for h in range(heads)]

    def score(index, c):
        n, h = chains[index]
        low = value_cols + h * HD
        found = lax.dot_general(
            kvq[pl.ds(pl.multiple_of(order[n] * own, own), own), low : low + HD],
            kvq[pl.ds(pl.multiple_of(c * chunk, chunk), chunk), h * HD : (h + 1) * HD],
            (((1,), (1,)), ((), ())),
            preferred_element_type=jnp.float32,
        )
        scores[index % 2][c] = found
        best = found[:, 0:128]
        for low in range(128, chunk, 128):
            best = jnp.maximum(best, found[:, low : low + 128])
        top = tops[index % 2]
        top[...] = jnp.maximum(top[...], best)

    def clear(index):
        tops[index % 2][...] = jnp.full(top_a.shape, -jnp.inf, jnp.float32)

    clear(0)

    def first_scores(c, carry):
        score(0, c)
        return carry

    lax.fori_loop(0, steps, first_scores, 0)
    for index, (n, h) in enumerate(chains):
        more = index + 1 < len(chains)
        if more:
            clear(index + 1)
        row_max = jnp.max(tops[index % 2][...], axis=1, keepdims=True)
        total[...] = jnp.zeros(total.shape, jnp.float32)
        low = key_cols + h * VP

        def weigh(c, carry):
            weights = jnp.exp2((scores[index % 2][c] - row_max).astype(jnp.bfloat16))
            if more:
                score(index + 1, c)
            total[...] += jnp.dot(
                weights,
                kvq[pl.ds(pl.multiple_of(c * chunk, chunk), chunk), low : low + VP],
                preferred_element_type=jnp.float32,
            )
            return carry

        lax.fori_loop(0, steps, weigh, 0)
        mixed = total[...]
        mixed = (mixed * (1.0 / mixed[:, VD : VD + 1])).astype(jnp.bfloat16)
        mixed = jnp.dot(pool, mixed, preferred_element_type=jnp.float32).astype(jnp.bfloat16)
        if h == 0:
            size = own // POOL
            pair = jnp.dot(
                pooled[pl.ds(pl.multiple_of(order[n] * size, size), size)].astype(jnp.bfloat16),
                w_pair[...],
                preferred_element_type=jnp.float32,
            )
        pair = pair + jnp.dot(mixed, w_mix[h], preferred_element_type=jnp.float32)
        if h == heads - 1:
            out[n] = pair.astype(out.dtype)


def pair_kernel(variants, order, table, *refs):
    row_feats = refs[:variants]
    col_feats = refs[variants : 2 * variants]
    out, rows, cols, blocks, sems = refs[2 * variants :]
    side = cols.shape[1]
    count = rows.shape[1]
    for s in range(variants):
        rows[order[s]] = row_feats[s][...].astype(jnp.float32)
        cols[order[variants + s]] = col_feats[s][...]

    def write(block, slot, variant):
        into = out.at[variant, pl.ds(block * ROWS, ROWS)]
        return pltpu.make_async_copy(blocks.at[slot, variant], into, sems.at[slot, variant])

    def one_block(block, carry):
        slot = lax.rem(block, 2)
        for variant in range(variants):
            pl.when(block >= 2)(write(block, slot, variant).wait)
            for r in range(ROWS):
                back = count - 1 - (block * ROWS + r)
                low = pl.multiple_of((back // SHIFTS) * SHIFTS, SHIFTS)
                relative = table[(count - 1 - r) % SHIFTS, pl.ds(low, side), :]
                row = rows[variant, pl.ds(block * ROWS + r, 1), :]
                row = jnp.broadcast_to(row, (SHIFTS, C)).astype(jnp.bfloat16)
                found = (cols[variant] + relative).reshape(side // SHIFTS, SHIFTS, C) + row[None]
                blocks[slot, variant, r] = found.reshape(side, C)
            write(block, slot, variant).start()
        return carry

    total = count // ROWS
    lax.fori_loop(0, total, one_block, 0)
    for block in range(max(total - 2, 0), total):
        for variant in range(variants):
            write(block, block % 2, variant).wait()


def distance_table(dist_table, row_start, col_start, rows, cols):
    at = jnp.arange(SHIFTS, dtype=jnp.int32)[:, None] + jnp.arange(
        rows + cols, dtype=jnp.int32
    )
    distance = jnp.abs(row_start - col_start + rows - 1 - at)
    buckets = jnp.zeros(distance.shape, jnp.int32)
    for power_index in range(NB - 1):
        buckets = buckets + (distance >= 2**power_index).astype(jnp.int32)
    one_hot = (buckets[:, :, None] == jnp.arange(NB, dtype=jnp.int32)).astype(jnp.float32)
    return jnp.einsum("skb,bc->skc", one_hot, dist_table, precision=lax.Precision.HIGHEST).astype(
        jnp.bfloat16
    )


def whole(memory=pltpu.VMEM):
    return pl.BlockSpec(memory_space=memory)


def shifts(array, axis):
    size = lax.axis_size(axis)
    return [array] + [
        lax.ppermute(array, axis, [(k, (k + s) % size) for k in range(size)])
        for s in range(1, size)
    ]


def head_order(n_head):
    return [0, 1, 3, 2] if n_head == 4 else list(range(n_head))


def gather_rows(block, taps, n_ctx, n_var, n_head, core):
    crossing = lambda array: lax.ppermute(array, "var", [(0, 1), (1, 0)])
    if n_ctx == 4 and n_head == 4 and n_var == 2:
        shift = lambda array, s: lax.ppermute(array, "head", [(k, (k + s) % 4) for k in range(4)])
        over = lambda array, bit: lax.ppermute(array, "ctx", [(k, k ^ bit) for k in range(4)])
        near = jnp.stack([block, shift(block, 1), shift(block, 3)])
        far = shift(block, 2)[None]
        slab, over_x, over_y = (
            jnp.concatenate(pair)
            for pair in (
                (near, far), (over(near, 1), over(far, 1)), (over(near, 2), over(far, 2))
            )
        )
        pairs = [(2 * k + c, 2 * (k ^ (c + 1)) + c) for k in range(4) for c in range(2)]
        corner = lax.ppermute(jnp.where(core == 0, over_y, over_x), ("ctx", "var"), pairs)
        pieces = [slab, over_x, over_y]
        corner, crossed, taps = lax.optimization_barrier(
            (corner, [crossing(piece) for piece in pieces], shifts(taps, "head"))
        )
        return pieces + [corner], crossed + [crossing(corner)], taps
    pieces = shifts(jnp.stack(shifts(block, "head")), "ctx")
    crossed = [crossing(piece) for piece in pieces]
    return pieces, crossed, shifts(taps, "head")


def local(sequence, deletions, conv_taps, conv_bias, w_proj, w_out, w_pair, dist_table):
    own, width = sequence.shape
    variants = deletions.shape[0]
    heads = w_out.shape[0] // VD
    n_ctx, n_head, n_var = (lax.axis_size(name) for name in ("ctx", "head", "var"))
    if n_ctx != n_head or n_var != 2 or n_ctx % variants:
        raise ValueError("mesh shape")
    step = own // n_var
    tokens = n_ctx * own
    pair_rows = own // POOL
    columns = heads * (2 * HD + VP)
    splits = n_ctx // variants
    mine, ours, core = (lax.axis_index(name) for name in ("ctx", "head", "var"))

    half = lax.dynamic_slice_in_dim(sequence, core * step, step, 0)
    taps = jnp.concatenate([conv_taps, conv_bias[None]], 0)
    pieces, crossed, taps = gather_rows(half, taps, n_ctx, n_var, n_head, core)
    if n_ctx == 4 and n_head == 4:
        blocks = [mine, mine ^ 1, mine ^ 2, mine ^ 3]
    else:
        blocks = [(mine + n_ctx - s) % n_ctx for s in range(n_ctx)]
    scalars = jnp.concatenate(
        [
            jnp.stack([ours, core]).astype(jnp.int32),
            lax.dynamic_index_in_dim(deletions, mine // splits, 0, keepdims=False),
            jnp.stack(blocks).astype(jnp.int32),
        ]
    )
    kvq, pooled = pl.pallas_call(
        functools.partial(project_kernel, heads, n_var, n_head, len(pieces)),
        out_shape=(
            jax.ShapeDtypeStruct((tokens, columns), jnp.bfloat16),
            jax.ShapeDtypeStruct((tokens // POOL, width), jnp.float32),
        ),
        in_specs=[whole(pltpu.SMEM), whole(pltpu.HBM)]
        + [whole()] * n_head
        + [whole(pltpu.HBM)] * (2 * len(pieces)),
        out_specs=(whole(), whole()),
        scratch_shapes=[
            pltpu.VMEM(w_proj.shape, jnp.bfloat16),
            pltpu.VMEM((n_head * width, columns), jnp.bfloat16),
            pltpu.VMEM((n_head, tokens + 2 * step, width), jnp.bfloat16),
            pltpu.VMEM((2 * step, n_head * width), jnp.bfloat16),
            pltpu.VMEM((2 * step, n_head * width), jnp.bfloat16),
            pltpu.SemaphoreType.DMA((2 * len(pieces) + 1, n_head)),
        ],
        compiler_params=pltpu.CompilerParams(vmem_limit_bytes=(34 if splits == 1 else 52) * MIB),
        cost_estimate=pl.CostEstimate(
            flops=2 * (tokens + 3 * WIN) * n_head * width * columns,
            bytes_accessed=4 * tokens * n_head * width,
            transcendentals=tokens * n_head * width,
        ),
        name="project",
    )(
        scalars, w_proj, *(taps[s] for s in head_order(n_head)), *pieces, *crossed
    )
    pair_parts, pooled = lax.optimization_barrier((shifts(w_pair, "head"), pooled))
    w_mix = jnp.zeros((heads * VD, 2 * C), jnp.float32)
    for s, part in enumerate(pair_parts):
        from_head = (ours + n_head - s) % n_head
        w_mix += jnp.dot(
            lax.dynamic_slice_in_dim(w_out, from_head * width, width, 1),
            part,
            preferred_element_type=jnp.float32,
        )
    w_mix = w_mix.astype(jnp.bfloat16).reshape(heads, VD, 2 * C)
    w_mix = jnp.pad(w_mix, ((0, 0), (0, VP - VD), (0, 0)))
    table = distance_table(dist_table, mine * pair_rows, ours * pair_rows, pair_rows, pair_rows)

    chunk = min(tokens, CHUNK)

    def attend(order, dtype):
        count = order.shape[0]
        return pl.pallas_call(
            functools.partial(attend_kernel, heads, own),
            out_shape=jax.ShapeDtypeStruct((count, pair_rows, 2 * C), dtype),
            in_specs=[whole(pltpu.SMEM)] + [whole()] * 4,
            out_specs=whole(),
            scratch_shapes=[
                pltpu.VMEM((tokens // chunk, own, chunk), jnp.float32),
                pltpu.VMEM((tokens // chunk, own, chunk), jnp.float32),
                pltpu.VMEM((own, 128), jnp.float32),
                pltpu.VMEM((own, 128), jnp.float32),
                pltpu.VMEM((own, VP), jnp.float32),
            ],
            compiler_params=pltpu.CompilerParams(vmem_limit_bytes=(20 if splits == 1 else 52) * MIB),
            cost_estimate=pl.CostEstimate(
                flops=2 * count * heads * own * tokens * (2 * HD + VP),
                bytes_accessed=2 * tokens * columns,
                transcendentals=count * heads * own * tokens,
            ),
            name="attend",
        )(order.astype(jnp.int32), kvq, pooled, w_mix, w_pair)

    if splits == 1:
        sent = attend((ours + jnp.arange(1, n_head)) % n_head, jnp.bfloat16)
        last_block, table = lax.optimization_barrier((ours[None], table))
        summed = attend(last_block, jnp.float32)[0]
        for s in range(1, n_head):
            pairs = [(k, (k + s) % n_head) for k in range(n_head)]
            summed += lax.ppermute(sent[s - 1], "head", pairs).astype(jnp.float32)
        turned = lax.ppermute(
            summed[:, :C].astype(jnp.bfloat16),
            ("ctx", "head"),
            [(i * n_head + h, h * n_head + i) for i in range(n_ctx) for h in range(n_head)],
        )
        row_feats = shifts(turned, "head")
        col_feats = shifts(summed[:, C:].astype(jnp.bfloat16), "ctx")
        order = [(at + n_ctx - s) % n_ctx for at in (ours, mine) for s in range(variants)]
    else:
        blocks_here = n_ctx // splits
        part = attend((mine % splits) * blocks_here + jnp.arange(blocks_here), jnp.bfloat16)
        feats = lax.all_gather(lax.psum(part, "head"), "ctx", axis=0, tiled=False)
        feats = feats.reshape(variants, n_ctx, pair_rows, 2 * C)
        row_feats = lax.dynamic_index_in_dim(feats, mine, 1, keepdims=False)[:, :, :C]
        col_feats = lax.dynamic_index_in_dim(feats, ours, 1, keepdims=False)[:, :, C:]
        row_feats, col_feats = list(row_feats), list(col_feats)
        order = list(range(variants)) * 2

    return pl.pallas_call(
        functools.partial(pair_kernel, variants),
        out_shape=jax.ShapeDtypeStruct((variants, pair_rows, pair_rows, C), jnp.bfloat16),
        in_specs=[whole(pltpu.SMEM)] + [whole()] * (1 + 2 * variants),
        out_specs=whole(pl.ANY),
        scratch_shapes=[
            pltpu.VMEM((variants, pair_rows, C), jnp.float32),
            pltpu.VMEM((variants, pair_rows, C), jnp.bfloat16),
            pltpu.VMEM((2, variants, ROWS, pair_rows, C), jnp.bfloat16),
            pltpu.SemaphoreType.DMA((2, variants)),
        ],
        compiler_params=pltpu.CompilerParams(vmem_limit_bytes=24 * MIB),
        name="pair_map",
    )(jnp.stack(order).astype(jnp.int32) if splits == 1 else jnp.array(order, jnp.int32),
      table, *row_feats, *col_feats)


def solution(mesh):
    in_specs = (
        P("ctx", "head"),
        P("var", None),
        P(None, "head"),
        P("head"),
        P(None, "head"),
        P("head", None),
        P("head", None),
        P(),
    )
    out_specs = P("var", "ctx", "head", None)
    return jax.shard_map(local, mesh=mesh, in_specs=in_specs, out_specs=out_specs, check_vma=False)
```

profile of v0, /device:TPU:0, one launch (start us, length us, event | category | flops | bytes accessed | tf_op | source)
XLA Modules:
  0.0 139.6 jit_solution(5171896538065434497)
XLA Ops:
  0.0 1.0 constant_dynamic-slice_fusion
  1.0 5.1 %collective-permute-start.1 = (bf16[256,384]{1,0:T(8,128)(2,1)S(1)}, bf16[256,384]{1,0:T(8,128)(2,1)S(1)}, u32[]{:S(2)}, u32[]{:S(2)}) collective-permute-start(bf16[256,384]{1,0:T(8,128)(2,1)S(1)} %constant_dynamic-slice_fusion), channel_id=1, source_target_pairs={{0,6},{2,0},{4,2},{6,4},{1,7},{3,1},{5,3},{7,5},{8,14},{10,8},{12,... | collective-permute-start | bytes 589832 | tf_op jit(solution)/shard_map/ppermute | solution.py:301
  6.2 0.9 fusion.41
  7.1 4.4 %collective-permute-done.1 = bf16[256,384]{1,0:T(8,128)(2,1)S(1)} collective-permute-done((bf16[256,384]{1,0:T(8,128)(2,1)S(1)}, bf16[256,384]{1,0:T(8,128)(2,1)S(1)}, u32[]{:S(2)}, u32[]{:S(2)}) %collective-permute-start.1) | collective-permute-done | bytes 196640 | tf_op jit(solution)/shard_map/ppermute | solution.py:301
  11.5 4.0 %collective-permute-done = bf16[256,384]{1,0:T(8,128)(2,1)S(1)} collective-permute-done((bf16[256,384]{1,0:T(8,128)(2,1)S(1)}, bf16[256,384]{1,0:T(8,128)(2,1)S(1)}, u32[]{:S(2)}, u32[]{:S(2)}) %collective-permute-start) | collective-permute-done | bytes 196640 | tf_op jit(solution)/shard_map/ppermute | solution.py:301
  15.5 1.6 %collective-permute-start.5 = (bf16[3,256,384]{2,1,0:T(8,128)(2,1)S(1)}, bf16[3,256,384]{2,1,0:T(8,128)(2,1)S(1)}, u32[]{:S(2)}, u32[]{:S(2)}) collective-permute-start(bf16[3,256,384]{2,1,0:T(8,128)(2,1)S(1)} %pad_maximum_fusion.1), channel_id=1, source_target_pairs={{0,8},{8,0},{16,24},{24,16},{1,9},{9,1},{17,25},{25,17},{2,10},{10... | collective-permute-start | bytes 1769480 | tf_op jit(solution)/shard_map/ppermute | solution.py:302
  17.1 1.5 %collective-permute-start.2 = (bf16[3,256,384]{2,1,0:T(8,128)(2,1)S(1)}, bf16[3,256,384]{2,1,0:T(8,128)(2,1)}, u32[]{:S(2)}, u32[]{:S(2)}) collective-permute-start(bf16[3,256,384]{2,1,0:T(8,128)(2,1)S(1)} %pad_maximum_fusion.1), channel_id=1, source_target_pairs={{0,16},{8,24},{16,0},{24,8},{1,17},{9,25},{17,1},{25,9},{2,18},{10... | collective-permute-start | bytes 1769480 | tf_op jit(solution)/shard_map/ppermute | solution.py:302
  18.6 0.7 collective-permute-start.3
  19.3 9.7 %collective-permute-done.3 = bf16[256,384]{1,0:T(8,128)(2,1)S(1)} collective-permute-done((bf16[256,384]{1,0:T(8,128)(2,1)S(1)}, bf16[256,384]{1,0:T(8,128)(2,1)S(1)}, u32[]{:S(2)}, u32[]{:S(2)}) %collective-permute-start.3) | collective-permute-done | bytes 196640 | tf_op jit(solution)/shard_map/ppermute | solution.py:301
  29.0 0.5 collective-permute-start.6
  30.4 4.4 %collective-permute-done.6 = bf16[1,256,384]{2,1,0:T(8,128)(2,1)S(1)} collective-permute-done((bf16[1,256,384]{2,1,0:T(8,128)(2,1)S(1)}, bf16[1,256,384]{2,1,0:T(8,128)(2,1)S(1)}, u32[]{:S(2)}, u32[]{:S(2)}) %collective-permute-start.6) | collective-permute-done | bytes 196640 | tf_op jit(solution)/shard_map/ppermute | solution.py:302
  34.8 1.4 %constant_dynamic-update-slice_fusion.1 = bf16[4,256,384]{2,1,0:T(8,128)(2,1)S(1)} fusion(bf16[3,256,384]{2,1,0:T(8,128)(2,1)} %collective-permute-done.2), kind=kLoop, calls=%fused_computation.42 | loop fusion | bytes 1179648
  36.5 0.9 collective-permute-start.7
  37.9 1.3 collective-permute-start.13
  39.2 2.3 %collective-permute-done.13.refs_2_ = f32[4,384]{1,0:T(4,128)S(1)} collective-permute-done((f32[4,384]{1,0:T(4,128)S(1)}, f32[4,384]{1,0:T(4,128)S(1)}, u32[]{:S(2)}, u32[]{:S(2)}) %collective-permute-start.13) | collective-permute-done | bytes 6176 | tf_op jit(solution)/shard_map/ppermute | solution.py:289
  41.6 0.7 collective-permute-start.12
  42.3 3.8 %collective-permute-done.12.refs_3_ = f32[4,384]{1,0:T(4,128)S(1)} collective-permute-done((f32[4,384]{1,0:T(4,128)S(1)}, f32[4,384]{1,0:T(4,128)S(1)}, u32[]{:S(2)}, u32[]{:S(2)}) %collective-permute-start.12) | collective-permute-done | bytes 6176 | tf_op jit(solution)/shard_map/ppermute | solution.py:289
  46.1 1.6 %collective-permute-start.11 = (f32[4,384]{1,0:T(4,128)S(1)}, f32[4,384]{1,0:T(4,128)S(1)}, u32[]{:S(2)}, u32[]{:S(2)}) collective-permute-start(f32[4,384]{1,0:T(4,128)S(1)} %pad_maximum_fusion.2.refs_0_), channel_id=1, source_target_pairs={{0,2},{2,4},{4,6},{6,0},{1,3},{3,5},{5,7},{7,1},{8,10},{10,12},{12... | collective-permute-start | bytes 18440 | tf_op jit(solution)/shard_map/ppermute | solution.py:289
  47.7 3.9 %collective-permute-done.11.refs_1_ = f32[4,384]{1,0:T(4,128)S(1)} collective-permute-done((f32[4,384]{1,0:T(4,128)S(1)}, f32[4,384]{1,0:T(4,128)S(1)}, u32[]{:S(2)}, u32[]{:S(2)}) %collective-permute-start.11) | collective-permute-done | bytes 6176 | tf_op jit(solution)/shard_map/ppermute | solution.py:289
  51.5 0.9 copy-done.7
  52.4 0.9 copy-done.9
  53.3 0.9 copy-done.11
  54.2 1.3 collective-permute-start.17
  55.5 0.7 collective-permute-start.15
  56.3 1.8 %convolution_convert_fusion.table = bf16[16,256,128]{2,1,0:T(8,128)(2,1)S(1)} fusion(s32[16,256]{1,0:T(8,128)S(1)} %convert_add_fusion, f32[16,128]{1,0:T(8,128)S(1)} %copy-done.13), kind=kOutput, calls=%fused_computation | convolution fusion | flops 101253120 | bytes 1073152 | tf_op jit(solution)/shard_map/skb,bc->skc/dot_general | solution.py:277
  58.4 1.1 copy-done.2
  59.5 1.1 copy-done.4
  60.7 1.8 %copy-done.6 = bf16[1536,896]{1,0:T(8,128)(2,1)S(1)} copy-done((bf16[1536,896]{1,0:T(8,128)(2,1)S(1)}, bf16[1536,896]{1,0:T(8,128)(2,1)}, u32[]{:S(2)}) %copy-start.6) | copy-done | bytes 2752536
  62.5 1.1 copy-done.8
  63.6 1.1 copy-done.10
  64.7 1.1 copy-done.12
  65.9 20.7 %project.1 = (bf16[2048,1024]{1,0:T(8,128)(2,1)S(1)}, f32[512,384]{1,0:T(8,128)S(1)}) custom-call(s32[8]{0:T(128)S(1)} %concatenate.16.scalars, bf16[1536,896]{1,0:T(8,128)(2,1)S(1)} %copy-done.6, f32[4,384]{1,0:T(4,128)S(1)} %pad_maximum_fusion.2.refs_0_, f32[4,384]{1,0:T(4,128)S(1)} %collective-permute-done.11.refs_1_, ...), custom_call_target="tpu_custom_call" | custom-call | flops 7952400384 | bytes 12582912 | tf_op jit(solution)/shard_map/project/pallas_call | solution.py:351
  86.6 1.2 fusion.7
  87.8 1.2 fusion.5
  89.5 15.5 %attend.3 = bf16[3,128,256]{2,1,0:T(8,128)(2,1)S(1)} custom-call(s32[3]{0:T(128)S(1)} %and_select_fusion.order, bf16[2048,1024]{1,0:T(8,128)(2,1)S(1)} %get-tuple-element.32.kvq, f32[512,384]{1,0:T(8,128)S(1)} %get-tuple-element.34.pooled, bf16[2,256,256]{2,1,0:T(8,128)(2,1)S(1)} %pad.4.w_mix, bf16[384,256]{1,0:T(8,128)(2,1)S(1)} %copy-done.5), custom_call_target="tpu_custom_call" | custom-call | flops 6442450944 | bytes 4194304 | tf_op jit(solution)/shard_map/attend/pallas_call | solution.py:396
  105.1 2.8 %collective-permute-start.18 = (bf16[128,256]{1,0:T(8,128)(2,1)S(1)}, bf16[128,256]{1,0:T(8,128)(2,1)S(1)}, u32[]{:S(2)}, u32[]{:S(2)}) collective-permute-start(bf16[128,256]{1,0:T(8,128)(2,1)S(1)} %get-tuple-element.39), channel_id=1, source_target_pairs={{0,2},{2,4},{4,6},{6,0},{1,3},{3,5},{5,7},{7,1},{8,10},{10,12},{12... | collective-permute-start | bytes 196616 | tf_op jit(solution)/shard_map/ppermute | solution.py:423
  107.9 1.1 collective-permute-start.20
  108.9 1.1 collective-permute-start.19
  110.1 5.4 %attend.2 = f32[1,128,256]{2,1,0:T(8,128)S(1)} custom-call(s32[1]{0:T(128)} %bitcast.8.order, bf16[2048,1024]{1,0:T(8,128)(2,1)S(1)} %get-tuple-element.32.kvq, f32[512,384]{1,0:T(8,128)S(1)} %get-tuple-element.34.pooled, bf16[2,256,256]{2,1,0:T(8,128)(2,1)S(1)} %pad.4.w_mix, bf16[384,256]{1,0:T(8,128)(2,1)S(1)} %copy-done.5), custom_call_target="tpu_custom_call" | custom-call | flops 2147483648 | bytes 4194304 | tf_op jit(solution)/shard_map/attend/pallas_call | solution.py:396
  115.5 0.7 collective-permute-start.21
  116.2 5.9 %collective-permute-start.27 = (bf16[128,128]{1,0:T(8,128)(2,1)S(1)}, bf16[128,128]{1,0:T(8,128)(2,1)S(1)}, u32[]{:S(2)}, u32[]{:S(2)}) collective-permute-start(bf16[128,128]{1,0:T(8,128)(2,1)S(1)} %get-tuple-element.42.refs_4_), channel_id=1, source_target_pairs={{0,24},{8,0},{16,8},{24,16},{1,25},{9,1},{17,9},{25,17},{2,26},{10... | collective-permute-start | bytes 98312 | tf_op jit(solution)/shard_map/ppermute | solution.py:289
  122.1 0.7 collective-permute-start.25
  122.8 4.3 %collective-permute-start.24 = (bf16[128,128]{1,0:T(8,128)(2,1)S(1)}, bf16[128,128]{1,0:T(8,128)(2,1)S(1)}, u32[]{:S(2)}, u32[]{:S(2)}) collective-permute-start(bf16[128,128]{1,0:T(8,128)(2,1)S(1)} %collective-permute-done.21.refs_0_), channel_id=1, source_target_pairs={{0,6},{2,0},{4,2},{6,4},{1,7},{3,1},{5,3},{7,5},{8,14},{10,8},{12,... | collective-permute-start | bytes 98312 | tf_op jit(solution)/shard_map/ppermute | solution.py:289
  127.2 0.6 collective-permute-start.22
  127.8 0.9 collective-permute-done.24.refs_3_
  128.7 3.2 %collective-permute-done.23.refs_2_ = bf16[128,128]{1,0:T(8,128)(2,1)S(1)} collective-permute-done((bf16[128,128]{1,0:T(8,128)(2,1)S(1)}, bf16[128,128]{1,0:T(8,128)(2,1)S(1)}, u32[]{:S(2)}, u32[]{:S(2)}) %collective-permute-start.23) | collective-permute-done | bytes 32800 | tf_op jit(solution)/shard_map/ppermute | solution.py:289
  132.0 0.9 collective-permute-done.22.refs_1_
  132.9 6.6 %pair_map.1 = bf16[4,128,128,128]{3,2,1,0:T(8,128)(2,1)} custom-call(s32[8]{0:T(128)S(1)} %stack.63.order, bf16[16,256,128]{2,1,0:T(8,128)(2,1)S(1)} %convolution_convert_fusion.table, bf16[128,128]{1,0:T(8,128)(2,1)S(1)} %collective-permute-done.21.refs_0_, bf16[128,128]{1,0:T(8,128)(2,1)S(1)} %collective-permute-done.22.refs_1_, ...), custom_call_target="tpu_custom_call" | custom-call | tf_op jit(solution)/shard_map/pair_map/pallas_call | solution.py:442
  (71 shorter events, 2.6 us)
Async XLA Ops:
  0.0 86.6 %copy-start = (bf16[384,1536]{1,0:T(8,128)(2,1)S(1)}, bf16[384,1536]{1,0:T(8,128)(2,1)}, u32[]{:S(2)}) copy-start(bf16[384,1536]{1,0:T(8,128)(2,1)} %param.13) | copy-start | bytes 3538948
  1.0 10.4 %collective-permute-start.1 = (bf16[256,384]{1,0:T(8,128)(2,1)S(1)}, bf16[256,384]{1,0:T(8,128)(2,1)S(1)}, u32[]{:S(2)}, u32[]{:S(2)}) collective-permute-start(bf16[256,384]{1,0:T(8,128)(2,1)S(1)} %constant_dynamic-slice_fusion), channel_id=1, source_target_pairs={{0,6},{2,0},{4,2},{6,4},{1,7},{3,1},{5,3},{7,5},{8,14},{10,8},{12,... | collective-permute-start | bytes 589832 | tf_op jit(solution)/shard_map/ppermute | solution.py:301
  6.2 9.3 %collective-permute-start = (bf16[256,384]{1,0:T(8,128)(2,1)S(1)}, bf16[256,384]{1,0:T(8,128)(2,1)S(1)}, u32[]{:S(2)}, u32[]{:S(2)}) collective-permute-start(bf16[256,384]{1,0:T(8,128)(2,1)S(1)} %constant_dynamic-slice_fusion), channel_id=1, source_target_pairs={{0,2},{2,4},{4,6},{6,0},{1,3},{3,5},{5,7},{7,1},{8,10},{10,12},{12... | collective-permute-start | bytes 589832 | tf_op jit(solution)/shard_map/ppermute | solution.py:301
  15.5 14.8 %collective-permute-start.5 = (bf16[3,256,384]{2,1,0:T(8,128)(2,1)S(1)}, bf16[3,256,384]{2,1,0:T(8,128)(2,1)S(1)}, u32[]{:S(2)}, u32[]{:S(2)}) collective-permute-start(bf16[3,256,384]{2,1,0:T(8,128)(2,1)S(1)} %pad_maximum_fusion.1), channel_id=1, source_target_pairs={{0,8},{8,0},{16,24},{24,16},{1,9},{9,1},{17,25},{25,17},{2,10},{10... | collective-permute-start | bytes 1769480 | tf_op jit(solution)/shard_map/ppermute | solution.py:302
  17.1 17.7 %collective-permute-start.2 = (bf16[3,256,384]{2,1,0:T(8,128)(2,1)S(1)}, bf16[3,256,384]{2,1,0:T(8,128)(2,1)}, u32[]{:S(2)}, u32[]{:S(2)}) collective-permute-start(bf16[3,256,384]{2,1,0:T(8,128)(2,1)S(1)} %pad_maximum_fusion.1), channel_id=1, source_target_pairs={{0,16},{8,24},{16,0},{24,8},{1,17},{9,25},{17,1},{25,9},{2,18},{10... | collective-permute-start | bytes 1769480 | tf_op jit(solution)/shard_map/ppermute | solution.py:302
  18.6 10.4 %collective-permute-start.3 = (bf16[256,384]{1,0:T(8,128)(2,1)S(1)}, bf16[256,384]{1,0:T(8,128)(2,1)S(1)}, u32[]{:S(2)}, u32[]{:S(2)}) collective-permute-start(bf16[256,384]{1,0:T(8,128)(2,1)S(1)} %constant_dynamic-slice_fusion), channel_id=1, source_target_pairs={{0,4},{2,6},{4,0},{6,2},{1,5},{3,7},{5,1},{7,3},{8,12},{10,14},{12... | collective-permute-start | bytes 589832 | tf_op jit(solution)/shard_map/ppermute | solution.py:301
  29.0 5.8 %collective-permute-start.6 = (bf16[1,256,384]{2,1,0:T(8,128)(2,1)S(1)}, bf16[1,256,384]{2,1,0:T(8,128)(2,1)S(1)}, u32[]{:S(2)}, u32[]{:S(2)}) collective-permute-start(bf16[1,256,384]{2,1,0:T(8,128)(2,1)S(1)} %bitcast.46), channel_id=1, source_target_pairs={{0,8},{8,0},{16,24},{24,16},{1,9},{9,1},{17,25},{25,17},{2,10},{10... | collective-permute-start | bytes 589832 | tf_op jit(solution)/shard_map/ppermute | solution.py:302
  29.5 6.7 %collective-permute-start.4 = (bf16[1,256,384]{2,1,0:T(8,128)(2,1)S(1)}, bf16[1,256,384]{2,1,0:T(8,128)(2,1)S(1)}, u32[]{:S(2)}, u32[]{:S(2)}) collective-permute-start(bf16[1,256,384]{2,1,0:T(8,128)(2,1)S(1)} %bitcast.47), channel_id=1, source_target_pairs={{0,16},{8,24},{16,0},{24,8},{1,17},{9,25},{17,1},{25,9},{2,18},{10... | collective-permute-start | bytes 589832 | tf_op jit(solution)/shard_map/ppermute | solution.py:302
  30.2 6.1 %copy-start.3 = (bf16[4,256,384]{2,1,0:T(8,128)(2,1)}, bf16[4,256,384]{2,1,0:T(8,128)(2,1)S(1)}, u32[]{:S(2)}) copy-start(bf16[4,256,384]{2,1,0:T(8,128)(2,1)S(1)} %pad_maximum_fusion.refs_4_) | copy-start | bytes 2359300
  30.2 21.3 %collective-permute-start.8 = (bf16[4,256,384]{2,1,0:T(8,128)(2,1)S(1)}, bf16[4,256,384]{2,1,0:T(8,128)(2,1)S(1)}, u32[]{:S(2)}, u32[]{:S(2)}) collective-permute-start(bf16[4,256,384]{2,1,0:T(8,128)(2,1)S(1)} %pad_maximum_fusion.refs_4_), channel_id=1, source_target_pairs={{0,1},{1,0},{2,3},{3,2},{4,5},{5,4},{6,7},{7,6},{8,9},{9,8},{10,11... | collective-permute-start | bytes 2359304 | tf_op jit(solution)/shard_map/ppermute | solution.py:299
  34.8 2.5 %copy-start.1 = (bf16[4,256,384]{2,1,0:T(8,128)(2,1)}, bf16[4,256,384]{2,1,0:T(8,128)(2,1)S(1)}, u32[]{:S(2)}) copy-start(bf16[4,256,384]{2,1,0:T(8,128)(2,1)S(1)} %constant_dynamic-update-slice_fusion.2.refs_5_) | copy-start | bytes 2359300
  36.3 1.6 %copy-start.15 = (f32[384]{0:T(512)S(1)}, f32[384]{0:T(512)}, u32[]{:S(2)}) copy-start(f32[384]{0:T(512)} %param.11) | copy-start | bytes 4612
  36.3 1.6 %copy-start.14 = (f32[3,384]{1,0:T(4,128)S(1)}, f32[3,384]{1,0:T(4,128)}, u32[]{:S(2)}) copy-start(f32[3,384]{1,0:T(4,128)} %param.10) | copy-start | bytes 13828
  36.3 17.9 %copy-start.5 = (bf16[384,256]{1,0:T(8,128)(2,1)S(1)}, bf16[384,256]{1,0:T(8,128)(2,1)}, u32[]{:S(2)}) copy-start(bf16[384,256]{1,0:T(8,128)(2,1)} %w_pair.3) | copy-start | bytes 589828
  36.3 19.9 %copy-start.13 = (f32[16,128]{1,0:T(8,128)S(1)}, f32[16,128]{1,0:T(8,128)}, u32[]{:S(2)}) copy-start(f32[16,128]{1,0:T(8,128)} %param.15) | copy-start | bytes 24580
  36.4 21.7 %copy-start.16 = (s32[4,2]{0,1:T(2,128)S(1)}, s32[4,2]{0,1:T(2,128)}, u32[]{:S(2)}) copy-start(s32[4,2]{0,1:T(2,128)} %param.9) | copy-start | bytes 100
  36.5 15.9 %collective-permute-start.7 = (bf16[4,256,384]{2,1,0:T(8,128)(2,1)S(1)}, bf16[4,256,384]{2,1,0:T(8,128)(2,1)}, u32[]{:S(2)}, u32[]{:S(2)}) collective-permute-start(bf16[4,256,384]{2,1,0:T(8,128)(2,1)S(1)} %broadcast_select_fusion), channel_id=1, source_target_pairs={{0,8},{1,17},{8,0},{9,25},{16,24},{17,1},{24,16},{25,9},{2,10},{3,... | collective-permute-start | bytes 2359304 | tf_op jit(solution)/shard_map/ppermute | solution.py:312
  37.3 15.1 %collective-permute-start.10 = (bf16[4,256,384]{2,1,0:T(8,128)(2,1)S(1)}, bf16[4,256,384]{2,1,0:T(8,128)(2,1)S(1)}, u32[]{:S(2)}, u32[]{:S(2)}) collective-permute-start(bf16[4,256,384]{2,1,0:T(8,128)(2,1)S(1)} %constant_dynamic-update-slice_fusion.refs_6_), channel_id=1, source_target_pairs={{0,1},{1,0},{2,3},{3,2},{4,5},{5,4},{6,7},{7,6},{8,9},{9,8},{10,11... | collective-permute-start | bytes 2359304 | tf_op jit(solution)/shard_map/ppermute | solution.py:299
  37.3 16.0 %collective-permute-start.9 = (bf16[4,256,384]{2,1,0:T(8,128)(2,1)S(1)}, bf16[4,256,384]{2,1,0:T(8,128)(2,1)S(1)}, u32[]{:S(2)}, u32[]{:S(2)}) collective-permute-start(bf16[4,256,384]{2,1,0:T(8,128)(2,1)S(1)} %constant_dynamic-update-slice_fusion.2.refs_5_), channel_id=1, source_target_pairs={{0,1},{1,0},{2,3},{3,2},{4,5},{5,4},{6,7},{7,6},{8,9},{9,8},{10,11... | collective-permute-start | bytes 2359304 | tf_op jit(solution)/shard_map/ppermute | solution.py:299
  37.9 3.7 %collective-permute-start.13 = (f32[4,384]{1,0:T(4,128)S(1)}, f32[4,384]{1,0:T(4,128)S(1)}, u32[]{:S(2)}, u32[]{:S(2)}) collective-permute-start(f32[4,384]{1,0:T(4,128)S(1)} %pad_maximum_fusion.2.refs_0_), channel_id=1, source_target_pairs={{0,6},{2,0},{4,2},{6,4},{1,7},{3,1},{5,3},{7,5},{8,14},{10,8},{12,... | collective-permute-start | bytes 18440 | tf_op jit(solution)/shard_map/ppermute | solution.py:289
  41.6 4.5 %collective-permute-start.12 = (f32[4,384]{1,0:T(4,128)S(1)}, f32[4,384]{1,0:T(4,128)S(1)}, u32[]{:S(2)}, u32[]{:S(2)}) collective-permute-start(f32[4,384]{1,0:T(4,128)S(1)} %pad_maximum_fusion.2.refs_0_), channel_id=1, source_target_pairs={{0,4},{2,6},{4,0},{6,2},{1,5},{3,7},{5,1},{7,3},{8,12},{10,14},{12... | collective-permute-start | bytes 18440 | tf_op jit(solution)/shard_map/ppermute | solution.py:289
  46.1 5.4 %collective-permute-start.11 = (f32[4,384]{1,0:T(4,128)S(1)}, f32[4,384]{1,0:T(4,128)S(1)}, u32[]{:S(2)}, u32[]{:S(2)}) collective-permute-start(f32[4,384]{1,0:T(4,128)S(1)} %pad_maximum_fusion.2.refs_0_), channel_id=1, source_target_pairs={{0,2},{2,4},{4,6},{6,0},{1,3},{3,5},{5,7},{7,1},{8,10},{10,12},{12... | collective-permute-start | bytes 18440 | tf_op jit(solution)/shard_map/ppermute | solution.py:289
  51.5 0.9 copy-start.7
  52.4 0.9 copy-start.9
  53.3 0.9 copy-start.11
  54.2 4.2 %collective-permute-start.14 = (bf16[4,256,384]{2,1,0:T(8,128)(2,1)}, bf16[4,256,384]{2,1,0:T(8,128)(2,1)}, u32[]{:S(2)}, u32[]{:S(2)}) collective-permute-start(bf16[4,256,384]{2,1,0:T(8,128)(2,1)} %collective-permute-done.7.refs_7_), channel_id=1, source_target_pairs={{0,1},{1,0},{2,3},{3,2},{4,5},{5,4},{6,7},{7,6},{8,9},{9,8},{10,11... | collective-permute-start | bytes 2359304 | tf_op jit(solution)/shard_map/ppermute | solution.py:299
  54.2 32.4 %collective-permute-start.17 = (bf16[384,256]{1,0:T(8,128)(2,1)S(1)}, bf16[384,256]{1,0:T(8,128)(2,1)S(1)}, u32[]{:S(2)}, u32[]{:S(2)}) collective-permute-start(bf16[384,256]{1,0:T(8,128)(2,1)S(1)} %copy-done.5), channel_id=1, source_target_pairs={{0,6},{2,0},{4,2},{6,4},{1,7},{3,1},{5,3},{7,5},{8,14},{10,8},{12,... | collective-permute-start | bytes 589832 | tf_op jit(solution)/shard_map/ppermute | solution.py:289
  55.5 31.1 %collective-permute-start.16 = (bf16[384,256]{1,0:T(8,128)(2,1)S(1)}, bf16[384,256]{1,0:T(8,128)(2,1)}, u32[]{:S(2)}, u32[]{:S(2)}) collective-permute-start(bf16[384,256]{1,0:T(8,128)(2,1)S(1)} %copy-done.5), channel_id=1, source_target_pairs={{0,4},{2,6},{4,0},{6,2},{1,5},{3,7},{5,1},{7,3},{8,12},{10,14},{12... | collective-permute-start | bytes 589832 | tf_op jit(solution)/shard_map/ppermute | solution.py:289
  55.5 31.1 %collective-permute-start.15 = (bf16[384,256]{1,0:T(8,128)(2,1)S(1)}, bf16[384,256]{1,0:T(8,128)(2,1)}, u32[]{:S(2)}, u32[]{:S(2)}) collective-permute-start(bf16[384,256]{1,0:T(8,128)(2,1)S(1)} %copy-done.5), channel_id=1, source_target_pairs={{0,2},{2,4},{4,6},{6,0},{1,3},{3,5},{5,7},{7,1},{8,10},{10,12},{12... | collective-permute-start | bytes 589832 | tf_op jit(solution)/shard_map/ppermute | solution.py:289
  58.4 1.1 copy-start.2
  59.5 1.1 copy-start.4
  60.7 1.8 %copy-start.6 = (bf16[1536,896]{1,0:T(8,128)(2,1)S(1)}, bf16[1536,896]{1,0:T(8,128)(2,1)}, u32[]{:S(2)}) copy-start(bf16[1536,896]{1,0:T(8,128)(2,1)} %w_proj.1) | copy-start | bytes 8257540
  62.5 1.1 copy-start.8
  63.6 1.1 copy-start.10
  64.7 1.1 copy-start.12
  105.1 10.4 %collective-permute-start.18 = (bf16[128,256]{1,0:T(8,128)(2,1)S(1)}, bf16[128,256]{1,0:T(8,128)(2,1)S(1)}, u32[]{:S(2)}, u32[]{:S(2)}) collective-permute-start(bf16[128,256]{1,0:T(8,128)(2,1)S(1)} %get-tuple-element.39), channel_id=1, source_target_pairs={{0,2},{2,4},{4,6},{6,0},{1,3},{3,5},{5,7},{7,1},{8,10},{10,12},{12... | collective-permute-start | bytes 196616 | tf_op jit(solution)/shard_map/ppermute | solution.py:423
  107.9 7.6 %collective-permute-start.20 = (bf16[128,256]{1,0:T(8,128)(2,1)S(1)}, bf16[128,256]{1,0:T(8,128)(2,1)S(1)}, u32[]{:S(2)}, u32[]{:S(2)}) collective-permute-start(bf16[128,256]{1,0:T(8,128)(2,1)S(1)} %get-tuple-element.40), channel_id=1, source_target_pairs={{0,6},{2,0},{4,2},{6,4},{1,7},{3,1},{5,3},{7,5},{8,14},{10,8},{12,... | collective-permute-start | bytes 196616 | tf_op jit(solution)/shard_map/ppermute | solution.py:423
  108.9 6.5 %collective-permute-start.19 = (bf16[128,256]{1,0:T(8,128)(2,1)S(1)}, bf16[128,256]{1,0:T(8,128)(2,1)S(1)}, u32[]{:S(2)}, u32[]{:S(2)}) collective-permute-start(bf16[128,256]{1,0:T(8,128)(2,1)S(1)} %get-tuple-element.41), channel_id=1, source_target_pairs={{0,4},{2,6},{4,0},{6,2},{1,5},{3,7},{5,1},{7,3},{8,12},{10,14},{12... | collective-permute-start | bytes 196616 | tf_op jit(solution)/shard_map/ppermute | solution.py:423
  115.5 7.3 %collective-permute-start.21 = (bf16[128,128]{1,0:T(8,128)(2,1)S(1)}, bf16[128,128]{1,0:T(8,128)(2,1)S(1)}, u32[]{:S(2)}, u32[]{:S(2)}) collective-permute-start(bf16[128,128]{1,0:T(8,128)(2,1)S(1)} %get-tuple-element.43), channel_id=1, source_target_pairs={{0,0},{2,8},{4,16},{6,24},{8,2},{10,10},{12,18},{14,26},{16,4},{18... | collective-permute-start | bytes 98312 | tf_op jit(solution)/shard_map/ppermute | solution.py:424
  116.2 10.9 %collective-permute-start.27 = (bf16[128,128]{1,0:T(8,128)(2,1)S(1)}, bf16[128,128]{1,0:T(8,128)(2,1)S(1)}, u32[]{:S(2)}, u32[]{:S(2)}) collective-permute-start(bf16[128,128]{1,0:T(8,128)(2,1)S(1)} %get-tuple-element.42.refs_4_), channel_id=1, source_target_pairs={{0,24},{8,0},{16,8},{24,16},{1,25},{9,1},{17,9},{25,17},{2,26},{10... | collective-permute-start | bytes 98312 | tf_op jit(solution)/shard_map/ppermute | solution.py:289
  122.1 5.7 %collective-permute-start.26 = (bf16[128,128]{1,0:T(8,128)(2,1)S(1)}, bf16[128,128]{1,0:T(8,128)(2,1)S(1)}, u32[]{:S(2)}, u32[]{:S(2)}) collective-permute-start(bf16[128,128]{1,0:T(8,128)(2,1)S(1)} %get-tuple-element.42.refs_4_), channel_id=1, source_target_pairs={{0,16},{8,24},{16,0},{24,8},{1,17},{9,25},{17,1},{25,9},{2,18},{10... | collective-permute-start | bytes 98312 | tf_op jit(solution)/shard_map/ppermute | solution.py:289
  122.1 5.7 %collective-permute-start.25 = (bf16[128,128]{1,0:T(8,128)(2,1)S(1)}, bf16[128,128]{1,0:T(8,128)(2,1)S(1)}, u32[]{:S(2)}, u32[]{:S(2)}) collective-permute-start(bf16[128,128]{1,0:T(8,128)(2,1)S(1)} %get-tuple-element.42.refs_4_), channel_id=1, source_target_pairs={{0,8},{8,16},{16,24},{24,0},{1,9},{9,17},{17,25},{25,1},{2,10},{10... | collective-permute-start | bytes 98312 | tf_op jit(solution)/shard_map/ppermute | solution.py:289
  122.8 5.9 %collective-permute-start.24 = (bf16[128,128]{1,0:T(8,128)(2,1)S(1)}, bf16[128,128]{1,0:T(8,128)(2,1)S(1)}, u32[]{:S(2)}, u32[]{:S(2)}) collective-permute-start(bf16[128,128]{1,0:T(8,128)(2,1)S(1)} %collective-permute-done.21.refs_0_), channel_id=1, source_target_pairs={{0,6},{2,0},{4,2},{6,4},{1,7},{3,1},{5,3},{7,5},{8,14},{10,8},{12,... | collective-permute-start | bytes 98312 | tf_op jit(solution)/shard_map/ppermute | solution.py:289
  127.1 4.8 %collective-permute-start.23 = (bf16[128,128]{1,0:T(8,128)(2,1)S(1)}, bf16[128,128]{1,0:T(8,128)(2,1)S(1)}, u32[]{:S(2)}, u32[]{:S(2)}) collective-permute-start(bf16[128,128]{1,0:T(8,128)(2,1)S(1)} %collective-permute-done.21.refs_0_), channel_id=1, source_target_pairs={{0,4},{2,6},{4,0},{6,2},{1,5},{3,7},{5,1},{7,3},{8,12},{10,14},{12... | collective-permute-start | bytes 98312 | tf_op jit(solution)/shard_map/ppermute | solution.py:289
  127.2 5.7 %collective-permute-start.22 = (bf16[128,128]{1,0:T(8,128)(2,1)S(1)}, bf16[128,128]{1,0:T(8,128)(2,1)S(1)}, u32[]{:S(2)}, u32[]{:S(2)}) collective-permute-start(bf16[128,128]{1,0:T(8,128)(2,1)S(1)} %collective-permute-done.21.refs_0_), channel_id=1, source_target_pairs={{0,2},{2,4},{4,6},{6,0},{1,3},{3,5},{5,7},{7,1},{8,10},{10,12},{12... | collective-permute-start | bytes 98312 | tf_op jit(solution)/shard_map/ppermute | solution.py:289
where the time goes:
time: 140 us
  Pallas kernels  48.1 us (34%)
  waiting for transfers between devices  37.5 us (27%)
  starting transfers between devices  34.3 us (24%)
  local copies, waits for them, and re-layouts  14 us (10%)
  matrix products  4.7 us (3%)
    pallas_call x2, Pallas kernels, attend(): pl.pallas_call(functools.partial(attend_kernel, heads, own), out_shape=ja...  20.9 us
    pallas_call x1, Pallas kernels, local(): pl.pallas_call(functools.partial(project_kernel, heads, n_var, n_head, le...  20.7 us
    ppermute x3, waiting for transfers between devices, gather_rows(): lax.ppermute(array, 'head', [(k, (k + s) % 4) for k in range(4)])  18 us
    ppermute x12, starting transfers between devices, shifts(): lax.ppermute(array, axis, [(k, (k + s) % size) for k in range(size)])  17.2 us
    ppermute x12, waiting for transfers between devices, shifts(): lax.ppermute(array, axis, [(k, (k + s) % size) for k in range(size)])  15 us
    unnamed x36, local copies, waits for them, and re-layouts  11.6 us
    pallas_call x1, Pallas kernels, local(): pl.pallas_call(functools.partial(pair_kernel, variants), out_shape=jax.Sh...  6.56 us
    ppermute x3, starting transfers between devices, gather_rows(): lax.ppermute(array, 'head', [(k, (k + s) % 4) for k in range(4)])  5.84 us
  transfers between devices with their start and end apart: 28, of which 10 were waited for; matrix products, arithmetic and copies ran while one was open for 4% of the time, Pallas kernels for 19%

commit v1 on v0

--- a/solution.py
+++ b/solution.py
@@ -156,10 +156,27 @@
         )
 
 
-def attend_kernel(
-    heads, own, order, kvq, pooled, w_mix, w_pair,
-    out, scores_a, scores_b, top_a, top_b, total,
-):
+def attend_kernel(heads, own, given, order, kvq, pooled, *refs):
+    mixing, out = refs[:given], refs[given]
+    *mix_out, scores_a, scores_b, top_a, top_b, total, parts = refs[given + 1 :]
+    if mix_out:
+        w_out, w_pair = mixing[:2]
+        (w_mix,) = mix_out
+        width = w_pair.shape[0]
+        for s in range(given - 1):
+            parts[order[out.shape[0] + s]] = mixing[1 + s][...]
+        for h in range(heads):
+            mix = jnp.zeros((VD, w_pair.shape[1]), jnp.float32)
+            for k in range(given - 1):
+                mix += jnp.dot(
+                    w_out[h * VD : (h + 1) * VD, k * width : (k + 1) * width],
+                    parts[k],
+                    preferred_element_type=jnp.float32,
+                )
+            w_mix[h, 0:VD] = mix.astype(jnp.bfloat16)
+            w_mix[h, VD:] = jnp.zeros((VP - VD, w_pair.shape[1]), jnp.bfloat16)
+    else:
+        w_mix, w_pair = mixing
     tokens = kvq.shape[0]
     chunk = scores_a.shape[2]
     steps = tokens // chunk
@@ -277,6 +294,10 @@
     return jnp.einsum("skb,bc->skc", one_hot, dist_table, precision=lax.Precision.HIGHEST).astype(
         jnp.bfloat16
     )
+
+
+def in_hbm(array):
+    return pltpu.with_memory_space_constraint(array, pltpu.HBM)
 
 
 def whole(memory=pltpu.VMEM):
@@ -374,50 +395,54 @@
         ),
         name="project",
     )(
-        scalars, w_proj, *(taps[s] for s in head_order(n_head)), *pieces, *crossed
+        scalars,
+        in_hbm(w_proj),
+        *(taps[s] for s in head_order(n_head)),
+        *(in_hbm(piece) for piece in pieces + crossed),
     )
-    pair_parts, pooled = lax.optimization_barrier((shifts(w_pair, "head"), pooled))
-    w_mix = jnp.zeros((heads * VD, 2 * C), jnp.float32)
-    for s, part in enumerate(pair_parts):
-        from_head = (ours + n_head - s) % n_head
-        w_mix += jnp.dot(
-            lax.dynamic_slice_in_dim(w_out, from_head * width, width, 1),
-            part,
-            preferred_element_type=jnp.float32,
-        )
-    w_mix = w_mix.astype(jnp.bfloat16).reshape(heads, VD, 2 * C)
-    w_mix = jnp.pad(w_mix, ((0, 0), (0, VP - VD), (0, 0)))
     table = distance_table(dist_table, mine * pair_rows, ours * pair_rows, pair_rows, pair_rows)
 
     chunk = min(tokens, CHUNK)
 
-    def attend(order, dtype):
+    pair_parts = shifts(w_pair, "head")
+    order_of_parts = [(ours + n_head - s) % n_head for s in range(n_head)]
+
+    def attend(order, dtype, w_mix):
         count = order.shape[0]
+        mix_shape = jax.ShapeDtypeStruct((heads, VP, 2 * C), jnp.bfloat16)
+        out_shape = [jax.ShapeDtypeStruct((count, pair_rows, 2 * C), dtype)]
+        if w_mix is None:
+            mixing, out_shape = [w_out, *pair_parts], out_shape + [mix_shape]
+            order = jnp.concatenate([order, jnp.stack(order_of_parts)])
+        else:
+            mixing = [w_mix, w_pair]
         return pl.pallas_call(
-            functools.partial(attend_kernel, heads, own),
-            out_shape=jax.ShapeDtypeStruct((count, pair_rows, 2 * C), dtype),
-            in_specs=[whole(pltpu.SMEM)] + [whole()] * 4,
-            out_specs=whole(),
+            functools.partial(attend_kernel, heads, own, len(mixing)),
+            out_shape=out_shape,
+            in_specs=[whole(pltpu.SMEM)] + [whole()] * (2 + len(mixing)),
+            out_specs=[whole()] * len(out_shape),
             scratch_shapes=[
                 pltpu.VMEM((tokens // chunk, own, chunk), jnp.float32),
                 pltpu.VMEM((tokens // chunk, own, chunk), jnp.float32),
                 pltpu.VMEM((own, 128), jnp.float32),
                 pltpu.VMEM((own, 128), jnp.float32),
                 pltpu.VMEM((own, VP), jnp.float32),
+                pltpu.VMEM((n_head, width, 2 * C), jnp.bfloat16),
             ],
-            compiler_params=pltpu.CompilerParams(vmem_limit_bytes=(20 if splits == 1 else 52) * MIB),
+            compiler_params=pltpu.CompilerParams(
+                vmem_limit_bytes=(22 if splits == 1 else 52) * MIB
+            ),
             cost_estimate=pl.CostEstimate(
                 flops=2 * count * heads * own * tokens * (2 * HD + VP),
                 bytes_accessed=2 * tokens * columns,
                 transcendentals=count * heads * own * tokens,
             ),
             name="attend",
-        )(order.astype(jnp.int32), kvq, pooled, w_mix, w_pair)
+        )(order.astype(jnp.int32), kvq, pooled, *mixing)
 
     if splits == 1:
-        sent = attend((ours + jnp.arange(1, n_head)) % n_head, jnp.bfloat16)
-        last_block, table = lax.optimization_barrier((ours[None], table))
-        summed = attend(last_block, jnp.float32)[0]
+        sent, w_mix = attend((ours + jnp.arange(1, n_head)) % n_head, jnp.bfloat16, None)
+        summed = attend(ours[None], jnp.float32, w_mix)[0][0]
         for s in range(1, n_head):
             pairs = [(k, (k + s) % n_head) for k in range(n_head)]
             summed += lax.ppermute(sent[s - 1], "head", pairs).astype(jnp.float32)
@@ -431,7 +456,8 @@
         order = [(at + n_ctx - s) % n_ctx for at in (ours, mine) for s in range(variants)]
     else:
         blocks_here = n_ctx // splits
-        part = attend((mine % splits) * blocks_here + jnp.arange(blocks_here), jnp.bfloat16)
+        here = (mine % splits) * blocks_here + jnp.arange(blocks_here)
+        part = attend(here, jnp.bfloat16, None)[0]
         feats = lax.all_gather(lax.psum(part, "head"), "ctx", axis=0, tiled=False)
         feats = feats.reshape(variants, n_ctx, pair_rows, 2 * C)
         row_feats = lax.dynamic_index_in_dim(feats, mine, 1, keepdims=False)[:, :, :C]

time: 140 us -> 121 us (0.86)
  local copies, waits for them, and re-layouts: 14 us -> 3.15 us
  Pallas kernels: 48.1 us -> 44.1 us
  matrix products: 4.7 us -> 1.81 us
    unnamed x36 -> x28, local copies, waits for them, and re-layouts: 11.6 us -> 2.59 us
    pallas_call x1, Pallas kernels: 20.7 us -> 16.3 us  [local(): pl.pallas_call(functools.partial(project_kernel, heads, n_var, n_head, le...]
    dot_general x4 -> x0, matrix products: 2.89 us -> none  [local(): jnp.dot(lax.dynamic_slice_in_dim(w_out, from_head * width, width, 1), par...]
    ppermute x4, waiting for transfers between devices: 4.42 us -> 2.6 us  [gather_rows(): lax.ppermute(array, 'ctx', [(k, k ^ bit) for k in range(4)])]
    ppermute x12, starting transfers between devices: 17.2 us -> 15.6 us  [shifts(): lax.ppermute(array, axis, [(k, (k + s) % size) for k in range(size)])]
  transfers between devices with their start and end apart: 28 -> 28, of which waited for: 10 -> 10; matrix products, arithmetic and copies ran while one was open for 4% -> 4% of each run, Pallas kernels for 19% -> 18%
where the time goes in v1:
time: 121 us
  Pallas kernels  44.1 us (36%)
  waiting for transfers between devices  36.7 us (30%)
  starting transfers between devices  33 us (27%)
  local copies, waits for them, and re-layouts  3.15 us (3%)
  matrix products  1.81 us (1%)
  other arithmetic  1.35 us (1%)
    pallas_call x2, Pallas kernels, attend(): pl.pallas_call(functools.partial(attend_kernel, heads, own, len(mixing)),...  21.2 us
    ppermute x3, waiting for transfers between devices, gather_rows(): lax.ppermute(array, 'head', [(k, (k + s) % 4) for k in range(4)])  19 us
    pallas_call x1, Pallas kernels, local(): pl.pallas_call(functools.partial(project_kernel, heads, n_var, n_head, le...  16.3 us
    ppermute x12, starting transfers between devices, shifts(): lax.ppermute(array, axis, [(k, (k + s) % size) for k in range(size)])  15.6 us
    ppermute x12, waiting for transfers between devices, shifts(): lax.ppermute(array, axis, [(k, (k + s) % size) for k in range(size)])  15 us
    pallas_call x1, Pallas kernels, local(): pl.pallas_call(functools.partial(pair_kernel, variants), out_shape=jax.Sh...  6.56 us
    ppermute x3, starting transfers between devices, gather_rows(): lax.ppermute(array, 'head', [(k, (k + s) % 4) for k in range(4)])  5.84 us
    ppermute x3, starting transfers between devices, local(): summed += lax.ppermute(sent[s - 1], 'head', pairs).astype(jnp.float32)  4.62 us
  transfers between devices with their start and end apart: 28, of which 10 were waited for; matrix products, arithmetic and copies ran while one was open for 4% of the time, Pallas kernels for 18%

profile of v1, /device:TPU:0, one launch (start us, length us, event | category | flops | bytes accessed | tf_op | source)
XLA Modules:
  0.0 120.7 jit_solution(11798154757615017720)
XLA Ops:
  0.0 1.0 copy-done
  1.0 5.1 %collective-permute-start.1 = (bf16[256,384]{1,0:T(8,128)(2,1)S(1)}, bf16[256,384]{1,0:T(8,128)(2,1)S(1)}, u32[]{:S(2)}, u32[]{:S(2)}) collective-permute-start(bf16[256,384]{1,0:T(8,128)(2,1)S(1)} %constant_dynamic-slice_fusion), channel_id=1, source_target_pairs={{0,6},{2,0},{4,2},{6,4},{1,7},{3,1},{5,3},{7,5},{8,14},{10,8},{12,... | collective-permute-start | bytes 589832 | tf_op jit(solution)/shard_map/ppermute | solution.py:322
  6.2 5.3 %collective-permute-done.1 = bf16[256,384]{1,0:T(8,128)(2,1)S(1)} collective-permute-done((bf16[256,384]{1,0:T(8,128)(2,1)S(1)}, bf16[256,384]{1,0:T(8,128)(2,1)S(1)}, u32[]{:S(2)}, u32[]{:S(2)}) %collective-permute-start.1) | collective-permute-done | bytes 196640 | tf_op jit(solution)/shard_map/ppermute | solution.py:322
  11.4 4.0 %collective-permute-done = bf16[256,384]{1,0:T(8,128)(2,1)S(1)} collective-permute-done((bf16[256,384]{1,0:T(8,128)(2,1)S(1)}, bf16[256,384]{1,0:T(8,128)(2,1)S(1)}, u32[]{:S(2)}, u32[]{:S(2)}) %collective-permute-start) | collective-permute-done | bytes 196640 | tf_op jit(solution)/shard_map/ppermute | solution.py:322
  15.4 0.1 pad_maximum_fusion.1
  15.5 1.6 %collective-permute-start.5 = (bf16[3,256,384]{2,1,0:T(8,128)(2,1)S(1)}, bf16[3,256,384]{2,1,0:T(8,128)(2,1)}, u32[]{:S(2)}, u32[]{:S(2)}) collective-permute-start(bf16[3,256,384]{2,1,0:T(8,128)(2,1)S(1)} %pad_maximum_fusion.1), channel_id=1, source_target_pairs={{0,8},{8,0},{16,24},{24,16},{1,9},{9,1},{17,25},{25,17},{2,10},{10... | collective-permute-start | bytes 1769480 | tf_op jit(solution)/shard_map/ppermute | solution.py:323
  17.0 1.5 %collective-permute-start.2 = (bf16[3,256,384]{2,1,0:T(8,128)(2,1)S(1)}, bf16[3,256,384]{2,1,0:T(8,128)(2,1)S(1)}, u32[]{:S(2)}, u32[]{:S(2)}) collective-permute-start(bf16[3,256,384]{2,1,0:T(8,128)(2,1)S(1)} %pad_maximum_fusion.1), channel_id=1, source_target_pairs={{0,16},{8,24},{16,0},{24,8},{1,17},{9,25},{17,1},{25,9},{2,18},{10... | collective-permute-start | bytes 1769480 | tf_op jit(solution)/shard_map/ppermute | solution.py:323
  18.6 0.7 collective-permute-start.3
  19.3 9.8 %collective-permute-done.3 = bf16[256,384]{1,0:T(8,128)(2,1)} collective-permute-done((bf16[256,384]{1,0:T(8,128)(2,1)S(1)}, bf16[256,384]{1,0:T(8,128)(2,1)}, u32[]{:S(2)}, u32[]{:S(2)}) %collective-permute-start.3) | collective-permute-done | bytes 196640 | tf_op jit(solution)/shard_map/ppermute | solution.py:322
  29.1 0.5 collective-permute-start.6
  29.6 0.5 collective-permute-start.4
  30.1 1.1 pad_maximum_fusion.refs_4_
  31.3 0.1 collective-permute-start.8
  31.4 1.4 %constant_dynamic-update-slice_fusion.3 = bf16[4,256,384]{2,1,0:T(8,128)(2,1)S(1)} fusion(bf16[3,256,384]{2,1,0:T(8,128)(2,1)} %collective-permute-done.5), kind=kLoop, calls=%fused_computation.33 | loop fusion | bytes 1179648
  32.8 2.3 %collective-permute-done.6 = bf16[1,256,384]{2,1,0:T(8,128)(2,1)S(1)} collective-permute-done((bf16[1,256,384]{2,1,0:T(8,128)(2,1)}, bf16[1,256,384]{2,1,0:T(8,128)(2,1)S(1)}, u32[]{:S(2)}, u32[]{:S(2)}) %collective-permute-start.6) | collective-permute-done | bytes 196640 | tf_op jit(solution)/shard_map/ppermute | solution.py:323
  35.1 0.1 constant_dynamic-update-slice_fusion.1
  35.2 0.3 collective-permute-done.4
  35.6 0.1 broadcast_select_fusion
  35.7 1.6 %collective-permute-start.7 = (bf16[4,256,384]{2,1,0:T(8,128)(2,1)S(1)}, bf16[4,256,384]{2,1,0:T(8,128)(2,1)}, u32[]{:S(2)}, u32[]{:S(2)}) collective-permute-start(bf16[4,256,384]{2,1,0:T(8,128)(2,1)S(1)} %broadcast_select_fusion), channel_id=1, source_target_pairs={{0,8},{1,17},{8,0},{9,25},{16,24},{17,1},{24,16},{25,9},{2,10},{3,... | collective-permute-start | bytes 2359304 | tf_op jit(solution)/shard_map/ppermute | solution.py:333
  37.2 0.5 collective-permute-start.9
  37.8 1.2 %collective-permute-start.13 = (f32[4,384]{1,0:T(4,128)S(1)}, f32[4,384]{1,0:T(4,128)S(1)}, u32[]{:S(2)}, u32[]{:S(2)}) collective-permute-start(f32[4,384]{1,0:T(4,128)S(1)} %pad_maximum_fusion.2.refs_0_), channel_id=1, source_target_pairs={{0,6},{2,0},{4,2},{6,4},{1,7},{3,1},{5,3},{7,5},{8,14},{10,8},{12,... | collective-permute-start | bytes 18440 | tf_op jit(solution)/shard_map/ppermute | solution.py:310
  39.0 2.4 %collective-permute-done.13.refs_2_ = f32[4,384]{1,0:T(4,128)S(1)} collective-permute-done((f32[4,384]{1,0:T(4,128)S(1)}, f32[4,384]{1,0:T(4,128)S(1)}, u32[]{:S(2)}, u32[]{:S(2)}) %collective-permute-start.13) | collective-permute-done | bytes 6176 | tf_op jit(solution)/shard_map/ppermute | solution.py:310
  41.4 4.5 %collective-permute-done.12.refs_3_ = f32[4,384]{1,0:T(4,128)S(1)} collective-permute-done((f32[4,384]{1,0:T(4,128)S(1)}, f32[4,384]{1,0:T(4,128)S(1)}, u32[]{:S(2)}, u32[]{:S(2)}) %collective-permute-start.12) | collective-permute-done | bytes 6176 | tf_op jit(solution)/shard_map/ppermute | solution.py:310
  46.0 0.6 collective-permute-start.11
  46.6 4.8 %collective-permute-done.11.refs_1_ = f32[4,384]{1,0:T(4,128)S(1)} collective-permute-done((f32[4,384]{1,0:T(4,128)S(1)}, f32[4,384]{1,0:T(4,128)S(1)}, u32[]{:S(2)}, u32[]{:S(2)}) %collective-permute-start.11) | collective-permute-done | bytes 6176 | tf_op jit(solution)/shard_map/ppermute | solution.py:310
  51.5 0.1 collective-permute-start.14
  51.5 1.2 %collective-permute-start.17 = (bf16[384,256]{1,0:T(8,128)(2,1)S(1)}, bf16[384,256]{1,0:T(8,128)(2,1)S(1)}, u32[]{:S(2)}, u32[]{:S(2)}) collective-permute-start(bf16[384,256]{1,0:T(8,128)(2,1)S(1)} %copy-done.2), channel_id=1, source_target_pairs={{0,6},{2,0},{4,2},{6,4},{1,7},{3,1},{5,3},{7,5},{8,14},{10,8},{12,... | collective-permute-start | bytes 589832 | tf_op jit(solution)/shard_map/ppermute | solution.py:310
  52.8 1.2 collective-permute-start.15
  54.0 0.2 dynamic-slice_reduce_fusion
  54.2 0.1 concatenate.24.order
  54.3 0.1 concatenate.19.scalars
  54.4 16.3 %project.1 = (bf16[2048,1024]{1,0:T(8,128)(2,1)S(1)}, f32[512,384]{1,0:T(8,128)S(1)}) custom-call(s32[8]{0:T(128)S(1)} %concatenate.19.scalars, bf16[1536,896]{1,0:T(8,128)(2,1)} %w_proj.1, f32[4,384]{1,0:T(4,128)S(1)} %pad_maximum_fusion.2.refs_0_, f32[4,384]{1,0:T(4,128)S(1)} %collective-permute-done.11.refs_1_, ...), custom_call_target="tpu_custom_call" | custom-call | flops 7952400384 | bytes 12582912 | tf_op jit(solution)/shard_map/project/pallas_call | solution.py:372
  70.8 15.9 %attend.2 = (bf16[3,128,256]{2,1,0:T(8,128)(2,1)S(1)}, bf16[2,256,256]{2,1,0:T(8,128)(2,1)S(1)}) custom-call(s32[7]{0:T(128)S(1)} %concatenate.24.order, bf16[2048,1024]{1,0:T(8,128)(2,1)S(1)} %get-tuple-element.25.kvq, f32[512,384]{1,0:T(8,128)S(1)} %get-tuple-element.26.pooled, bf16[384,1536]{1,0:T(8,128)(2,1)S(1)} %copy-done.1, ...), custom_call_target="tpu_custom_call" | custom-call | flops 6442450944 | bytes 4194304 | tf_op jit(solution)/shard_map/attend/pallas_call | solution.py:419
  86.7 2.3 %collective-permute-start.18 = (bf16[128,256]{1,0:T(8,128)(2,1)S(1)}, bf16[128,256]{1,0:T(8,128)(2,1)S(1)}, u32[]{:S(2)}, u32[]{:S(2)}) collective-permute-start(bf16[128,256]{1,0:T(8,128)(2,1)S(1)} %get-tuple-element.29), channel_id=1, source_target_pairs={{0,2},{2,4},{4,6},{6,0},{1,3},{3,5},{5,7},{7,1},{8,10},{10,12},{12... | collective-permute-start | bytes 196616 | tf_op jit(solution)/shard_map/ppermute | solution.py:448
  89.0 1.6 %collective-permute-start.20 = (bf16[128,256]{1,0:T(8,128)(2,1)S(1)}, bf16[128,256]{1,0:T(8,128)(2,1)S(1)}, u32[]{:S(2)}, u32[]{:S(2)}) collective-permute-start(bf16[128,256]{1,0:T(8,128)(2,1)S(1)} %get-tuple-element.30), channel_id=1, source_target_pairs={{0,6},{2,0},{4,2},{6,4},{1,7},{3,1},{5,3},{7,5},{8,14},{10,8},{12,... | collective-permute-start | bytes 196616 | tf_op jit(solution)/shard_map/ppermute | solution.py:448
  90.6 0.7 collective-permute-start.19
  91.3 5.4 %attend.3 = f32[1,128,256]{2,1,0:T(8,128)S(1)} custom-call(s32[1]{0:T(128)} %bitcast.9.order, bf16[2048,1024]{1,0:T(8,128)(2,1)S(1)} %get-tuple-element.25.kvq, f32[512,384]{1,0:T(8,128)S(1)} %get-tuple-element.26.pooled, bf16[2,256,256]{2,1,0:T(8,128)(2,1)S(1)} %get-tuple-element.27.refs_0_, bf16[384,256]{1,0:T(8,128)(2,1)S(1)} %copy-done.2), custom_call_target="tpu_custom_call" | custom-call | flops 2147483648 | bytes 4194304 | tf_op jit(solution)/shard_map/attend/pallas_call | solution.py:419
  96.8 0.7 collective-permute-start.21
  97.4 5.7 %collective-permute-start.27 = (bf16[128,128]{1,0:T(8,128)(2,1)S(1)}, bf16[128,128]{1,0:T(8,128)(2,1)S(1)}, u32[]{:S(2)}, u32[]{:S(2)}) collective-permute-start(bf16[128,128]{1,0:T(8,128)(2,1)S(1)} %get-tuple-element.32.refs_4_), channel_id=1, source_target_pairs={{0,24},{8,0},{16,8},{24,16},{1,25},{9,1},{17,9},{25,17},{2,26},{10... | collective-permute-start | bytes 98312 | tf_op jit(solution)/shard_map/ppermute | solution.py:310
  103.2 0.1 collective-permute-start.26
  103.2 1.2 %collective-permute-start.25 = (bf16[128,128]{1,0:T(8,128)(2,1)S(1)}, bf16[128,128]{1,0:T(8,128)(2,1)S(1)}, u32[]{:S(2)}, u32[]{:S(2)}) collective-permute-start(bf16[128,128]{1,0:T(8,128)(2,1)S(1)} %get-tuple-element.32.refs_4_), channel_id=1, source_target_pairs={{0,8},{8,16},{16,24},{24,0},{1,9},{9,17},{17,25},{25,1},{2,10},{10... | collective-permute-start | bytes 98312 | tf_op jit(solution)/shard_map/ppermute | solution.py:310
  104.5 3.7 %collective-permute-start.24 = (bf16[128,128]{1,0:T(8,128)(2,1)S(1)}, bf16[128,128]{1,0:T(8,128)(2,1)S(1)}, u32[]{:S(2)}, u32[]{:S(2)}) collective-permute-start(bf16[128,128]{1,0:T(8,128)(2,1)S(1)} %collective-permute-done.21.refs_0_), channel_id=1, source_target_pairs={{0,6},{2,0},{4,2},{6,4},{1,7},{3,1},{5,3},{7,5},{8,14},{10,8},{12,... | collective-permute-start | bytes 98312 | tf_op jit(solution)/shard_map/ppermute | solution.py:310
  108.2 0.6 collective-permute-start.22
  108.8 1.8 %convolution_convert_fusion.table = bf16[16,256,128]{2,1,0:T(8,128)(2,1)S(1)} fusion(s32[16,256]{1,0:T(8,128)S(1)} %convert_add_fusion, f32[16,128]{1,0:T(8,128)S(1)} %copy-done.6), kind=kOutput, calls=%fused_computation | convolution fusion | flops 101253120 | bytes 1073152 | tf_op jit(solution)/shard_map/skb,bc->skc/dot_general | solution.py:294
  110.6 0.1 stack.67.order
  110.8 2.3 %collective-permute-done.23.refs_2_ = bf16[128,128]{1,0:T(8,128)(2,1)S(1)} collective-permute-done((bf16[128,128]{1,0:T(8,128)(2,1)S(1)}, bf16[128,128]{1,0:T(8,128)(2,1)S(1)}, u32[]{:S(2)}, u32[]{:S(2)}) %collective-permute-start.23) | collective-permute-done | bytes 32800 | tf_op jit(solution)/shard_map/ppermute | solution.py:310
  113.0 0.9 collective-permute-done.22.refs_1_
  113.9 6.6 %pair_map.1 = bf16[4,128,128,128]{3,2,1,0:T(8,128)(2,1)} custom-call(s32[8]{0:T(128)S(1)} %stack.67.order, bf16[16,256,128]{2,1,0:T(8,128)(2,1)S(1)} %convolution_convert_fusion.table, bf16[128,128]{1,0:T(8,128)(2,1)S(1)} %collective-permute-done.21.refs_0_, bf16[128,128]{1,0:T(8,128)(2,1)S(1)} %collective-permute-done.22.refs_1_, ...), custom_call_target="tpu_custom_call" | custom-call | tf_op jit(solution)/shard_map/pair_map/pallas_call | solution.py:468
  (59 shorter events, 0.4 us)
Async XLA Ops:
  0.0 1.0 copy-start
  1.0 10.4 %collective-permute-start.1 = (bf16[256,384]{1,0:T(8,128)(2,1)S(1)}, bf16[256,384]{1,0:T(8,128)(2,1)S(1)}, u32[]{:S(2)}, u32[]{:S(2)}) collective-permute-start(bf16[256,384]{1,0:T(8,128)(2,1)S(1)} %constant_dynamic-slice_fusion), channel_id=1, source_target_pairs={{0,6},{2,0},{4,2},{6,4},{1,7},{3,1},{5,3},{7,5},{8,14},{10,8},{12,... | collective-permute-start | bytes 589832 | tf_op jit(solution)/shard_map/ppermute | solution.py:322
  6.1 9.3 %collective-permute-start = (bf16[256,384]{1,0:T(8,128)(2,1)S(1)}, bf16[256,384]{1,0:T(8,128)(2,1)S(1)}, u32[]{:S(2)}, u32[]{:S(2)}) collective-permute-start(bf16[256,384]{1,0:T(8,128)(2,1)S(1)} %constant_dynamic-slice_fusion), channel_id=1, source_target_pairs={{0,2},{2,4},{4,6},{6,0},{1,3},{3,5},{5,7},{7,1},{8,10},{10,12},{12... | collective-permute-start | bytes 589832 | tf_op jit(solution)/shard_map/ppermute | solution.py:322
  15.5 15.9 %collective-permute-start.5 = (bf16[3,256,384]{2,1,0:T(8,128)(2,1)S(1)}, bf16[3,256,384]{2,1,0:T(8,128)(2,1)}, u32[]{:S(2)}, u32[]{:S(2)}) collective-permute-start(bf16[3,256,384]{2,1,0:T(8,128)(2,1)S(1)} %pad_maximum_fusion.1), channel_id=1, source_target_pairs={{0,8},{8,0},{16,24},{24,16},{1,9},{9,1},{17,25},{25,17},{2,10},{10... | collective-permute-start | bytes 1769480 | tf_op jit(solution)/shard_map/ppermute | solution.py:323
  17.0 18.1 %collective-permute-start.2 = (bf16[3,256,384]{2,1,0:T(8,128)(2,1)S(1)}, bf16[3,256,384]{2,1,0:T(8,128)(2,1)S(1)}, u32[]{:S(2)}, u32[]{:S(2)}) collective-permute-start(bf16[3,256,384]{2,1,0:T(8,128)(2,1)S(1)} %pad_maximum_fusion.1), channel_id=1, source_target_pairs={{0,16},{8,24},{16,0},{24,8},{1,17},{9,25},{17,1},{25,9},{2,18},{10... | collective-permute-start | bytes 1769480 | tf_op jit(solution)/shard_map/ppermute | solution.py:323
  18.6 10.5 %collective-permute-start.3 = (bf16[256,384]{1,0:T(8,128)(2,1)S(1)}, bf16[256,384]{1,0:T(8,128)(2,1)}, u32[]{:S(2)}, u32[]{:S(2)}) collective-permute-start(bf16[256,384]{1,0:T(8,128)(2,1)S(1)} %constant_dynamic-slice_fusion), channel_id=1, source_target_pairs={{0,4},{2,6},{4,0},{6,2},{1,5},{3,7},{5,1},{7,3},{8,12},{10,14},{12... | collective-permute-start | bytes 589832 | tf_op jit(solution)/shard_map/ppermute | solution.py:322
  29.1 6.0 %collective-permute-start.6 = (bf16[1,256,384]{2,1,0:T(8,128)(2,1)}, bf16[1,256,384]{2,1,0:T(8,128)(2,1)S(1)}, u32[]{:S(2)}, u32[]{:S(2)}) collective-permute-start(bf16[1,256,384]{2,1,0:T(8,128)(2,1)} %bitcast.18), channel_id=1, source_target_pairs={{0,8},{8,0},{16,24},{24,16},{1,9},{9,1},{17,25},{25,17},{2,10},{10... | collective-permute-start | bytes 589832 | tf_op jit(solution)/shard_map/ppermute | solution.py:323
  29.6 5.9 %collective-permute-start.4 = (bf16[1,256,384]{2,1,0:T(8,128)(2,1)}, bf16[1,256,384]{2,1,0:T(8,128)(2,1)S(1)}, u32[]{:S(2)}, u32[]{:S(2)}) collective-permute-start(bf16[1,256,384]{2,1,0:T(8,128)(2,1)} %bitcast.18), channel_id=1, source_target_pairs={{0,16},{8,24},{16,0},{24,8},{1,17},{9,25},{17,1},{25,9},{2,18},{10... | collective-permute-start | bytes 589832 | tf_op jit(solution)/shard_map/ppermute | solution.py:323
  31.2 4.4 %copy-start.5 = (bf16[4,256,384]{2,1,0:T(8,128)(2,1)}, bf16[4,256,384]{2,1,0:T(8,128)(2,1)S(1)}, u32[]{:S(2)}) copy-start(bf16[4,256,384]{2,1,0:T(8,128)(2,1)S(1)} %pad_maximum_fusion.refs_4_) | copy-start | bytes 2359300
  31.2 6.5 %copy-start.8 = (f32[384]{0:T(512)S(1)}, f32[384]{0:T(512)}, u32[]{:S(2)}) copy-start(f32[384]{0:T(512)} %param.11) | copy-start | bytes 4612
  31.2 6.5 %copy-start.7 = (f32[3,384]{1,0:T(4,128)S(1)}, f32[3,384]{1,0:T(4,128)}, u32[]{:S(2)}) copy-start(f32[3,384]{1,0:T(4,128)} %param.10) | copy-start | bytes 13828
  31.3 20.3 %copy-start.2 = (bf16[384,256]{1,0:T(8,128)(2,1)S(1)}, bf16[384,256]{1,0:T(8,128)(2,1)}, u32[]{:S(2)}) copy-start(bf16[384,256]{1,0:T(8,128)(2,1)} %refs_1_.3) | copy-start | bytes 589828
  31.3 22.8 %copy-start.9 = (s32[4,2]{0,1:T(2,128)S(1)}, s32[4,2]{0,1:T(2,128)}, u32[]{:S(2)}) copy-start(s32[4,2]{0,1:T(2,128)} %param.9) | copy-start | bytes 100
  31.3 20.1 %collective-permute-start.8 = (bf16[4,256,384]{2,1,0:T(8,128)(2,1)S(1)}, bf16[4,256,384]{2,1,0:T(8,128)(2,1)S(1)}, u32[]{:S(2)}, u32[]{:S(2)}) collective-permute-start(bf16[4,256,384]{2,1,0:T(8,128)(2,1)S(1)} %pad_maximum_fusion.refs_4_), channel_id=1, source_target_pairs={{0,1},{1,0},{2,3},{3,2},{4,5},{5,4},{6,7},{7,6},{8,9},{9,8},{10,11... | collective-permute-start | bytes 2359304 | tf_op jit(solution)/shard_map/ppermute | solution.py:320
  35.1 19.3 %copy-start.4 = (bf16[4,256,384]{2,1,0:T(8,128)(2,1)}, bf16[4,256,384]{2,1,0:T(8,128)(2,1)S(1)}, u32[]{:S(2)}) copy-start(bf16[4,256,384]{2,1,0:T(8,128)(2,1)S(1)} %constant_dynamic-update-slice_fusion.2.refs_5_) | copy-start | bytes 2359300
  35.5 18.9 %copy-start.3 = (bf16[4,256,384]{2,1,0:T(8,128)(2,1)}, bf16[4,256,384]{2,1,0:T(8,128)(2,1)S(1)}, u32[]{:S(2)}) copy-start(bf16[4,256,384]{2,1,0:T(8,128)(2,1)S(1)} %constant_dynamic-update-slice_fusion.refs_6_) | copy-start | bytes 2359300
  35.7 15.7 %collective-permute-start.7 = (bf16[4,256,384]{2,1,0:T(8,128)(2,1)S(1)}, bf16[4,256,384]{2,1,0:T(8,128)(2,1)}, u32[]{:S(2)}, u32[]{:S(2)}) collective-permute-start(bf16[4,256,384]{2,1,0:T(8,128)(2,1)S(1)} %broadcast_select_fusion), channel_id=1, source_target_pairs={{0,8},{1,17},{8,0},{9,25},{16,24},{17,1},{24,16},{25,9},{2,10},{3,... | collective-permute-start | bytes 2359304 | tf_op jit(solution)/shard_map/ppermute | solution.py:333
  37.2 14.2 %collective-permute-start.10 = (bf16[4,256,384]{2,1,0:T(8,128)(2,1)S(1)}, bf16[4,256,384]{2,1,0:T(8,128)(2,1)S(1)}, u32[]{:S(2)}, u32[]{:S(2)}) collective-permute-start(bf16[4,256,384]{2,1,0:T(8,128)(2,1)S(1)} %constant_dynamic-update-slice_fusion.refs_6_), channel_id=1, source_target_pairs={{0,1},{1,0},{2,3},{3,2},{4,5},{5,4},{6,7},{7,6},{8,9},{9,8},{10,11... | collective-permute-start | bytes 2359304 | tf_op jit(solution)/shard_map/ppermute | solution.py:320
  37.2 14.2 %collective-permute-start.9 = (bf16[4,256,384]{2,1,0:T(8,128)(2,1)S(1)}, bf16[4,256,384]{2,1,0:T(8,128)(2,1)S(1)}, u32[]{:S(2)}, u32[]{:S(2)}) collective-permute-start(bf16[4,256,384]{2,1,0:T(8,128)(2,1)S(1)} %constant_dynamic-update-slice_fusion.2.refs_5_), channel_id=1, source_target_pairs={{0,1},{1,0},{2,3},{3,2},{4,5},{5,4},{6,7},{7,6},{8,9},{9,8},{10,11... | collective-permute-start | bytes 2359304 | tf_op jit(solution)/shard_map/ppermute | solution.py:320
  37.8 3.7 %collective-permute-start.13 = (f32[4,384]{1,0:T(4,128)S(1)}, f32[4,384]{1,0:T(4,128)S(1)}, u32[]{:S(2)}, u32[]{:S(2)}) collective-permute-start(f32[4,384]{1,0:T(4,128)S(1)} %pad_maximum_fusion.2.refs_0_), channel_id=1, source_target_pairs={{0,6},{2,0},{4,2},{6,4},{1,7},{3,1},{5,3},{7,5},{8,14},{10,8},{12,... | collective-permute-start | bytes 18440 | tf_op jit(solution)/shard_map/ppermute | solution.py:310
  41.4 4.5 %collective-permute-start.12 = (f32[4,384]{1,0:T(4,128)S(1)}, f32[4,384]{1,0:T(4,128)S(1)}, u32[]{:S(2)}, u32[]{:S(2)}) collective-permute-start(f32[4,384]{1,0:T(4,128)S(1)} %pad_maximum_fusion.2.refs_0_), channel_id=1, source_target_pairs={{0,4},{2,6},{4,0},{6,2},{1,5},{3,7},{5,1},{7,3},{8,12},{10,14},{12... | collective-permute-start | bytes 18440 | tf_op jit(solution)/shard_map/ppermute | solution.py:310
  46.0 5.4 %collective-permute-start.11 = (f32[4,384]{1,0:T(4,128)S(1)}, f32[4,384]{1,0:T(4,128)S(1)}, u32[]{:S(2)}, u32[]{:S(2)}) collective-permute-start(f32[4,384]{1,0:T(4,128)S(1)} %pad_maximum_fusion.2.refs_0_), channel_id=1, source_target_pairs={{0,2},{2,4},{4,6},{6,0},{1,3},{3,5},{5,7},{7,1},{8,10},{10,12},{12... | collective-permute-start | bytes 18440 | tf_op jit(solution)/shard_map/ppermute | solution.py:310
  51.4 1.4 %copy-start.10 = (bf16[4,256,384]{2,1,0:T(8,128)(2,1)}, bf16[4,256,384]{2,1,0:T(8,128)(2,1)S(1)}, u32[]{:S(2)}) copy-start(bf16[4,256,384]{2,1,0:T(8,128)(2,1)S(1)} %collective-permute-done.8.refs_8_) | copy-start | bytes 2359300
  51.4 1.4 %copy-start.11 = (bf16[4,256,384]{2,1,0:T(8,128)(2,1)}, bf16[4,256,384]{2,1,0:T(8,128)(2,1)S(1)}, u32[]{:S(2)}) copy-start(bf16[4,256,384]{2,1,0:T(8,128)(2,1)S(1)} %collective-permute-done.10.refs_10_) | copy-start | bytes 2359300
  51.4 1.4 %copy-start.12 = (bf16[4,256,384]{2,1,0:T(8,128)(2,1)}, bf16[4,256,384]{2,1,0:T(8,128)(2,1)S(1)}, u32[]{:S(2)}) copy-start(bf16[4,256,384]{2,1,0:T(8,128)(2,1)S(1)} %collective-permute-done.9.refs_9_) | copy-start | bytes 2359300
  51.5 3.0 %collective-permute-start.14 = (bf16[4,256,384]{2,1,0:T(8,128)(2,1)}, bf16[4,256,384]{2,1,0:T(8,128)(2,1)}, u32[]{:S(2)}, u32[]{:S(2)}) collective-permute-start(bf16[4,256,384]{2,1,0:T(8,128)(2,1)} %collective-permute-done.7.refs_7_), channel_id=1, source_target_pairs={{0,1},{1,0},{2,3},{3,2},{4,5},{5,4},{6,7},{7,6},{8,9},{9,8},{10,11... | collective-permute-start | bytes 2359304 | tf_op jit(solution)/shard_map/ppermute | solution.py:320
  51.5 19.2 %collective-permute-start.17 = (bf16[384,256]{1,0:T(8,128)(2,1)S(1)}, bf16[384,256]{1,0:T(8,128)(2,1)S(1)}, u32[]{:S(2)}, u32[]{:S(2)}) collective-permute-start(bf16[384,256]{1,0:T(8,128)(2,1)S(1)} %copy-done.2), channel_id=1, source_target_pairs={{0,6},{2,0},{4,2},{6,4},{1,7},{3,1},{5,3},{7,5},{8,14},{10,8},{12,... | collective-permute-start | bytes 589832 | tf_op jit(solution)/shard_map/ppermute | solution.py:310
  52.8 18.0 %collective-permute-start.16 = (bf16[384,256]{1,0:T(8,128)(2,1)S(1)}, bf16[384,256]{1,0:T(8,128)(2,1)S(1)}, u32[]{:S(2)}, u32[]{:S(2)}) collective-permute-start(bf16[384,256]{1,0:T(8,128)(2,1)S(1)} %copy-done.2), channel_id=1, source_target_pairs={{0,4},{2,6},{4,0},{6,2},{1,5},{3,7},{5,1},{7,3},{8,12},{10,14},{12... | collective-permute-start | bytes 589832 | tf_op jit(solution)/shard_map/ppermute | solution.py:310
  52.8 17.9 %collective-permute-start.15 = (bf16[384,256]{1,0:T(8,128)(2,1)S(1)}, bf16[384,256]{1,0:T(8,128)(2,1)S(1)}, u32[]{:S(2)}, u32[]{:S(2)}) collective-permute-start(bf16[384,256]{1,0:T(8,128)(2,1)S(1)} %copy-done.2), channel_id=1, source_target_pairs={{0,2},{2,4},{4,6},{6,0},{1,3},{3,5},{5,7},{7,1},{8,10},{10,12},{12... | collective-permute-start | bytes 589832 | tf_op jit(solution)/shard_map/ppermute | solution.py:310
  54.4 16.3 %copy-start.1 = (bf16[384,1536]{1,0:T(8,128)(2,1)S(1)}, bf16[384,1536]{1,0:T(8,128)(2,1)}, u32[]{:S(2)}) copy-start(bf16[384,1536]{1,0:T(8,128)(2,1)} %refs_0_.1) | copy-start | bytes 3538948
  86.7 10.0 %collective-permute-start.18 = (bf16[128,256]{1,0:T(8,128)(2,1)S(1)}, bf16[128,256]{1,0:T(8,128)(2,1)S(1)}, u32[]{:S(2)}, u32[]{:S(2)}) collective-permute-start(bf16[128,256]{1,0:T(8,128)(2,1)S(1)} %get-tuple-element.29), channel_id=1, source_target_pairs={{0,2},{2,4},{4,6},{6,0},{1,3},{3,5},{5,7},{7,1},{8,10},{10,12},{12... | collective-permute-start | bytes 196616 | tf_op jit(solution)/shard_map/ppermute | solution.py:448
  89.0 7.7 %collective-permute-start.20 = (bf16[128,256]{1,0:T(8,128)(2,1)S(1)}, bf16[128,256]{1,0:T(8,128)(2,1)S(1)}, u32[]{:S(2)}, u32[]{:S(2)}) collective-permute-start(bf16[128,256]{1,0:T(8,128)(2,1)S(1)} %get-tuple-element.30), channel_id=1, source_target_pairs={{0,6},{2,0},{4,2},{6,4},{1,7},{3,1},{5,3},{7,5},{8,14},{10,8},{12,... | collective-permute-start | bytes 196616 | tf_op jit(solution)/shard_map/ppermute | solution.py:448
  90.6 6.1 %collective-permute-start.19 = (bf16[128,256]{1,0:T(8,128)(2,1)S(1)}, bf16[128,256]{1,0:T(8,128)(2,1)S(1)}, u32[]{:S(2)}, u32[]{:S(2)}) collective-permute-start(bf16[128,256]{1,0:T(8,128)(2,1)S(1)} %get-tuple-element.31), channel_id=1, source_target_pairs={{0,4},{2,6},{4,0},{6,2},{1,5},{3,7},{5,1},{7,3},{8,12},{10,14},{12... | collective-permute-start | bytes 196616 | tf_op jit(solution)/shard_map/ppermute | solution.py:448
  91.3 17.5 %copy-start.6 = (f32[16,128]{1,0:T(8,128)S(1)}, f32[16,128]{1,0:T(8,128)}, u32[]{:S(2)}) copy-start(f32[16,128]{1,0:T(8,128)} %param.15) | copy-start | bytes 24580
  96.8 7.7 %collective-permute-start.21 = (bf16[128,128]{1,0:T(8,128)(2,1)S(1)}, bf16[128,128]{1,0:T(8,128)(2,1)S(1)}, u32[]{:S(2)}, u32[]{:S(2)}) collective-permute-start(bf16[128,128]{1,0:T(8,128)(2,1)S(1)} %get-tuple-element.33), channel_id=1, source_target_pairs={{0,0},{2,8},{4,16},{6,24},{8,2},{10,10},{12,18},{14,26},{16,4},{18... | collective-permute-start | bytes 98312 | tf_op jit(solution)/shard_map/ppermute | solution.py:449
  97.4 10.8 %collective-permute-start.27 = (bf16[128,128]{1,0:T(8,128)(2,1)S(1)}, bf16[128,128]{1,0:T(8,128)(2,1)S(1)}, u32[]{:S(2)}, u32[]{:S(2)}) collective-permute-start(bf16[128,128]{1,0:T(8,128)(2,1)S(1)} %get-tuple-element.32.refs_4_), channel_id=1, source_target_pairs={{0,24},{8,0},{16,8},{24,16},{1,25},{9,1},{17,9},{25,17},{2,26},{10... | collective-permute-start | bytes 98312 | tf_op jit(solution)/shard_map/ppermute | solution.py:310
  103.2 7.6 %collective-permute-start.26 = (bf16[128,128]{1,0:T(8,128)(2,1)S(1)}, bf16[128,128]{1,0:T(8,128)(2,1)S(1)}, u32[]{:S(2)}, u32[]{:S(2)}) collective-permute-start(bf16[128,128]{1,0:T(8,128)(2,1)S(1)} %get-tuple-element.32.refs_4_), channel_id=1, source_target_pairs={{0,16},{8,24},{16,0},{24,8},{1,17},{9,25},{17,1},{25,9},{2,18},{10... | collective-permute-start | bytes 98312 | tf_op jit(solution)/shard_map/ppermute | solution.py:310
  103.2 7.5 %collective-permute-start.25 = (bf16[128,128]{1,0:T(8,128)(2,1)S(1)}, bf16[128,128]{1,0:T(8,128)(2,1)S(1)}, u32[]{:S(2)}, u32[]{:S(2)}) collective-permute-start(bf16[128,128]{1,0:T(8,128)(2,1)S(1)} %get-tuple-element.32.refs_4_), channel_id=1, source_target_pairs={{0,8},{8,16},{16,24},{24,0},{1,9},{9,17},{17,25},{25,1},{2,10},{10... | collective-permute-start | bytes 98312 | tf_op jit(solution)/shard_map/ppermute | solution.py:310
  104.5 6.2 %collective-permute-start.24 = (bf16[128,128]{1,0:T(8,128)(2,1)S(1)}, bf16[128,128]{1,0:T(8,128)(2,1)S(1)}, u32[]{:S(2)}, u32[]{:S(2)}) collective-permute-start(bf16[128,128]{1,0:T(8,128)(2,1)S(1)} %collective-permute-done.21.refs_0_), channel_id=1, source_target_pairs={{0,6},{2,0},{4,2},{6,4},{1,7},{3,1},{5,3},{7,5},{8,14},{10,8},{12,... | collective-permute-start | bytes 98312 | tf_op jit(solution)/shard_map/ppermute | solution.py:310
  108.2 4.8 %collective-permute-start.23 = (bf16[128,128]{1,0:T(8,128)(2,1)S(1)}, bf16[128,128]{1,0:T(8,128)(2,1)S(1)}, u32[]{:S(2)}, u32[]{:S(2)}) collective-permute-start(bf16[128,128]{1,0:T(8,128)(2,1)S(1)} %collective-permute-done.21.refs_0_), channel_id=1, source_target_pairs={{0,4},{2,6},{4,0},{6,2},{1,5},{3,7},{5,1},{7,3},{8,12},{10,14},{12... | collective-permute-start | bytes 98312 | tf_op jit(solution)/shard_map/ppermute | solution.py:310
  108.2 5.7 %collective-permute-start.22 = (bf16[128,128]{1,0:T(8,128)(2,1)S(1)}, bf16[128,128]{1,0:T(8,128)(2,1)S(1)}, u32[]{:S(2)}, u32[]{:S(2)}) collective-permute-start(bf16[128,128]{1,0:T(8,128)(2,1)S(1)} %collective-permute-done.21.refs_0_), channel_id=1, source_target_pairs={{0,2},{2,4},{4,6},{6,0},{1,3},{3,5},{5,7},{7,1},{8,10},{10,12},{12... | collective-permute-start | bytes 98312 | tf_op jit(solution)/shard_map/ppermute | solution.py:310

commit v2 on v1

--- a/solution.py
+++ b/solution.py
@@ -16,7 +16,7 @@
 POOL = 4
 WIN = 160
 ALIGN = 32
-CHUNK = 512
+CHUNK = 2048
 SHIFTS = 16
 ROWS = 16
 MIB = 1024 * 1024
@@ -246,16 +246,28 @@
             out[n] = pair.astype(out.dtype)
 
 
-def pair_kernel(variants, order, table, *refs):
+def pair_kernel(variants, order, dist_table, *refs):
     row_feats = refs[:variants]
     col_feats = refs[variants : 2 * variants]
-    out, rows, cols, blocks, sems = refs[2 * variants :]
+    out, rows, cols, table, span, blocks, sems = refs[2 * variants :]
     side = cols.shape[1]
     count = rows.shape[1]
     for s in range(variants):
         rows[order[s]] = row_feats[s][...].astype(jnp.float32)
         cols[order[variants + s]] = col_feats[s][...]
 
+    offset = order[2 * variants] + count - 1
+    bucket = lax.broadcasted_iota(jnp.int32, (count + side, NB), 1)
+    distance = jnp.abs(offset - lax.broadcasted_iota(jnp.int32, (count + side, NB), 0))
+    above = distance >= jnp.where(bucket == 0, 0, jnp.left_shift(1, jnp.maximum(bucket - 1, 0)))
+    below = jnp.logical_or(bucket == NB - 1, distance < jnp.left_shift(1, bucket))
+    one_hot = jnp.where(jnp.logical_and(above, below), 1.0, 0.0).astype(jnp.bfloat16)
+    span[...] = jnp.dot(
+        one_hot, dist_table[...].astype(jnp.bfloat16), preferred_element_type=jnp.float32
+    )
+    for s in range(SHIFTS):
+        table[s] = span[s : s + count + side - SHIFTS].astype(jnp.bfloat16)
+
     def write(block, slot, variant):
         into = out.at[variant, pl.ds(block * ROWS, ROWS)]
         return pltpu.make_async_copy(blocks.at[slot, variant], into, sems.at[slot, variant])
@@ -264,12 +276,12 @@
         slot = lax.rem(block, 2)
         for variant in range(variants):
             pl.when(block >= 2)(write(block, slot, variant).wait)
+            row_block = rows[variant, pl.ds(pl.multiple_of(block * ROWS, ROWS), ROWS), :]
             for r in range(ROWS):
                 back = count - 1 - (block * ROWS + r)
                 low = pl.multiple_of((back // SHIFTS) * SHIFTS, SHIFTS)
                 relative = table[(count - 1 - r) % SHIFTS, pl.ds(low, side), :]
-                row = rows[variant, pl.ds(block * ROWS + r, 1), :]
-                row = jnp.broadcast_to(row, (SHIFTS, C)).astype(jnp.bfloat16)
+                row = jnp.broadcast_to(row_block[r : r + 1], (SHIFTS, C)).astype(jnp.bfloat16)
                 found = (cols[variant] + relative).reshape(side // SHIFTS, SHIFTS, C) + row[None]
                 blocks[slot, variant, r] = found.reshape(side, C)
             write(block, slot, variant).start()
@@ -280,20 +292,6 @@
     for block in range(max(total - 2, 0), total):
         for variant in range(variants):
             write(block, block % 2, variant).wait()
-
-
-def distance_table(dist_table, row_start, col_start, rows, cols):
-    at = jnp.arange(SHIFTS, dtype=jnp.int32)[:, None] + jnp.arange(
-        rows + cols, dtype=jnp.int32
-    )
-    distance = jnp.abs(row_start - col_start + rows - 1 - at)
-    buckets = jnp.zeros(distance.shape, jnp.int32)
-    for power_index in range(NB - 1):
-        buckets = buckets + (distance >= 2**power_index).astype(jnp.int32)
-    one_hot = (buckets[:, :, None] == jnp.arange(NB, dtype=jnp.int32)).astype(jnp.float32)
-    return jnp.einsum("skb,bc->skc", one_hot, dist_table, precision=lax.Precision.HIGHEST).astype(
-        jnp.bfloat16
-    )
 
 
 def in_hbm(array):
@@ -400,7 +398,6 @@
         *(taps[s] for s in head_order(n_head)),
         *(in_hbm(piece) for piece in pieces + crossed),
     )
-    table = distance_table(dist_table, mine * pair_rows, ours * pair_rows, pair_rows, pair_rows)
 
     chunk = min(tokens, CHUNK)
 
@@ -473,13 +470,19 @@
         scratch_shapes=[
             pltpu.VMEM((variants, pair_rows, C), jnp.float32),
             pltpu.VMEM((variants, pair_rows, C), jnp.bfloat16),
+            pltpu.VMEM((SHIFTS, 2 * pair_rows - SHIFTS, C), jnp.bfloat16),
+            pltpu.VMEM((2 * pair_rows, C), jnp.float32),
             pltpu.VMEM((2, variants, ROWS, pair_rows, C), jnp.bfloat16),
             pltpu.SemaphoreType.DMA((2, variants)),
         ],
         compiler_params=pltpu.CompilerParams(vmem_limit_bytes=24 * MIB),
         name="pair_map",
-    )(jnp.stack(order).astype(jnp.int32) if splits == 1 else jnp.array(order, jnp.int32),
-      table, *row_feats, *col_feats)
+    )(
+        jnp.stack([*order, (mine - ours) * pair_rows]).astype(jnp.int32),
+        dist_table,
+        *row_feats,
+        *col_feats,
+    )
 
 
 def solution(mesh):

time: 121 us -> 118 us (0.975)
  Pallas kernels: 44.1 us -> 39.7 us
  waiting for transfers between devices: 36.7 us -> 39.2 us
  matrix products: 1.81 us -> 0 us
    pallas_call x2, Pallas kernels: 21.2 us -> 16.7 us  [attend(): pl.pallas_call(functools.partial(attend_kernel, heads, own, len(mixing)),...]
    ppermute x12, waiting for transfers between devices: 15 us -> 16.9 us  [shifts(): lax.ppermute(array, axis, [(k, (k + s) % size) for k in range(size)])]
    dot_general x1 -> x0, matrix products: 1.81 us -> none  [distance_table(): jnp.einsum('skb,bc->skc', one_hot, dist_table, precision=lax.Precision.HI...]
  transfers between devices with their start and end apart: 28 -> 28, of which waited for: 10 -> 12; matrix products, arithmetic and copies ran while one was open for 4% -> 3% of each run, Pallas kernels for 18% -> 18%
where the time goes in v2:
time: 118 us; the launch traced here: 117 us
  Pallas kernels  39.7 us (34%)
  waiting for transfers between devices  39.2 us (33%)
  starting transfers between devices  33.5 us (28%)
  local copies, waits for them, and re-layouts  3.04 us (3%)
  other arithmetic  1.31 us (1%)
    ppermute x3, waiting for transfers between devices, gather_rows(): lax.ppermute(array, 'head', [(k, (k + s) % 4) for k in range(4)])  19 us
    ppermute x12, waiting for transfers between devices, shifts(): lax.ppermute(array, axis, [(k, (k + s) % size) for k in range(size)])  16.9 us
    pallas_call x2, Pallas kernels, attend(): pl.pallas_call(functools.partial(attend_kernel, heads, own, len(mixing)),...  16.7 us
    pallas_call x1, Pallas kernels, local(): pl.pallas_call(functools.partial(project_kernel, heads, n_var, n_head, le...  16.3 us
    ppermute x12, starting transfers between devices, shifts(): lax.ppermute(array, axis, [(k, (k + s) % size) for k in range(size)])  15.7 us
    pallas_call x1, Pallas kernels, local(): pl.pallas_call(functools.partial(pair_kernel, variants), out_shape=jax.Sh...  6.76 us
    ppermute x3, starting transfers between devices, gather_rows(): lax.ppermute(array, 'head', [(k, (k + s) % 4) for k in range(4)])  5.84 us
    ppermute x3, starting transfers between devices, local(): summed += lax.ppermute(sent[s - 1], 'head', pairs).astype(jnp.float32)  4.98 us
  transfers between devices with their start and end apart: 28, of which 12 were waited for; matrix products, arithmetic and copies ran while one was open for 3% of the time, Pallas kernels for 18%

profile of v2, /device:TPU:0, one launch (start us, length us, event | category | flops | bytes accessed | tf_op | source)
XLA Modules:
  0.0 117.4 jit_solution(5485514687804214928)
XLA Ops:
  0.0 1.0 copy-done
  1.0 5.1 %collective-permute-start.1 = (bf16[256,384]{1,0:T(8,128)(2,1)S(1)}, bf16[256,384]{1,0:T(8,128)(2,1)S(1)}, u32[]{:S(2)}, u32[]{:S(2)}) collective-permute-start(bf16[256,384]{1,0:T(8,128)(2,1)S(1)} %constant_dynamic-slice_fusion), channel_id=1, source_target_pairs={{0,6},{2,0},{4,2},{6,4},{1,7},{3,1},{5,3},{7,5},{8,14},{10,8},{12,... | collective-permute-start | bytes 589832 | tf_op jit(solution)/shard_map/ppermute | solution.py:320
  6.2 5.2 %collective-permute-done.1 = bf16[256,384]{1,0:T(8,128)(2,1)S(1)} collective-permute-done((bf16[256,384]{1,0:T(8,128)(2,1)S(1)}, bf16[256,384]{1,0:T(8,128)(2,1)S(1)}, u32[]{:S(2)}, u32[]{:S(2)}) %collective-permute-start.1) | collective-permute-done | bytes 196640 | tf_op jit(solution)/shard_map/ppermute | solution.py:320
  11.4 4.0 %collective-permute-done = bf16[256,384]{1,0:T(8,128)(2,1)S(1)} collective-permute-done((bf16[256,384]{1,0:T(8,128)(2,1)S(1)}, bf16[256,384]{1,0:T(8,128)(2,1)S(1)}, u32[]{:S(2)}, u32[]{:S(2)}) %collective-permute-start) | collective-permute-done | bytes 196640 | tf_op jit(solution)/shard_map/ppermute | solution.py:320
  15.4 0.1 pad_maximum_fusion.1
  15.5 1.6 %collective-permute-start.5 = (bf16[3,256,384]{2,1,0:T(8,128)(2,1)S(1)}, bf16[3,256,384]{2,1,0:T(8,128)(2,1)}, u32[]{:S(2)}, u32[]{:S(2)}) collective-permute-start(bf16[3,256,384]{2,1,0:T(8,128)(2,1)S(1)} %pad_maximum_fusion.1), channel_id=1, source_target_pairs={{0,8},{8,0},{16,24},{24,16},{1,9},{9,1},{17,25},{25,17},{2,10},{10... | collective-permute-start | bytes 1769480 | tf_op jit(solution)/shard_map/ppermute | solution.py:321
  17.0 1.5 %collective-permute-start.2 = (bf16[3,256,384]{2,1,0:T(8,128)(2,1)S(1)}, bf16[3,256,384]{2,1,0:T(8,128)(2,1)S(1)}, u32[]{:S(2)}, u32[]{:S(2)}) collective-permute-start(bf16[3,256,384]{2,1,0:T(8,128)(2,1)S(1)} %pad_maximum_fusion.1), channel_id=1, source_target_pairs={{0,16},{8,24},{16,0},{24,8},{1,17},{9,25},{17,1},{25,9},{2,18},{10... | collective-permute-start | bytes 1769480 | tf_op jit(solution)/shard_map/ppermute | solution.py:321
  18.6 0.7 collective-permute-start.3
  19.3 9.8 %collective-permute-done.3 = bf16[256,384]{1,0:T(8,128)(2,1)} collective-permute-done((bf16[256,384]{1,0:T(8,128)(2,1)S(1)}, bf16[256,384]{1,0:T(8,128)(2,1)}, u32[]{:S(2)}, u32[]{:S(2)}) %collective-permute-start.3) | collective-permute-done | bytes 196640 | tf_op jit(solution)/shard_map/ppermute | solution.py:320
  29.1 0.5 collective-permute-start.6
  29.6 0.5 collective-permute-start.4
  30.1 1.1 pad_maximum_fusion.refs_4_
  31.2 0.1 collective-permute-start.8
  31.3 1.3 %constant_dynamic-update-slice_fusion.3 = bf16[4,256,384]{2,1,0:T(8,128)(2,1)S(1)} fusion(bf16[3,256,384]{2,1,0:T(8,128)(2,1)} %collective-permute-done.5), kind=kLoop, calls=%fused_computation.13 | loop fusion | bytes 1179648
  32.6 2.4 %collective-permute-done.6 = bf16[1,256,384]{2,1,0:T(8,128)(2,1)S(1)} collective-permute-done((bf16[1,256,384]{2,1,0:T(8,128)(2,1)}, bf16[1,256,384]{2,1,0:T(8,128)(2,1)S(1)}, u32[]{:S(2)}, u32[]{:S(2)}) %collective-permute-start.6) | collective-permute-done | bytes 196640 | tf_op jit(solution)/shard_map/ppermute | solution.py:321
  35.1 0.1 constant_dynamic-update-slice_fusion.1
  35.2 0.3 collective-permute-done.4
  35.6 0.1 broadcast_select_fusion
  35.7 1.6 %collective-permute-start.7 = (bf16[4,256,384]{2,1,0:T(8,128)(2,1)S(1)}, bf16[4,256,384]{2,1,0:T(8,128)(2,1)}, u32[]{:S(2)}, u32[]{:S(2)}) collective-permute-start(bf16[4,256,384]{2,1,0:T(8,128)(2,1)S(1)} %broadcast_select_fusion), channel_id=1, source_target_pairs={{0,8},{1,17},{8,0},{9,25},{16,24},{17,1},{24,16},{25,9},{2,10},{3,... | collective-permute-start | bytes 2359304 | tf_op jit(solution)/shard_map/ppermute | solution.py:331
  37.2 0.5 collective-permute-start.9
  37.7 1.2 %collective-permute-start.13 = (f32[4,384]{1,0:T(4,128)S(1)}, f32[4,384]{1,0:T(4,128)S(1)}, u32[]{:S(2)}, u32[]{:S(2)}) collective-permute-start(f32[4,384]{1,0:T(4,128)S(1)} %pad_maximum_fusion.2.refs_0_), channel_id=1, source_target_pairs={{0,6},{2,0},{4,2},{6,4},{1,7},{3,1},{5,3},{7,5},{8,14},{10,8},{12,... | collective-permute-start | bytes 18440 | tf_op jit(solution)/shard_map/ppermute | solution.py:308
  39.0 2.4 %collective-permute-done.13.refs_2_ = f32[4,384]{1,0:T(4,128)S(1)} collective-permute-done((f32[4,384]{1,0:T(4,128)S(1)}, f32[4,384]{1,0:T(4,128)S(1)}, u32[]{:S(2)}, u32[]{:S(2)}) %collective-permute-start.13) | collective-permute-done | bytes 6176 | tf_op jit(solution)/shard_map/ppermute | solution.py:308
  41.4 4.5 %collective-permute-done.12.refs_3_ = f32[4,384]{1,0:T(4,128)S(1)} collective-permute-done((f32[4,384]{1,0:T(4,128)S(1)}, f32[4,384]{1,0:T(4,128)S(1)}, u32[]{:S(2)}, u32[]{:S(2)}) %collective-permute-start.12) | collective-permute-done | bytes 6176 | tf_op jit(solution)/shard_map/ppermute | solution.py:308
  46.0 0.6 collective-permute-start.11
  46.6 4.8 %collective-permute-done.11.refs_1_ = f32[4,384]{1,0:T(4,128)S(1)} collective-permute-done((f32[4,384]{1,0:T(4,128)S(1)}, f32[4,384]{1,0:T(4,128)S(1)}, u32[]{:S(2)}, u32[]{:S(2)}) %collective-permute-start.11) | collective-permute-done | bytes 6176 | tf_op jit(solution)/shard_map/ppermute | solution.py:308
  51.4 0.1 collective-permute-start.14
  51.5 1.2 %collective-permute-start.17 = (bf16[384,256]{1,0:T(8,128)(2,1)S(1)}, bf16[384,256]{1,0:T(8,128)(2,1)S(1)}, u32[]{:S(2)}, u32[]{:S(2)}) collective-permute-start(bf16[384,256]{1,0:T(8,128)(2,1)S(1)} %copy-done.3), channel_id=1, source_target_pairs={{0,6},{2,0},{4,2},{6,4},{1,7},{3,1},{5,3},{7,5},{8,14},{10,8},{12,... | collective-permute-start | bytes 589832 | tf_op jit(solution)/shard_map/ppermute | solution.py:308
  52.8 1.0 collective-permute-start.15
  53.9 0.2 dynamic-slice_reduce_fusion
  54.1 0.1 concatenate.24.order
  54.2 0.1 concatenate.19.scalars
  54.3 16.3 %project.1 = (bf16[2048,1024]{1,0:T(8,128)(2,1)S(1)}, f32[512,384]{1,0:T(8,128)S(1)}) custom-call(s32[8]{0:T(128)S(1)} %concatenate.19.scalars, bf16[1536,896]{1,0:T(8,128)(2,1)} %w_proj.1, f32[4,384]{1,0:T(4,128)S(1)} %pad_maximum_fusion.2.refs_0_, f32[4,384]{1,0:T(4,128)S(1)} %collective-permute-done.11.refs_1_, ...), custom_call_target="tpu_custom_call" | custom-call | flops 7952400384 | bytes 12582912 | tf_op jit(solution)/shard_map/project/pallas_call | solution.py:370
  70.6 12.2 %attend.2 = (bf16[3,128,256]{2,1,0:T(8,128)(2,1)S(1)}, bf16[2,256,256]{2,1,0:T(8,128)(2,1)S(1)}) custom-call(s32[7]{0:T(128)S(1)} %concatenate.24.order, bf16[2048,1024]{1,0:T(8,128)(2,1)S(1)} %get-tuple-element.25.kvq, f32[512,384]{1,0:T(8,128)S(1)} %get-tuple-element.26.pooled, bf16[384,1536]{1,0:T(8,128)(2,1)S(1)} %copy-done.2, ...), custom_call_target="tpu_custom_call" | custom-call | flops 6442450944 | bytes 4194304 | tf_op jit(solution)/shard_map/attend/pallas_call | solution.py:416
  82.9 2.7 %collective-permute-start.18 = (bf16[128,256]{1,0:T(8,128)(2,1)S(1)}, bf16[128,256]{1,0:T(8,128)(2,1)S(1)}, u32[]{:S(2)}, u32[]{:S(2)}) collective-permute-start(bf16[128,256]{1,0:T(8,128)(2,1)S(1)} %get-tuple-element.29), channel_id=1, source_target_pairs={{0,2},{2,4},{4,6},{6,0},{1,3},{3,5},{5,7},{7,1},{8,10},{10,12},{12... | collective-permute-start | bytes 196616 | tf_op jit(solution)/shard_map/ppermute | solution.py:445
  85.5 1.2 %collective-permute-start.20 = (bf16[128,256]{1,0:T(8,128)(2,1)S(1)}, bf16[128,256]{1,0:T(8,128)(2,1)S(1)}, u32[]{:S(2)}, u32[]{:S(2)}) collective-permute-start(bf16[128,256]{1,0:T(8,128)(2,1)S(1)} %get-tuple-element.30), channel_id=1, source_target_pairs={{0,6},{2,0},{4,2},{6,4},{1,7},{3,1},{5,3},{7,5},{8,14},{10,8},{12,... | collective-permute-start | bytes 196616 | tf_op jit(solution)/shard_map/ppermute | solution.py:445
  86.8 1.1 collective-permute-start.19
  87.9 4.4 %attend.3 = f32[1,128,256]{2,1,0:T(8,128)S(1)} custom-call(s32[1]{0:T(128)} %bitcast.9.order, bf16[2048,1024]{1,0:T(8,128)(2,1)S(1)} %get-tuple-element.25.kvq, f32[512,384]{1,0:T(8,128)S(1)} %get-tuple-element.26.pooled, bf16[2,256,256]{2,1,0:T(8,128)(2,1)S(1)} %get-tuple-element.27.refs_0_, bf16[384,256]{1,0:T(8,128)(2,1)S(1)} %copy-done.3), custom_call_target="tpu_custom_call" | custom-call | flops 2147483648 | bytes 4194304 | tf_op jit(solution)/shard_map/attend/pallas_call | solution.py:416
  92.3 0.6 collective-permute-done.19
  93.0 0.7 collective-permute-start.21
  93.7 5.9 %collective-permute-start.27 = (bf16[128,128]{1,0:T(8,128)(2,1)S(1)}, bf16[128,128]{1,0:T(8,128)(2,1)S(1)}, u32[]{:S(2)}, u32[]{:S(2)}) collective-permute-start(bf16[128,128]{1,0:T(8,128)(2,1)S(1)} %get-tuple-element.32.refs_4_), channel_id=1, source_target_pairs={{0,24},{8,0},{16,8},{24,16},{1,25},{9,1},{17,9},{25,17},{2,26},{10... | collective-permute-start | bytes 98312 | tf_op jit(solution)/shard_map/ppermute | solution.py:308
  99.6 0.6 collective-permute-start.25
  100.2 4.4 %collective-permute-start.24 = (bf16[128,128]{1,0:T(8,128)(2,1)S(1)}, bf16[128,128]{1,0:T(8,128)(2,1)S(1)}, u32[]{:S(2)}, u32[]{:S(2)}) collective-permute-start(bf16[128,128]{1,0:T(8,128)(2,1)S(1)} %collective-permute-done.21.refs_0_), channel_id=1, source_target_pairs={{0,6},{2,0},{4,2},{6,4},{1,7},{3,1},{5,3},{7,5},{8,14},{10,8},{12,... | collective-permute-start | bytes 98312 | tf_op jit(solution)/shard_map/ppermute | solution.py:308
  104.7 0.6 collective-permute-start.22
  105.2 0.1 stack.71.order
  105.3 0.9 collective-permute-done.24.refs_3_
  106.3 3.2 %collective-permute-done.23.refs_2_ = bf16[128,128]{1,0:T(8,128)(2,1)S(1)} collective-permute-done((bf16[128,128]{1,0:T(8,128)(2,1)S(1)}, bf16[128,128]{1,0:T(8,128)(2,1)S(1)}, u32[]{:S(2)}, u32[]{:S(2)}) %collective-permute-start.23) | collective-permute-done | bytes 32800 | tf_op jit(solution)/shard_map/ppermute | solution.py:308
  109.5 0.9 collective-permute-done.22.refs_1_
  110.4 6.8 %pair_map.1 = bf16[4,128,128,128]{3,2,1,0:T(8,128)(2,1)} custom-call(s32[9]{0:T(128)S(1)} %stack.71.order, f32[16,128]{1,0:T(8,128)S(1)} %copy-done.1, bf16[128,128]{1,0:T(8,128)(2,1)S(1)} %collective-permute-done.21.refs_0_, bf16[128,128]{1,0:T(8,128)(2,1)S(1)} %collective-permute-done.22.refs_1_, bf16[128,128]{1,0:T(8,128)(2,1)S(1)} %collective-permute-done.23.refs_2_, ...), custom_call_target="tpu_custom_call" | custom-call | tf_op jit(solution)/shard_map/pair_map/pallas_call | solution.py:465
  (57 shorter events, 0.4 us)
Async XLA Ops:
  0.0 1.0 copy-start
  1.0 10.4 %collective-permute-start.1 = (bf16[256,384]{1,0:T(8,128)(2,1)S(1)}, bf16[256,384]{1,0:T(8,128)(2,1)S(1)}, u32[]{:S(2)}, u32[]{:S(2)}) collective-permute-start(bf16[256,384]{1,0:T(8,128)(2,1)S(1)} %constant_dynamic-slice_fusion), channel_id=1, source_target_pairs={{0,6},{2,0},{4,2},{6,4},{1,7},{3,1},{5,3},{7,5},{8,14},{10,8},{12,... | collective-permute-start | bytes 589832 | tf_op jit(solution)/shard_map/ppermute | solution.py:320
  6.1 9.3 %collective-permute-start = (bf16[256,384]{1,0:T(8,128)(2,1)S(1)}, bf16[256,384]{1,0:T(8,128)(2,1)S(1)}, u32[]{:S(2)}, u32[]{:S(2)}) collective-permute-start(bf16[256,384]{1,0:T(8,128)(2,1)S(1)} %constant_dynamic-slice_fusion), channel_id=1, source_target_pairs={{0,2},{2,4},{4,6},{6,0},{1,3},{3,5},{5,7},{7,1},{8,10},{10,12},{12... | collective-permute-start | bytes 589832 | tf_op jit(solution)/shard_map/ppermute | solution.py:320
  6.2 31.6 %copy-start.8 = (f32[384]{0:T(512)S(1)}, f32[384]{0:T(512)}, u32[]{:S(2)}) copy-start(f32[384]{0:T(512)} %param.11) | copy-start | bytes 4612
  6.2 31.6 %copy-start.7 = (f32[3,384]{1,0:T(4,128)S(1)}, f32[3,384]{1,0:T(4,128)}, u32[]{:S(2)}) copy-start(f32[3,384]{1,0:T(4,128)} %param.10) | copy-start | bytes 13828
  6.2 45.4 %copy-start.3 = (bf16[384,256]{1,0:T(8,128)(2,1)S(1)}, bf16[384,256]{1,0:T(8,128)(2,1)}, u32[]{:S(2)}) copy-start(bf16[384,256]{1,0:T(8,128)(2,1)} %refs_1_.3) | copy-start | bytes 589828
  15.4 38.5 %copy-start.9 = (s32[4,2]{0,1:T(2,128)S(1)}, s32[4,2]{0,1:T(2,128)}, u32[]{:S(2)}) copy-start(s32[4,2]{0,1:T(2,128)} %param.9) | copy-start | bytes 100
  15.5 15.8 %collective-permute-start.5 = (bf16[3,256,384]{2,1,0:T(8,128)(2,1)S(1)}, bf16[3,256,384]{2,1,0:T(8,128)(2,1)}, u32[]{:S(2)}, u32[]{:S(2)}) collective-permute-start(bf16[3,256,384]{2,1,0:T(8,128)(2,1)S(1)} %pad_maximum_fusion.1), channel_id=1, source_target_pairs={{0,8},{8,0},{16,24},{24,16},{1,9},{9,1},{17,25},{25,17},{2,10},{10... | collective-permute-start | bytes 1769480 | tf_op jit(solution)/shard_map/ppermute | solution.py:321
  17.0 18.1 %collective-permute-start.2 = (bf16[3,256,384]{2,1,0:T(8,128)(2,1)S(1)}, bf16[3,256,384]{2,1,0:T(8,128)(2,1)S(1)}, u32[]{:S(2)}, u32[]{:S(2)}) collective-permute-start(bf16[3,256,384]{2,1,0:T(8,128)(2,1)S(1)} %pad_maximum_fusion.1), channel_id=1, source_target_pairs={{0,16},{8,24},{16,0},{24,8},{1,17},{9,25},{17,1},{25,9},{2,18},{10... | collective-permute-start | bytes 1769480 | tf_op jit(solution)/shard_map/ppermute | solution.py:321
  18.6 10.5 %collective-permute-start.3 = (bf16[256,384]{1,0:T(8,128)(2,1)S(1)}, bf16[256,384]{1,0:T(8,128)(2,1)}, u32[]{:S(2)}, u32[]{:S(2)}) collective-permute-start(bf16[256,384]{1,0:T(8,128)(2,1)S(1)} %constant_dynamic-slice_fusion), channel_id=1, source_target_pairs={{0,4},{2,6},{4,0},{6,2},{1,5},{3,7},{5,1},{7,3},{8,12},{10,14},{12... | collective-permute-start | bytes 589832 | tf_op jit(solution)/shard_map/ppermute | solution.py:320
  29.1 6.0 %collective-permute-start.6 = (bf16[1,256,384]{2,1,0:T(8,128)(2,1)}, bf16[1,256,384]{2,1,0:T(8,128)(2,1)S(1)}, u32[]{:S(2)}, u32[]{:S(2)}) collective-permute-start(bf16[1,256,384]{2,1,0:T(8,128)(2,1)} %bitcast.18), channel_id=1, source_target_pairs={{0,8},{8,0},{16,24},{24,16},{1,9},{9,1},{17,25},{25,17},{2,10},{10... | collective-permute-start | bytes 589832 | tf_op jit(solution)/shard_map/ppermute | solution.py:321
  29.6 5.9 %collective-permute-start.4 = (bf16[1,256,384]{2,1,0:T(8,128)(2,1)}, bf16[1,256,384]{2,1,0:T(8,128)(2,1)S(1)}, u32[]{:S(2)}, u32[]{:S(2)}) collective-permute-start(bf16[1,256,384]{2,1,0:T(8,128)(2,1)} %bitcast.18), channel_id=1, source_target_pairs={{0,16},{8,24},{16,0},{24,8},{1,17},{9,25},{17,1},{25,9},{2,18},{10... | collective-permute-start | bytes 589832 | tf_op jit(solution)/shard_map/ppermute | solution.py:321
  31.2 21.5 %copy-start.6 = (bf16[4,256,384]{2,1,0:T(8,128)(2,1)}, bf16[4,256,384]{2,1,0:T(8,128)(2,1)S(1)}, u32[]{:S(2)}) copy-start(bf16[4,256,384]{2,1,0:T(8,128)(2,1)S(1)} %pad_maximum_fusion.refs_4_) | copy-start | bytes 2359300
  31.2 20.2 %collective-permute-start.8 = (bf16[4,256,384]{2,1,0:T(8,128)(2,1)S(1)}, bf16[4,256,384]{2,1,0:T(8,128)(2,1)S(1)}, u32[]{:S(2)}, u32[]{:S(2)}) collective-permute-start(bf16[4,256,384]{2,1,0:T(8,128)(2,1)S(1)} %pad_maximum_fusion.refs_4_), channel_id=1, source_target_pairs={{0,1},{1,0},{2,3},{3,2},{4,5},{5,4},{6,7},{7,6},{8,9},{9,8},{10,11... | collective-permute-start | bytes 2359304 | tf_op jit(solution)/shard_map/ppermute | solution.py:318
  35.1 19.2 %copy-start.5 = (bf16[4,256,384]{2,1,0:T(8,128)(2,1)}, bf16[4,256,384]{2,1,0:T(8,128)(2,1)S(1)}, u32[]{:S(2)}) copy-start(bf16[4,256,384]{2,1,0:T(8,128)(2,1)S(1)} %constant_dynamic-update-slice_fusion.2.refs_5_) | copy-start | bytes 2359300
  35.5 18.7 %copy-start.4 = (bf16[4,256,384]{2,1,0:T(8,128)(2,1)}, bf16[4,256,384]{2,1,0:T(8,128)(2,1)S(1)}, u32[]{:S(2)}) copy-start(bf16[4,256,384]{2,1,0:T(8,128)(2,1)S(1)} %constant_dynamic-update-slice_fusion.refs_6_) | copy-start | bytes 2359300
  35.7 15.7 %collective-permute-start.7 = (bf16[4,256,384]{2,1,0:T(8,128)(2,1)S(1)}, bf16[4,256,384]{2,1,0:T(8,128)(2,1)}, u32[]{:S(2)}, u32[]{:S(2)}) collective-permute-start(bf16[4,256,384]{2,1,0:T(8,128)(2,1)S(1)} %broadcast_select_fusion), channel_id=1, source_target_pairs={{0,8},{1,17},{8,0},{9,25},{16,24},{17,1},{24,16},{25,9},{2,10},{3,... | collective-permute-start | bytes 2359304 | tf_op jit(solution)/shard_map/ppermute | solution.py:331
  37.2 14.2 %collective-permute-start.10 = (bf16[4,256,384]{2,1,0:T(8,128)(2,1)S(1)}, bf16[4,256,384]{2,1,0:T(8,128)(2,1)S(1)}, u32[]{:S(2)}, u32[]{:S(2)}) collective-permute-start(bf16[4,256,384]{2,1,0:T(8,128)(2,1)S(1)} %constant_dynamic-update-slice_fusion.refs_6_), channel_id=1, source_target_pairs={{0,1},{1,0},{2,3},{3,2},{4,5},{5,4},{6,7},{7,6},{8,9},{9,8},{10,11... | collective-permute-start | bytes 2359304 | tf_op jit(solution)/shard_map/ppermute | solution.py:318
  37.2 14.2 %collective-permute-start.9 = (bf16[4,256,384]{2,1,0:T(8,128)(2,1)S(1)}, bf16[4,256,384]{2,1,0:T(8,128)(2,1)S(1)}, u32[]{:S(2)}, u32[]{:S(2)}) collective-permute-start(bf16[4,256,384]{2,1,0:T(8,128)(2,1)S(1)} %constant_dynamic-update-slice_fusion.2.refs_5_), channel_id=1, source_target_pairs={{0,1},{1,0},{2,3},{3,2},{4,5},{5,4},{6,7},{7,6},{8,9},{9,8},{10,11... | collective-permute-start | bytes 2359304 | tf_op jit(solution)/shard_map/ppermute | solution.py:318
  37.7 3.7 %collective-permute-start.13 = (f32[4,384]{1,0:T(4,128)S(1)}, f32[4,384]{1,0:T(4,128)S(1)}, u32[]{:S(2)}, u32[]{:S(2)}) collective-permute-start(f32[4,384]{1,0:T(4,128)S(1)} %pad_maximum_fusion.2.refs_0_), channel_id=1, source_target_pairs={{0,6},{2,0},{4,2},{6,4},{1,7},{3,1},{5,3},{7,5},{8,14},{10,8},{12,... | collective-permute-start | bytes 18440 | tf_op jit(solution)/shard_map/ppermute | solution.py:308
  41.4 4.5 %collective-permute-start.12 = (f32[4,384]{1,0:T(4,128)S(1)}, f32[4,384]{1,0:T(4,128)S(1)}, u32[]{:S(2)}, u32[]{:S(2)}) collective-permute-start(f32[4,384]{1,0:T(4,128)S(1)} %pad_maximum_fusion.2.refs_0_), channel_id=1, source_target_pairs={{0,4},{2,6},{4,0},{6,2},{1,5},{3,7},{5,1},{7,3},{8,12},{10,14},{12... | collective-permute-start | bytes 18440 | tf_op jit(solution)/shard_map/ppermute | solution.py:308
  46.0 5.4 %collective-permute-start.11 = (f32[4,384]{1,0:T(4,128)S(1)}, f32[4,384]{1,0:T(4,128)S(1)}, u32[]{:S(2)}, u32[]{:S(2)}) collective-permute-start(f32[4,384]{1,0:T(4,128)S(1)} %pad_maximum_fusion.2.refs_0_), channel_id=1, source_target_pairs={{0,2},{2,4},{4,6},{6,0},{1,3},{3,5},{5,7},{7,1},{8,10},{10,12},{12... | collective-permute-start | bytes 18440 | tf_op jit(solution)/shard_map/ppermute | solution.py:308
  51.4 1.4 %copy-start.10 = (bf16[4,256,384]{2,1,0:T(8,128)(2,1)}, bf16[4,256,384]{2,1,0:T(8,128)(2,1)S(1)}, u32[]{:S(2)}) copy-start(bf16[4,256,384]{2,1,0:T(8,128)(2,1)S(1)} %collective-permute-done.8.refs_8_) | copy-start | bytes 2359300
  51.4 1.4 %copy-start.11 = (bf16[4,256,384]{2,1,0:T(8,128)(2,1)}, bf16[4,256,384]{2,1,0:T(8,128)(2,1)S(1)}, u32[]{:S(2)}) copy-start(bf16[4,256,384]{2,1,0:T(8,128)(2,1)S(1)} %collective-permute-done.10.refs_10_) | copy-start | bytes 2359300
  51.4 1.4 %copy-start.12 = (bf16[4,256,384]{2,1,0:T(8,128)(2,1)}, bf16[4,256,384]{2,1,0:T(8,128)(2,1)S(1)}, u32[]{:S(2)}) copy-start(bf16[4,256,384]{2,1,0:T(8,128)(2,1)S(1)} %collective-permute-done.9.refs_9_) | copy-start | bytes 2359300
  51.4 2.8 %collective-permute-start.14 = (bf16[4,256,384]{2,1,0:T(8,128)(2,1)}, bf16[4,256,384]{2,1,0:T(8,128)(2,1)}, u32[]{:S(2)}, u32[]{:S(2)}) collective-permute-start(bf16[4,256,384]{2,1,0:T(8,128)(2,1)} %collective-permute-done.7.refs_7_), channel_id=1, source_target_pairs={{0,1},{1,0},{2,3},{3,2},{4,5},{5,4},{6,7},{7,6},{8,9},{9,8},{10,11... | collective-permute-start | bytes 2359304 | tf_op jit(solution)/shard_map/ppermute | solution.py:318
  51.5 19.1 %collective-permute-start.17 = (bf16[384,256]{1,0:T(8,128)(2,1)S(1)}, bf16[384,256]{1,0:T(8,128)(2,1)S(1)}, u32[]{:S(2)}, u32[]{:S(2)}) collective-permute-start(bf16[384,256]{1,0:T(8,128)(2,1)S(1)} %copy-done.3), channel_id=1, source_target_pairs={{0,6},{2,0},{4,2},{6,4},{1,7},{3,1},{5,3},{7,5},{8,14},{10,8},{12,... | collective-permute-start | bytes 589832 | tf_op jit(solution)/shard_map/ppermute | solution.py:308
  52.8 17.8 %collective-permute-start.16 = (bf16[384,256]{1,0:T(8,128)(2,1)S(1)}, bf16[384,256]{1,0:T(8,128)(2,1)S(1)}, u32[]{:S(2)}, u32[]{:S(2)}) collective-permute-start(bf16[384,256]{1,0:T(8,128)(2,1)S(1)} %copy-done.3), channel_id=1, source_target_pairs={{0,4},{2,6},{4,0},{6,2},{1,5},{3,7},{5,1},{7,3},{8,12},{10,14},{12... | collective-permute-start | bytes 589832 | tf_op jit(solution)/shard_map/ppermute | solution.py:308
  52.8 17.8 %collective-permute-start.15 = (bf16[384,256]{1,0:T(8,128)(2,1)S(1)}, bf16[384,256]{1,0:T(8,128)(2,1)S(1)}, u32[]{:S(2)}, u32[]{:S(2)}) collective-permute-start(bf16[384,256]{1,0:T(8,128)(2,1)S(1)} %copy-done.3), channel_id=1, source_target_pairs={{0,2},{2,4},{4,6},{6,0},{1,3},{3,5},{5,7},{7,1},{8,10},{10,12},{12... | collective-permute-start | bytes 589832 | tf_op jit(solution)/shard_map/ppermute | solution.py:308
  54.2 16.4 %copy-start.2 = (bf16[384,1536]{1,0:T(8,128)(2,1)S(1)}, bf16[384,1536]{1,0:T(8,128)(2,1)}, u32[]{:S(2)}) copy-start(bf16[384,1536]{1,0:T(8,128)(2,1)} %refs_0_.1) | copy-start | bytes 3538948
  82.9 9.4 %collective-permute-start.18 = (bf16[128,256]{1,0:T(8,128)(2,1)S(1)}, bf16[128,256]{1,0:T(8,128)(2,1)S(1)}, u32[]{:S(2)}, u32[]{:S(2)}) collective-permute-start(bf16[128,256]{1,0:T(8,128)(2,1)S(1)} %get-tuple-element.29), channel_id=1, source_target_pairs={{0,2},{2,4},{4,6},{6,0},{1,3},{3,5},{5,7},{7,1},{8,10},{10,12},{12... | collective-permute-start | bytes 196616 | tf_op jit(solution)/shard_map/ppermute | solution.py:445
  85.5 6.8 %collective-permute-start.20 = (bf16[128,256]{1,0:T(8,128)(2,1)S(1)}, bf16[128,256]{1,0:T(8,128)(2,1)S(1)}, u32[]{:S(2)}, u32[]{:S(2)}) collective-permute-start(bf16[128,256]{1,0:T(8,128)(2,1)S(1)} %get-tuple-element.30), channel_id=1, source_target_pairs={{0,6},{2,0},{4,2},{6,4},{1,7},{3,1},{5,3},{7,5},{8,14},{10,8},{12,... | collective-permute-start | bytes 196616 | tf_op jit(solution)/shard_map/ppermute | solution.py:445
  86.8 6.2 %collective-permute-start.19 = (bf16[128,256]{1,0:T(8,128)(2,1)S(1)}, bf16[128,256]{1,0:T(8,128)(2,1)S(1)}, u32[]{:S(2)}, u32[]{:S(2)}) collective-permute-start(bf16[128,256]{1,0:T(8,128)(2,1)S(1)} %get-tuple-element.31), channel_id=1, source_target_pairs={{0,4},{2,6},{4,0},{6,2},{1,5},{3,7},{5,1},{7,3},{8,12},{10,14},{12... | collective-permute-start | bytes 196616 | tf_op jit(solution)/shard_map/ppermute | solution.py:445
  87.9 22.5 %copy-start.1 = (f32[16,128]{1,0:T(8,128)S(1)}, f32[16,128]{1,0:T(8,128)}, u32[]{:S(2)}) copy-start(f32[16,128]{1,0:T(8,128)} %dist_table.1) | copy-start | bytes 24580
  93.0 7.3 %collective-permute-start.21 = (bf16[128,128]{1,0:T(8,128)(2,1)S(1)}, bf16[128,128]{1,0:T(8,128)(2,1)S(1)}, u32[]{:S(2)}, u32[]{:S(2)}) collective-permute-start(bf16[128,128]{1,0:T(8,128)(2,1)S(1)} %get-tuple-element.33), channel_id=1, source_target_pairs={{0,0},{2,8},{4,16},{6,24},{8,2},{10,10},{12,18},{14,26},{16,4},{18... | collective-permute-start | bytes 98312 | tf_op jit(solution)/shard_map/ppermute | solution.py:446
  93.7 11.0 %collective-permute-start.27 = (bf16[128,128]{1,0:T(8,128)(2,1)S(1)}, bf16[128,128]{1,0:T(8,128)(2,1)S(1)}, u32[]{:S(2)}, u32[]{:S(2)}) collective-permute-start(bf16[128,128]{1,0:T(8,128)(2,1)S(1)} %get-tuple-element.32.refs_4_), channel_id=1, source_target_pairs={{0,24},{8,0},{16,8},{24,16},{1,25},{9,1},{17,9},{25,17},{2,26},{10... | collective-permute-start | bytes 98312 | tf_op jit(solution)/shard_map/ppermute | solution.py:308
  99.6 5.7 %collective-permute-start.26 = (bf16[128,128]{1,0:T(8,128)(2,1)S(1)}, bf16[128,128]{1,0:T(8,128)(2,1)S(1)}, u32[]{:S(2)}, u32[]{:S(2)}) collective-permute-start(bf16[128,128]{1,0:T(8,128)(2,1)S(1)} %get-tuple-element.32.refs_4_), channel_id=1, source_target_pairs={{0,16},{8,24},{16,0},{24,8},{1,17},{9,25},{17,1},{25,9},{2,18},{10... | collective-permute-start | bytes 98312 | tf_op jit(solution)/shard_map/ppermute | solution.py:308
  99.6 5.7 %collective-permute-start.25 = (bf16[128,128]{1,0:T(8,128)(2,1)S(1)}, bf16[128,128]{1,0:T(8,128)(2,1)S(1)}, u32[]{:S(2)}, u32[]{:S(2)}) collective-permute-start(bf16[128,128]{1,0:T(8,128)(2,1)S(1)} %get-tuple-element.32.refs_4_), channel_id=1, source_target_pairs={{0,8},{8,16},{16,24},{24,0},{1,9},{9,17},{17,25},{25,1},{2,10},{10... | collective-permute-start | bytes 98312 | tf_op jit(solution)/shard_map/ppermute | solution.py:308
  100.2 6.0 %collective-permute-start.24 = (bf16[128,128]{1,0:T(8,128)(2,1)S(1)}, bf16[128,128]{1,0:T(8,128)(2,1)S(1)}, u32[]{:S(2)}, u32[]{:S(2)}) collective-permute-start(bf16[128,128]{1,0:T(8,128)(2,1)S(1)} %collective-permute-done.21.refs_0_), channel_id=1, source_target_pairs={{0,6},{2,0},{4,2},{6,4},{1,7},{3,1},{5,3},{7,5},{8,14},{10,8},{12,... | collective-permute-start | bytes 98312 | tf_op jit(solution)/shard_map/ppermute | solution.py:308
  104.7 4.8 %collective-permute-start.23 = (bf16[128,128]{1,0:T(8,128)(2,1)S(1)}, bf16[128,128]{1,0:T(8,128)(2,1)S(1)}, u32[]{:S(2)}, u32[]{:S(2)}) collective-permute-start(bf16[128,128]{1,0:T(8,128)(2,1)S(1)} %collective-permute-done.21.refs_0_), channel_id=1, source_target_pairs={{0,4},{2,6},{4,0},{6,2},{1,5},{3,7},{5,1},{7,3},{8,12},{10,14},{12... | collective-permute-start | bytes 98312 | tf_op jit(solution)/shard_map/ppermute | solution.py:308
  104.7 5.7 %collective-permute-start.22 = (bf16[128,128]{1,0:T(8,128)(2,1)S(1)}, bf16[128,128]{1,0:T(8,128)(2,1)S(1)}, u32[]{:S(2)}, u32[]{:S(2)}) collective-permute-start(bf16[128,128]{1,0:T(8,128)(2,1)S(1)} %collective-permute-done.21.refs_0_), channel_id=1, source_target_pairs={{0,2},{2,4},{4,6},{6,0},{1,3},{3,5},{5,7},{7,1},{8,10},{10,12},{12... | collective-permute-start | bytes 98312 | tf_op jit(solution)/shard_map/ppermute | solution.py:308

commit v3 on v2

--- a/solution.py
+++ b/solution.py
@@ -39,8 +39,8 @@
 
 
 def project_kernel(heads, n_var, n_head, count, scalars, w_proj, *refs):
-    taps, pieces = refs[:n_head], refs[n_head : n_head + 2 * count]
-    out, pooled_out, given, weights, rows, left, right, sems = refs[n_head + 2 * count :]
+    taps, pieces = refs[0], refs[1 : 1 + 2 * count]
+    out, pooled_out, given, weights, rows, left, right, sems = refs[1 + 2 * count :]
     step, width = pieces[0].shape[1:]
     tokens = rows.shape[1] - 2 * step
     size = step // POOL
@@ -77,7 +77,10 @@
     scale = jnp.where(at >= heads * (HD + VP), QSCALE, 1.0)
     for h in range(heads):
         ones = jnp.where(at == heads * HD + h * VP + VD, 1.0, ones)
-    low_taps = [tap[...].astype(jnp.bfloat16) for tap in taps]
+    low_taps = []
+    for s, back in enumerate(head_order(n_head)):
+        place = jnp.bitwise_xor(ours, lax.rem(ours + n_head - back, n_head)) if n_head == 4 else s
+        low_taps.append(taps[place].astype(jnp.bfloat16))
     for copy in copies:
         copy.wait()
 
@@ -316,7 +319,7 @@
 
 def gather_rows(block, taps, n_ctx, n_var, n_head, core):
     crossing = lambda array: lax.ppermute(array, "var", [(0, 1), (1, 0)])
-    if n_ctx == 4 and n_head == 4 and n_var == 2:
+    if n_head == 4:
         shift = lambda array, s: lax.ppermute(array, "head", [(k, (k + s) % 4) for k in range(4)])
         over = lambda array, bit: lax.ppermute(array, "ctx", [(k, k ^ bit) for k in range(4)])
         near = jnp.stack([block, shift(block, 1), shift(block, 3)])
@@ -330,13 +333,16 @@
         pairs = [(2 * k + c, 2 * (k ^ (c + 1)) + c) for k in range(4) for c in range(2)]
         corner = lax.ppermute(jnp.where(core == 0, over_y, over_x), ("ctx", "var"), pairs)
         pieces = [slab, over_x, over_y]
+        for bit in (1, 2):
+            moved = lax.ppermute(taps, "head", [(k, k ^ bit) for k in range(4)])
+            taps = jnp.concatenate([taps, moved])
         corner, crossed, taps = lax.optimization_barrier(
-            (corner, [crossing(piece) for piece in pieces], shifts(taps, "head"))
+            (corner, [crossing(piece) for piece in pieces], taps)
         )
         return pieces + [corner], crossed + [crossing(corner)], taps
     pieces = shifts(jnp.stack(shifts(block, "head")), "ctx")
     crossed = [crossing(piece) for piece in pieces]
-    return pieces, crossed, shifts(taps, "head")
+    return pieces, crossed, jnp.concatenate(shifts(taps, "head"))
 
 
 def local(sequence, deletions, conv_taps, conv_bias, w_proj, w_out, w_pair, dist_table):
@@ -374,7 +380,7 @@
             jax.ShapeDtypeStruct((tokens // POOL, width), jnp.float32),
         ),
         in_specs=[whole(pltpu.SMEM), whole(pltpu.HBM)]
-        + [whole()] * n_head
+        + [whole()]
         + [whole(pltpu.HBM)] * (2 * len(pieces)),
         out_specs=(whole(), whole()),
         scratch_shapes=[
@@ -395,7 +401,7 @@
     )(
         scalars,
         in_hbm(w_proj),
-        *(taps[s] for s in head_order(n_head)),
+        taps.reshape(n_head, 4, width),
         *(in_hbm(piece) for piece in pieces + crossed),
     )
 

time: 118 us -> 115 us (0.975)
  starting transfers between devices: 33.5 us -> 31.8 us
    ppermute x12 -> x9, waiting for transfers between devices: 16.9 us -> 6.04 us  [shifts(): lax.ppermute(array, axis, [(k, (k + s) % size) for k in range(size)])]
    ppermute x0 -> x2, waiting for transfers between devices: none -> 7.83 us  [gather_rows(): moved = lax.ppermute(taps, 'head', [(k, k ^ bit) for k in range(4)])]
    ppermute x1, waiting for transfers between devices: 0.01 us -> 1.67 us  [gather_rows(): lax.ppermute(jnp.where(core == 0, over_y, over_x), ('ctx', 'var'), pairs)]
    ppermute x12 -> x9, starting transfers between devices: 15.7 us -> 14.6 us  [shifts(): lax.ppermute(array, axis, [(k, (k + s) % size) for k in range(size)])]
  transfers between devices with their start and end apart: 28 -> 27, of which waited for: 12 -> 13; matrix products, arithmetic and copies ran while one was open for 3% -> 3% of each run, Pallas kernels for 18% -> 18%
where the time goes in v3:
time: 115 us
  Pallas kernels  39.7 us (35%)
  waiting for transfers between devices  38.1 us (33%)
  starting transfers between devices  31.8 us (28%)
  local copies, waits for them, and re-layouts  3.02 us (3%)
  other arithmetic  1.34 us (1%)
    ppermute x3, waiting for transfers between devices, gather_rows(): lax.ppermute(array, 'head', [(k, (k + s) % 4) for k in range(4)])  19 us
    pallas_call x2, Pallas kernels, attend(): pl.pallas_call(functools.partial(attend_kernel, heads, own, len(mixing)),...  16.6 us
    pallas_call x1, Pallas kernels, local(): pl.pallas_call(functools.partial(project_kernel, heads, n_var, n_head, le...  16.3 us
    ppermute x9, starting transfers between devices, shifts(): lax.ppermute(array, axis, [(k, (k + s) % size) for k in range(size)])  14.6 us
    ppermute x2, waiting for transfers between devices, gather_rows(): moved = lax.ppermute(taps, 'head', [(k, k ^ bit) for k in range(4)])  7.83 us
    pallas_call x1, Pallas kernels, local(): pl.pallas_call(functools.partial(pair_kernel, variants), out_shape=jax.Sh...  6.76 us
    ppermute x9, waiting for transfers between devices, shifts(): lax.ppermute(array, axis, [(k, (k + s) % size) for k in range(size)])  6.04 us
    ppermute x3, starting transfers between devices, gather_rows(): lax.ppermute(array, 'head', [(k, (k + s) % 4) for k in range(4)])  5.84 us
  transfers between devices with their start and end apart: 27, of which 13 were waited for; matrix products, arithmetic and copies ran while one was open for 3% of the time, Pallas kernels for 18%

profile of v3, /device:TPU:0, one launch (start us, length us, event | category | flops | bytes accessed | tf_op | source)
XLA Modules:
  0.0 114.5 jit_solution(11246899898088265069)
XLA Ops:
  0.0 1.0 copy-done
  1.0 5.1 %collective-permute-start.1 = (bf16[256,384]{1,0:T(8,128)(2,1)S(1)}, bf16[256,384]{1,0:T(8,128)(2,1)S(1)}, u32[]{:S(2)}, u32[]{:S(2)}) collective-permute-start(bf16[256,384]{1,0:T(8,128)(2,1)S(1)} %constant_dynamic-slice_fusion), channel_id=1, source_target_pairs={{0,6},{2,0},{4,2},{6,4},{1,7},{3,1},{5,3},{7,5},{8,14},{10,8},{12,... | collective-permute-start | bytes 589832 | tf_op jit(solution)/shard_map/ppermute | solution.py:323
  6.2 5.2 %collective-permute-done.1 = bf16[256,384]{1,0:T(8,128)(2,1)S(1)} collective-permute-done((bf16[256,384]{1,0:T(8,128)(2,1)S(1)}, bf16[256,384]{1,0:T(8,128)(2,1)S(1)}, u32[]{:S(2)}, u32[]{:S(2)}) %collective-permute-start.1) | collective-permute-done | bytes 196640 | tf_op jit(solution)/shard_map/ppermute | solution.py:323
  11.4 4.0 %collective-permute-done = bf16[256,384]{1,0:T(8,128)(2,1)S(1)} collective-permute-done((bf16[256,384]{1,0:T(8,128)(2,1)S(1)}, bf16[256,384]{1,0:T(8,128)(2,1)S(1)}, u32[]{:S(2)}, u32[]{:S(2)}) %collective-permute-start) | collective-permute-done | bytes 196640 | tf_op jit(solution)/shard_map/ppermute | solution.py:323
  15.4 0.1 pad_maximum_fusion.1
  15.5 1.6 %collective-permute-start.5 = (bf16[3,256,384]{2,1,0:T(8,128)(2,1)S(1)}, bf16[3,256,384]{2,1,0:T(8,128)(2,1)}, u32[]{:S(2)}, u32[]{:S(2)}) collective-permute-start(bf16[3,256,384]{2,1,0:T(8,128)(2,1)S(1)} %pad_maximum_fusion.1), channel_id=1, source_target_pairs={{0,8},{8,0},{16,24},{24,16},{1,9},{9,1},{17,25},{25,17},{2,10},{10... | collective-permute-start | bytes 1769480 | tf_op jit(solution)/shard_map/ppermute | solution.py:324
  17.0 1.5 %collective-permute-start.2 = (bf16[3,256,384]{2,1,0:T(8,128)(2,1)S(1)}, bf16[3,256,384]{2,1,0:T(8,128)(2,1)S(1)}, u32[]{:S(2)}, u32[]{:S(2)}) collective-permute-start(bf16[3,256,384]{2,1,0:T(8,128)(2,1)S(1)} %pad_maximum_fusion.1), channel_id=1, source_target_pairs={{0,16},{8,24},{16,0},{24,8},{1,17},{9,25},{17,1},{25,9},{2,18},{10... | collective-permute-start | bytes 1769480 | tf_op jit(solution)/shard_map/ppermute | solution.py:324
  18.6 0.7 collective-permute-start.3
  19.3 9.8 %collective-permute-done.3 = bf16[256,384]{1,0:T(8,128)(2,1)} collective-permute-done((bf16[256,384]{1,0:T(8,128)(2,1)S(1)}, bf16[256,384]{1,0:T(8,128)(2,1)}, u32[]{:S(2)}, u32[]{:S(2)}) %collective-permute-start.3) | collective-permute-done | bytes 196640 | tf_op jit(solution)/shard_map/ppermute | solution.py:323
  29.1 0.5 collective-permute-start.6
  29.6 0.5 collective-permute-start.4
  30.1 1.1 pad_maximum_fusion.refs_1_
  31.2 0.1 collective-permute-start.8
  31.3 1.3 %constant_dynamic-update-slice_fusion.3 = bf16[4,256,384]{2,1,0:T(8,128)(2,1)S(1)} fusion(bf16[3,256,384]{2,1,0:T(8,128)(2,1)} %collective-permute-done.5), kind=kLoop, calls=%fused_computation.15 | loop fusion | bytes 1179648
  32.6 2.4 %collective-permute-done.6 = bf16[1,256,384]{2,1,0:T(8,128)(2,1)S(1)} collective-permute-done((bf16[1,256,384]{2,1,0:T(8,128)(2,1)}, bf16[1,256,384]{2,1,0:T(8,128)(2,1)S(1)}, u32[]{:S(2)}, u32[]{:S(2)}) %collective-permute-start.6) | collective-permute-done | bytes 196640 | tf_op jit(solution)/shard_map/ppermute | solution.py:324
  35.1 0.1 constant_dynamic-update-slice_fusion.1
  35.2 0.3 collective-permute-done.4
  35.6 0.1 broadcast_select_fusion
  35.7 1.6 %collective-permute-start.7 = (bf16[4,256,384]{2,1,0:T(8,128)(2,1)S(1)}, bf16[4,256,384]{2,1,0:T(8,128)(2,1)}, u32[]{:S(2)}, u32[]{:S(2)}) collective-permute-start(bf16[4,256,384]{2,1,0:T(8,128)(2,1)S(1)} %broadcast_select_fusion), channel_id=1, source_target_pairs={{0,8},{1,17},{8,0},{9,25},{16,24},{17,1},{24,16},{25,9},{2,10},{3,... | collective-permute-start | bytes 2359304 | tf_op jit(solution)/shard_map/ppermute | solution.py:334
  37.2 0.5 collective-permute-start.9
  37.7 0.4 collective-permute-start.11
  38.2 3.3 %collective-permute-done.11 = f32[4,384]{1,0:T(4,128)S(1)} collective-permute-done((f32[4,384]{1,0:T(4,128)S(1)}, f32[4,384]{1,0:T(4,128)S(1)}, u32[]{:S(2)}, u32[]{:S(2)}) %collective-permute-start.11) | collective-permute-done | bytes 6176 | tf_op jit(solution)/shard_map/ppermute | solution.py:337
  41.5 0.1 collective-permute-start.12
  41.5 4.6 %collective-permute-done.12 = f32[8,384]{1,0:T(8,128)S(1)} collective-permute-done((f32[8,384]{1,0:T(8,128)S(1)}, f32[8,384]{1,0:T(8,128)S(1)}, u32[]{:S(2)}, u32[]{:S(2)}) %collective-permute-start.12) | collective-permute-done | bytes 12320 | tf_op jit(solution)/shard_map/ppermute | solution.py:337
  46.1 1.7 %collective-permute-done.7.refs_4_ = bf16[4,256,384]{2,1,0:T(8,128)(2,1)} collective-permute-done((bf16[4,256,384]{2,1,0:T(8,128)(2,1)S(1)}, bf16[4,256,384]{2,1,0:T(8,128)(2,1)}, u32[]{:S(2)}, u32[]{:S(2)}) %collective-permute-start.7) | collective-permute-done | bytes 786464 | tf_op jit(solution)/shard_map/ppermute | solution.py:334
  47.8 0.1 collective-permute-start.13
  47.9 1.2 %collective-permute-start.16 = (bf16[384,256]{1,0:T(8,128)(2,1)S(1)}, bf16[384,256]{1,0:T(8,128)(2,1)S(1)}, u32[]{:S(2)}, u32[]{:S(2)}) collective-permute-start(bf16[384,256]{1,0:T(8,128)(2,1)S(1)} %copy-done.3), channel_id=1, source_target_pairs={{0,6},{2,0},{4,2},{6,4},{1,7},{3,1},{5,3},{7,5},{8,14},{10,8},{12,... | collective-permute-start | bytes 589832 | tf_op jit(solution)/shard_map/ppermute | solution.py:311
  49.2 1.6 %collective-permute-start.15 = (bf16[384,256]{1,0:T(8,128)(2,1)S(1)}, bf16[384,256]{1,0:T(8,128)(2,1)S(1)}, u32[]{:S(2)}, u32[]{:S(2)}) collective-permute-start(bf16[384,256]{1,0:T(8,128)(2,1)S(1)} %copy-done.3), channel_id=1, source_target_pairs={{0,4},{2,6},{4,0},{6,2},{1,5},{3,7},{5,1},{7,3},{8,12},{10,14},{12... | collective-permute-start | bytes 589832 | tf_op jit(solution)/shard_map/ppermute | solution.py:311
  50.9 0.2 dynamic-slice_reduce_fusion
  51.1 0.1 concatenate.34.order
  51.2 0.1 concatenate.27.scalars
  51.3 16.3 %project.1 = (bf16[2048,1024]{1,0:T(8,128)(2,1)S(1)}, f32[512,384]{1,0:T(8,128)S(1)}) custom-call(s32[8]{0:T(128)S(1)} %concatenate.27.scalars, bf16[1536,896]{1,0:T(8,128)(2,1)} %w_proj.1, f32[4,4,384]{2,1,0:T(4,128)S(1)} %reshape.3.refs_0_, bf16[4,256,384]{2,1,0:T(8,128)(2,1)} %copy-done.6, bf16[4,256,384]{2,1,0:T(8,128)(2,1)} %copy-done.5, ...), custom_call_target="tpu_custom_call" | custom-call | flops 7952400384 | bytes 12582912 | tf_op jit(solution)/shard_map/project/pallas_call | solution.py:376
  67.7 1.0 collective-permute-done.15.refs_3_
  68.6 12.2 %attend.2 = (bf16[3,128,256]{2,1,0:T(8,128)(2,1)S(1)}, bf16[2,256,256]{2,1,0:T(8,128)(2,1)S(1)}) custom-call(s32[7]{0:T(128)S(1)} %concatenate.34.order, bf16[2048,1024]{1,0:T(8,128)(2,1)S(1)} %get-tuple-element.19.kvq, f32[512,384]{1,0:T(8,128)S(1)} %get-tuple-element.20.pooled, bf16[384,1536]{1,0:T(8,128)(2,1)S(1)} %copy-done.2, ...), custom_call_target="tpu_custom_call" | custom-call | flops 6442450944 | bytes 4194304 | tf_op jit(solution)/shard_map/attend/pallas_call | solution.py:422
  80.9 0.9 collective-permute-start.17
  81.8 3.0 %collective-permute-start.19 = (bf16[128,256]{1,0:T(8,128)(2,1)S(1)}, bf16[128,256]{1,0:T(8,128)(2,1)S(1)}, u32[]{:S(2)}, u32[]{:S(2)}) collective-permute-start(bf16[128,256]{1,0:T(8,128)(2,1)S(1)} %get-tuple-element.24), channel_id=1, source_target_pairs={{0,6},{2,0},{4,2},{6,4},{1,7},{3,1},{5,3},{7,5},{8,14},{10,8},{12,... | collective-permute-start | bytes 196616 | tf_op jit(solution)/shard_map/ppermute | solution.py:451
  84.7 4.4 %attend.3 = f32[1,128,256]{2,1,0:T(8,128)S(1)} custom-call(s32[1]{0:T(128)} %bitcast.9.order, bf16[2048,1024]{1,0:T(8,128)(2,1)S(1)} %get-tuple-element.19.kvq, f32[512,384]{1,0:T(8,128)S(1)} %get-tuple-element.20.pooled, bf16[2,256,256]{2,1,0:T(8,128)(2,1)S(1)} %get-tuple-element.21.refs_0_, bf16[384,256]{1,0:T(8,128)(2,1)S(1)} %copy-done.3), custom_call_target="tpu_custom_call" | custom-call | flops 2147483648 | bytes 4194304 | tf_op jit(solution)/shard_map/attend/pallas_call | solution.py:422
  89.2 0.8 collective-permute-done.18
  90.1 0.7 collective-permute-start.20
  90.8 6.0 %collective-permute-start.26 = (bf16[128,128]{1,0:T(8,128)(2,1)S(1)}, bf16[128,128]{1,0:T(8,128)(2,1)S(1)}, u32[]{:S(2)}, u32[]{:S(2)}) collective-permute-start(bf16[128,128]{1,0:T(8,128)(2,1)S(1)} %get-tuple-element.26.refs_4_), channel_id=1, source_target_pairs={{0,24},{8,0},{16,8},{24,16},{1,25},{9,1},{17,9},{25,17},{2,26},{10... | collective-permute-start | bytes 98312 | tf_op jit(solution)/shard_map/ppermute | solution.py:311
  96.8 0.8 collective-permute-start.24
  97.6 4.2 %collective-permute-start.23 = (bf16[128,128]{1,0:T(8,128)(2,1)S(1)}, bf16[128,128]{1,0:T(8,128)(2,1)S(1)}, u32[]{:S(2)}, u32[]{:S(2)}) collective-permute-start(bf16[128,128]{1,0:T(8,128)(2,1)S(1)} %collective-permute-done.20.refs_0_), channel_id=1, source_target_pairs={{0,6},{2,0},{4,2},{6,4},{1,7},{3,1},{5,3},{7,5},{8,14},{10,8},{12,... | collective-permute-start | bytes 98312 | tf_op jit(solution)/shard_map/ppermute | solution.py:311
  101.9 0.6 collective-permute-start.21
  102.4 0.1 stack.71.order
  102.5 0.9 collective-permute-done.23.refs_3_
  103.5 3.2 %collective-permute-done.22.refs_2_ = bf16[128,128]{1,0:T(8,128)(2,1)S(1)} collective-permute-done((bf16[128,128]{1,0:T(8,128)(2,1)S(1)}, bf16[128,128]{1,0:T(8,128)(2,1)S(1)}, u32[]{:S(2)}, u32[]{:S(2)}) %collective-permute-start.22) | collective-permute-done | bytes 32800 | tf_op jit(solution)/shard_map/ppermute | solution.py:311
  106.7 0.9 collective-permute-done.21.refs_1_
  107.6 6.8 %pair_map.1 = bf16[4,128,128,128]{3,2,1,0:T(8,128)(2,1)} custom-call(s32[9]{0:T(128)S(1)} %stack.71.order, f32[16,128]{1,0:T(8,128)S(1)} %copy-done.1, bf16[128,128]{1,0:T(8,128)(2,1)S(1)} %collective-permute-done.20.refs_0_, bf16[128,128]{1,0:T(8,128)(2,1)S(1)} %collective-permute-done.21.refs_1_, bf16[128,128]{1,0:T(8,128)(2,1)S(1)} %collective-permute-done.22.refs_2_, ...), custom_call_target="tpu_custom_call" | custom-call | tf_op jit(solution)/shard_map/pair_map/pallas_call | solution.py:471
  (58 shorter events, 0.4 us)
Async XLA Ops:
  0.0 1.0 copy-start
  1.0 10.4 %collective-permute-start.1 = (bf16[256,384]{1,0:T(8,128)(2,1)S(1)}, bf16[256,384]{1,0:T(8,128)(2,1)S(1)}, u32[]{:S(2)}, u32[]{:S(2)}) collective-permute-start(bf16[256,384]{1,0:T(8,128)(2,1)S(1)} %constant_dynamic-slice_fusion), channel_id=1, source_target_pairs={{0,6},{2,0},{4,2},{6,4},{1,7},{3,1},{5,3},{7,5},{8,14},{10,8},{12,... | collective-permute-start | bytes 589832 | tf_op jit(solution)/shard_map/ppermute | solution.py:323
  6.1 9.3 %collective-permute-start = (bf16[256,384]{1,0:T(8,128)(2,1)S(1)}, bf16[256,384]{1,0:T(8,128)(2,1)S(1)}, u32[]{:S(2)}, u32[]{:S(2)}) collective-permute-start(bf16[256,384]{1,0:T(8,128)(2,1)S(1)} %constant_dynamic-slice_fusion), channel_id=1, source_target_pairs={{0,2},{2,4},{4,6},{6,0},{1,3},{3,5},{5,7},{7,1},{8,10},{10,12},{12... | collective-permute-start | bytes 589832 | tf_op jit(solution)/shard_map/ppermute | solution.py:323
  6.2 31.6 %copy-start.8 = (f32[384]{0:T(512)S(1)}, f32[384]{0:T(512)}, u32[]{:S(2)}) copy-start(f32[384]{0:T(512)} %param.11) | copy-start | bytes 4612
  6.2 31.6 %copy-start.7 = (f32[3,384]{1,0:T(4,128)S(1)}, f32[3,384]{1,0:T(4,128)}, u32[]{:S(2)}) copy-start(f32[3,384]{1,0:T(4,128)} %param.10) | copy-start | bytes 13828
  6.2 41.7 %copy-start.3 = (bf16[384,256]{1,0:T(8,128)(2,1)S(1)}, bf16[384,256]{1,0:T(8,128)(2,1)}, u32[]{:S(2)}) copy-start(bf16[384,256]{1,0:T(8,128)(2,1)} %refs_1_.3) | copy-start | bytes 589828
  15.4 35.5 %copy-start.9 = (s32[4,2]{0,1:T(2,128)S(1)}, s32[4,2]{0,1:T(2,128)}, u32[]{:S(2)}) copy-start(s32[4,2]{0,1:T(2,128)} %param.9) | copy-start | bytes 100
  15.5 15.8 %collective-permute-start.5 = (bf16[3,256,384]{2,1,0:T(8,128)(2,1)S(1)}, bf16[3,256,384]{2,1,0:T(8,128)(2,1)}, u32[]{:S(2)}, u32[]{:S(2)}) collective-permute-start(bf16[3,256,384]{2,1,0:T(8,128)(2,1)S(1)} %pad_maximum_fusion.1), channel_id=1, source_target_pairs={{0,8},{8,0},{16,24},{24,16},{1,9},{9,1},{17,25},{25,17},{2,10},{10... | collective-permute-start | bytes 1769480 | tf_op jit(solution)/shard_map/ppermute | solution.py:324
  17.0 18.1 %collective-permute-start.2 = (bf16[3,256,384]{2,1,0:T(8,128)(2,1)S(1)}, bf16[3,256,384]{2,1,0:T(8,128)(2,1)S(1)}, u32[]{:S(2)}, u32[]{:S(2)}) collective-permute-start(bf16[3,256,384]{2,1,0:T(8,128)(2,1)S(1)} %pad_maximum_fusion.1), channel_id=1, source_target_pairs={{0,16},{8,24},{16,0},{24,8},{1,17},{9,25},{17,1},{25,9},{2,18},{10... | collective-permute-start | bytes 1769480 | tf_op jit(solution)/shard_map/ppermute | solution.py:324
  18.6 10.5 %collective-permute-start.3 = (bf16[256,384]{1,0:T(8,128)(2,1)S(1)}, bf16[256,384]{1,0:T(8,128)(2,1)}, u32[]{:S(2)}, u32[]{:S(2)}) collective-permute-start(bf16[256,384]{1,0:T(8,128)(2,1)S(1)} %constant_dynamic-slice_fusion), channel_id=1, source_target_pairs={{0,4},{2,6},{4,0},{6,2},{1,5},{3,7},{5,1},{7,3},{8,12},{10,14},{12... | collective-permute-start | bytes 589832 | tf_op jit(solution)/shard_map/ppermute | solution.py:323
  29.1 6.0 %collective-permute-start.6 = (bf16[1,256,384]{2,1,0:T(8,128)(2,1)}, bf16[1,256,384]{2,1,0:T(8,128)(2,1)S(1)}, u32[]{:S(2)}, u32[]{:S(2)}) collective-permute-start(bf16[1,256,384]{2,1,0:T(8,128)(2,1)} %bitcast.18), channel_id=1, source_target_pairs={{0,8},{8,0},{16,24},{24,16},{1,9},{9,1},{17,25},{25,17},{2,10},{10... | collective-permute-start | bytes 589832 | tf_op jit(solution)/shard_map/ppermute | solution.py:324
  29.6 5.9 %collective-permute-start.4 = (bf16[1,256,384]{2,1,0:T(8,128)(2,1)}, bf16[1,256,384]{2,1,0:T(8,128)(2,1)S(1)}, u32[]{:S(2)}, u32[]{:S(2)}) collective-permute-start(bf16[1,256,384]{2,1,0:T(8,128)(2,1)} %bitcast.18), channel_id=1, source_target_pairs={{0,16},{8,24},{16,0},{24,8},{1,17},{9,25},{17,1},{25,9},{2,18},{10... | collective-permute-start | bytes 589832 | tf_op jit(solution)/shard_map/ppermute | solution.py:324
  31.2 17.9 %copy-start.6 = (bf16[4,256,384]{2,1,0:T(8,128)(2,1)}, bf16[4,256,384]{2,1,0:T(8,128)(2,1)S(1)}, u32[]{:S(2)}) copy-start(bf16[4,256,384]{2,1,0:T(8,128)(2,1)S(1)} %pad_maximum_fusion.refs_1_) | copy-start | bytes 2359300
  31.2 14.9 %collective-permute-start.8 = (bf16[4,256,384]{2,1,0:T(8,128)(2,1)S(1)}, bf16[4,256,384]{2,1,0:T(8,128)(2,1)S(1)}, u32[]{:S(2)}, u32[]{:S(2)}) collective-permute-start(bf16[4,256,384]{2,1,0:T(8,128)(2,1)S(1)} %pad_maximum_fusion.refs_1_), channel_id=1, source_target_pairs={{0,1},{1,0},{2,3},{3,2},{4,5},{5,4},{6,7},{7,6},{8,9},{9,8},{10,11... | collective-permute-start | bytes 2359304 | tf_op jit(solution)/shard_map/ppermute | solution.py:321
  35.1 16.2 %copy-start.5 = (bf16[4,256,384]{2,1,0:T(8,128)(2,1)}, bf16[4,256,384]{2,1,0:T(8,128)(2,1)S(1)}, u32[]{:S(2)}) copy-start(bf16[4,256,384]{2,1,0:T(8,128)(2,1)S(1)} %constant_dynamic-update-slice_fusion.2.refs_2_) | copy-start | bytes 2359300
  35.5 15.8 %copy-start.4 = (bf16[4,256,384]{2,1,0:T(8,128)(2,1)}, bf16[4,256,384]{2,1,0:T(8,128)(2,1)S(1)}, u32[]{:S(2)}) copy-start(bf16[4,256,384]{2,1,0:T(8,128)(2,1)S(1)} %constant_dynamic-update-slice_fusion.refs_3_) | copy-start | bytes 2359300
  35.7 12.2 %collective-permute-start.7 = (bf16[4,256,384]{2,1,0:T(8,128)(2,1)S(1)}, bf16[4,256,384]{2,1,0:T(8,128)(2,1)}, u32[]{:S(2)}, u32[]{:S(2)}) collective-permute-start(bf16[4,256,384]{2,1,0:T(8,128)(2,1)S(1)} %broadcast_select_fusion), channel_id=1, source_target_pairs={{0,8},{1,17},{8,0},{9,25},{16,24},{17,1},{24,16},{25,9},{2,10},{3,... | collective-permute-start | bytes 2359304 | tf_op jit(solution)/shard_map/ppermute | solution.py:334
  37.2 10.6 %collective-permute-start.10 = (bf16[4,256,384]{2,1,0:T(8,128)(2,1)S(1)}, bf16[4,256,384]{2,1,0:T(8,128)(2,1)S(1)}, u32[]{:S(2)}, u32[]{:S(2)}) collective-permute-start(bf16[4,256,384]{2,1,0:T(8,128)(2,1)S(1)} %constant_dynamic-update-slice_fusion.refs_3_), channel_id=1, source_target_pairs={{0,1},{1,0},{2,3},{3,2},{4,5},{5,4},{6,7},{7,6},{8,9},{9,8},{10,11... | collective-permute-start | bytes 2359304 | tf_op jit(solution)/shard_map/ppermute | solution.py:321
  37.2 10.6 %collective-permute-start.9 = (bf16[4,256,384]{2,1,0:T(8,128)(2,1)S(1)}, bf16[4,256,384]{2,1,0:T(8,128)(2,1)S(1)}, u32[]{:S(2)}, u32[]{:S(2)}) collective-permute-start(bf16[4,256,384]{2,1,0:T(8,128)(2,1)S(1)} %constant_dynamic-update-slice_fusion.2.refs_2_), channel_id=1, source_target_pairs={{0,1},{1,0},{2,3},{3,2},{4,5},{5,4},{6,7},{7,6},{8,9},{9,8},{10,11... | collective-permute-start | bytes 2359304 | tf_op jit(solution)/shard_map/ppermute | solution.py:321
  37.7 3.7 %collective-permute-start.11 = (f32[4,384]{1,0:T(4,128)S(1)}, f32[4,384]{1,0:T(4,128)S(1)}, u32[]{:S(2)}, u32[]{:S(2)}) collective-permute-start(f32[4,384]{1,0:T(4,128)S(1)} %pad_maximum_fusion.4), channel_id=1, source_target_pairs={{0,2},{2,0},{4,6},{6,4},{1,3},{3,1},{5,7},{7,5},{8,10},{10,8},{12,... | collective-permute-start | bytes 18440 | tf_op jit(solution)/shard_map/ppermute | solution.py:337
  41.5 4.7 %collective-permute-start.12 = (f32[8,384]{1,0:T(8,128)S(1)}, f32[8,384]{1,0:T(8,128)S(1)}, u32[]{:S(2)}, u32[]{:S(2)}) collective-permute-start(f32[8,384]{1,0:T(8,128)S(1)} %pad_maximum_fusion.3), channel_id=1, source_target_pairs={{0,4},{2,6},{4,0},{6,2},{1,5},{3,7},{5,1},{7,3},{8,12},{10,14},{12... | collective-permute-start | bytes 36872 | tf_op jit(solution)/shard_map/ppermute | solution.py:337
  46.1 4.6 %copy-start.10 = (bf16[4,256,384]{2,1,0:T(8,128)(2,1)}, bf16[4,256,384]{2,1,0:T(8,128)(2,1)S(1)}, u32[]{:S(2)}) copy-start(bf16[4,256,384]{2,1,0:T(8,128)(2,1)S(1)} %collective-permute-done.8.refs_5_) | copy-start | bytes 2359300
  47.8 3.0 %copy-start.11 = (bf16[4,256,384]{2,1,0:T(8,128)(2,1)}, bf16[4,256,384]{2,1,0:T(8,128)(2,1)S(1)}, u32[]{:S(2)}) copy-start(bf16[4,256,384]{2,1,0:T(8,128)(2,1)S(1)} %collective-permute-done.10.refs_7_) | copy-start | bytes 2359300
  47.8 3.0 %copy-start.12 = (bf16[4,256,384]{2,1,0:T(8,128)(2,1)}, bf16[4,256,384]{2,1,0:T(8,128)(2,1)S(1)}, u32[]{:S(2)}) copy-start(bf16[4,256,384]{2,1,0:T(8,128)(2,1)S(1)} %collective-permute-done.9.refs_6_) | copy-start | bytes 2359300
  47.8 3.5 %collective-permute-start.13 = (bf16[4,256,384]{2,1,0:T(8,128)(2,1)}, bf16[4,256,384]{2,1,0:T(8,128)(2,1)}, u32[]{:S(2)}, u32[]{:S(2)}) collective-permute-start(bf16[4,256,384]{2,1,0:T(8,128)(2,1)} %collective-permute-done.7.refs_4_), channel_id=1, source_target_pairs={{0,1},{1,0},{2,3},{3,2},{4,5},{5,4},{6,7},{7,6},{8,9},{9,8},{10,11... | collective-permute-start | bytes 2359304 | tf_op jit(solution)/shard_map/ppermute | solution.py:321
  47.9 19.7 %collective-permute-start.16 = (bf16[384,256]{1,0:T(8,128)(2,1)S(1)}, bf16[384,256]{1,0:T(8,128)(2,1)S(1)}, u32[]{:S(2)}, u32[]{:S(2)}) collective-permute-start(bf16[384,256]{1,0:T(8,128)(2,1)S(1)} %copy-done.3), channel_id=1, source_target_pairs={{0,6},{2,0},{4,2},{6,4},{1,7},{3,1},{5,3},{7,5},{8,14},{10,8},{12,... | collective-permute-start | bytes 589832 | tf_op jit(solution)/shard_map/ppermute | solution.py:311
  49.2 19.5 %collective-permute-start.15 = (bf16[384,256]{1,0:T(8,128)(2,1)S(1)}, bf16[384,256]{1,0:T(8,128)(2,1)S(1)}, u32[]{:S(2)}, u32[]{:S(2)}) collective-permute-start(bf16[384,256]{1,0:T(8,128)(2,1)S(1)} %copy-done.3), channel_id=1, source_target_pairs={{0,4},{2,6},{4,0},{6,2},{1,5},{3,7},{5,1},{7,3},{8,12},{10,14},{12... | collective-permute-start | bytes 589832 | tf_op jit(solution)/shard_map/ppermute | solution.py:311
  50.8 17.8 %collective-permute-start.14 = (bf16[384,256]{1,0:T(8,128)(2,1)S(1)}, bf16[384,256]{1,0:T(8,128)(2,1)S(1)}, u32[]{:S(2)}, u32[]{:S(2)}) collective-permute-start(bf16[384,256]{1,0:T(8,128)(2,1)S(1)} %copy-done.3), channel_id=1, source_target_pairs={{0,2},{2,4},{4,6},{6,0},{1,3},{3,5},{5,7},{7,1},{8,10},{10,12},{12... | collective-permute-start | bytes 589832 | tf_op jit(solution)/shard_map/ppermute | solution.py:311
  51.3 17.3 %copy-start.2 = (bf16[384,1536]{1,0:T(8,128)(2,1)S(1)}, bf16[384,1536]{1,0:T(8,128)(2,1)}, u32[]{:S(2)}) copy-start(bf16[384,1536]{1,0:T(8,128)(2,1)} %refs_0_.1) | copy-start | bytes 3538948
  80.9 8.3 %collective-permute-start.17 = (bf16[128,256]{1,0:T(8,128)(2,1)S(1)}, bf16[128,256]{1,0:T(8,128)(2,1)S(1)}, u32[]{:S(2)}, u32[]{:S(2)}) collective-permute-start(bf16[128,256]{1,0:T(8,128)(2,1)S(1)} %get-tuple-element.23), channel_id=1, source_target_pairs={{0,2},{2,4},{4,6},{6,0},{1,3},{3,5},{5,7},{7,1},{8,10},{10,12},{12... | collective-permute-start | bytes 196616 | tf_op jit(solution)/shard_map/ppermute | solution.py:451
  81.8 7.4 %collective-permute-start.19 = (bf16[128,256]{1,0:T(8,128)(2,1)S(1)}, bf16[128,256]{1,0:T(8,128)(2,1)S(1)}, u32[]{:S(2)}, u32[]{:S(2)}) collective-permute-start(bf16[128,256]{1,0:T(8,128)(2,1)S(1)} %get-tuple-element.24), channel_id=1, source_target_pairs={{0,6},{2,0},{4,2},{6,4},{1,7},{3,1},{5,3},{7,5},{8,14},{10,8},{12,... | collective-permute-start | bytes 196616 | tf_op jit(solution)/shard_map/ppermute | solution.py:451
  84.7 5.3 %collective-permute-start.18 = (bf16[128,256]{1,0:T(8,128)(2,1)S(1)}, bf16[128,256]{1,0:T(8,128)(2,1)S(1)}, u32[]{:S(2)}, u32[]{:S(2)}) collective-permute-start(bf16[128,256]{1,0:T(8,128)(2,1)S(1)} %get-tuple-element.25), channel_id=1, source_target_pairs={{0,4},{2,6},{4,0},{6,2},{1,5},{3,7},{5,1},{7,3},{8,12},{10,14},{12... | collective-permute-start | bytes 196616 | tf_op jit(solution)/shard_map/ppermute | solution.py:451
  84.7 22.9 %copy-start.1 = (f32[16,128]{1,0:T(8,128)S(1)}, f32[16,128]{1,0:T(8,128)}, u32[]{:S(2)}) copy-start(f32[16,128]{1,0:T(8,128)} %dist_table.1) | copy-start | bytes 24580
  90.1 7.6 %collective-permute-start.20 = (bf16[128,128]{1,0:T(8,128)(2,1)S(1)}, bf16[128,128]{1,0:T(8,128)(2,1)S(1)}, u32[]{:S(2)}, u32[]{:S(2)}) collective-permute-start(bf16[128,128]{1,0:T(8,128)(2,1)S(1)} %get-tuple-element.27), channel_id=1, source_target_pairs={{0,0},{2,8},{4,16},{6,24},{8,2},{10,10},{12,18},{14,26},{16,4},{18... | collective-permute-start | bytes 98312 | tf_op jit(solution)/shard_map/ppermute | solution.py:452
  90.8 11.1 %collective-permute-start.26 = (bf16[128,128]{1,0:T(8,128)(2,1)S(1)}, bf16[128,128]{1,0:T(8,128)(2,1)S(1)}, u32[]{:S(2)}, u32[]{:S(2)}) collective-permute-start(bf16[128,128]{1,0:T(8,128)(2,1)S(1)} %get-tuple-element.26.refs_4_), channel_id=1, source_target_pairs={{0,24},{8,0},{16,8},{24,16},{1,25},{9,1},{17,9},{25,17},{2,26},{10... | collective-permute-start | bytes 98312 | tf_op jit(solution)/shard_map/ppermute | solution.py:311
  96.8 5.7 %collective-permute-start.25 = (bf16[128,128]{1,0:T(8,128)(2,1)S(1)}, bf16[128,128]{1,0:T(8,128)(2,1)S(1)}, u32[]{:S(2)}, u32[]{:S(2)}) collective-permute-start(bf16[128,128]{1,0:T(8,128)(2,1)S(1)} %get-tuple-element.26.refs_4_), channel_id=1, source_target_pairs={{0,16},{8,24},{16,0},{24,8},{1,17},{9,25},{17,1},{25,9},{2,18},{10... | collective-permute-start | bytes 98312 | tf_op jit(solution)/shard_map/ppermute | solution.py:311
  96.8 5.7 %collective-permute-start.24 = (bf16[128,128]{1,0:T(8,128)(2,1)S(1)}, bf16[128,128]{1,0:T(8,128)(2,1)S(1)}, u32[]{:S(2)}, u32[]{:S(2)}) collective-permute-start(bf16[128,128]{1,0:T(8,128)(2,1)S(1)} %get-tuple-element.26.refs_4_), channel_id=1, source_target_pairs={{0,8},{8,16},{16,24},{24,0},{1,9},{9,17},{17,25},{25,1},{2,10},{10... | collective-permute-start | bytes 98312 | tf_op jit(solution)/shard_map/ppermute | solution.py:311
  97.6 5.8 %collective-permute-start.23 = (bf16[128,128]{1,0:T(8,128)(2,1)S(1)}, bf16[128,128]{1,0:T(8,128)(2,1)S(1)}, u32[]{:S(2)}, u32[]{:S(2)}) collective-permute-start(bf16[128,128]{1,0:T(8,128)(2,1)S(1)} %collective-permute-done.20.refs_0_), channel_id=1, source_target_pairs={{0,6},{2,0},{4,2},{6,4},{1,7},{3,1},{5,3},{7,5},{8,14},{10,8},{12,... | collective-permute-start | bytes 98312 | tf_op jit(solution)/shard_map/ppermute | solution.py:311
  101.9 4.8 %collective-permute-start.22 = (bf16[128,128]{1,0:T(8,128)(2,1)S(1)}, bf16[128,128]{1,0:T(8,128)(2,1)S(1)}, u32[]{:S(2)}, u32[]{:S(2)}) collective-permute-start(bf16[128,128]{1,0:T(8,128)(2,1)S(1)} %collective-permute-done.20.refs_0_), channel_id=1, source_target_pairs={{0,4},{2,6},{4,0},{6,2},{1,5},{3,7},{5,1},{7,3},{8,12},{10,14},{12... | collective-permute-start | bytes 98312 | tf_op jit(solution)/shard_map/ppermute | solution.py:311
  101.9 5.7 %collective-permute-start.21 = (bf16[128,128]{1,0:T(8,128)(2,1)S(1)}, bf16[128,128]{1,0:T(8,128)(2,1)S(1)}, u32[]{:S(2)}, u32[]{:S(2)}) collective-permute-start(bf16[128,128]{1,0:T(8,128)(2,1)S(1)} %collective-permute-done.20.refs_0_), channel_id=1, source_target_pairs={{0,2},{2,4},{4,6},{6,0},{1,3},{3,5},{5,7},{7,1},{8,10},{10,12},{12... | collective-permute-start | bytes 98312 | tf_op jit(solution)/shard_map/ppermute | solution.py:311

commit v4 on v3

--- a/solution.py
+++ b/solution.py
@@ -249,15 +249,15 @@
             out[n] = pair.astype(out.dtype)
 
 
-def pair_kernel(variants, order, dist_table, *refs):
-    row_feats = refs[:variants]
-    col_feats = refs[variants : 2 * variants]
-    out, rows, cols, table, span, blocks, sems = refs[2 * variants :]
+def pair_kernel(
+    variants, order, dist_table, row_feats, col_feats,
+    out, rows, cols, table, span, blocks, sems,
+):
     side = cols.shape[1]
     count = rows.shape[1]
     for s in range(variants):
-        rows[order[s]] = row_feats[s][...].astype(jnp.float32)
-        cols[order[variants + s]] = col_feats[s][...]
+        rows[order[s]] = row_feats[s].astype(jnp.float32)
+        cols[order[variants + s]] = col_feats[s]
 
     offset = order[2 * variants] + count - 1
     bucket = lax.broadcasted_iota(jnp.int32, (count + side, NB), 1)
@@ -311,6 +311,14 @@
         lax.ppermute(array, axis, [(k, (k + s) % size) for k in range(size)])
         for s in range(1, size)
     ]
+
+
+def doubled(array, axis):
+    size, found, bit = lax.axis_size(axis), array[None], 1
+    while bit < size:
+        moved = lax.ppermute(found, axis, [(k, k ^ bit) for k in range(size)])
+        found, bit = jnp.concatenate([found, moved]), 2 * bit
+    return found
 
 
 def head_order(n_head):
@@ -454,9 +462,9 @@
             ("ctx", "head"),
             [(i * n_head + h, h * n_head + i) for i in range(n_ctx) for h in range(n_head)],
         )
-        row_feats = shifts(turned, "head")
-        col_feats = shifts(summed[:, C:].astype(jnp.bfloat16), "ctx")
-        order = [(at + n_ctx - s) % n_ctx for at in (ours, mine) for s in range(variants)]
+        row_feats = doubled(turned, "head")
+        col_feats = doubled(summed[:, C:].astype(jnp.bfloat16), "ctx")
+        order = [at ^ s for at in (ours, mine) for s in range(variants)]
     else:
         blocks_here = n_ctx // splits
         here = (mine % splits) * blocks_here + jnp.arange(blocks_here)
@@ -465,13 +473,12 @@
         feats = feats.reshape(variants, n_ctx, pair_rows, 2 * C)
         row_feats = lax.dynamic_index_in_dim(feats, mine, 1, keepdims=False)[:, :, :C]
         col_feats = lax.dynamic_index_in_dim(feats, ours, 1, keepdims=False)[:, :, C:]
-        row_feats, col_feats = list(row_feats), list(col_feats)
         order = list(range(variants)) * 2
 
     return pl.pallas_call(
         functools.partial(pair_kernel, variants),
         out_shape=jax.ShapeDtypeStruct((variants, pair_rows, pair_rows, C), jnp.bfloat16),
-        in_specs=[whole(pltpu.SMEM)] + [whole()] * (1 + 2 * variants),
+        in_specs=[whole(pltpu.SMEM)] + [whole()] * 3,
         out_specs=whole(pl.ANY),
         scratch_shapes=[
             pltpu.VMEM((variants, pair_rows, C), jnp.float32),
@@ -486,8 +493,8 @@
     )(
         jnp.stack([*order, (mine - ours) * pair_rows]).astype(jnp.int32),
         dist_table,
-        *row_feats,
-        *col_feats,
+        row_feats,
+        col_feats,
     )
 
 

time: 115 us -> 114 us (level)
  waiting for transfers between devices: 38.1 us -> 35.4 us
  starting transfers between devices: 31.8 us -> 33.7 us
    ppermute x0 -> x4, starting transfers between devices: none -> 13.6 us  [doubled(): moved = lax.ppermute(found, axis, [(k, k ^ bit) for k in range(size)])]
    ppermute x9 -> x3, starting transfers between devices: 14.6 us -> 2.9 us  [shifts(): lax.ppermute(array, axis, [(k, (k + s) % size) for k in range(size)])]
    ppermute x9 -> x3, waiting for transfers between devices: 6.04 us -> 1.05 us  [shifts(): lax.ppermute(array, axis, [(k, (k + s) % size) for k in range(size)])]
    ppermute x0 -> x4, waiting for transfers between devices: none -> 2.23 us  [doubled(): moved = lax.ppermute(found, axis, [(k, k ^ bit) for k in range(size)])]
  transfers between devices with their start and end apart: 27 -> 25, of which waited for: 13 -> 11; matrix products, arithmetic and copies ran while one was open for 3% -> 3% of each run, Pallas kernels for 18% -> 18%
where the time goes in v4:
time: 114 us
  Pallas kernels  39.6 us (35%)
  waiting for transfers between devices  35.4 us (31%)
  starting transfers between devices  33.7 us (30%)
  local copies, waits for them, and re-layouts  3.02 us (3%)
  other arithmetic  1.38 us (1%)
    ppermute x3, waiting for transfers between devices, gather_rows(): lax.ppermute(array, 'head', [(k, (k + s) % 4) for k in range(4)])  19 us
    pallas_call x2, Pallas kernels, attend(): pl.pallas_call(functools.partial(attend_kernel, heads, own, len(mixing)),...  16.6 us
    pallas_call x1, Pallas kernels, local(): pl.pallas_call(functools.partial(project_kernel, heads, n_var, n_head, le...  16.2 us
    ppermute x4, starting transfers between devices, doubled(): moved = lax.ppermute(found, axis, [(k, k ^ bit) for k in range(size)])  13.6 us
    ppermute x2, waiting for transfers between devices, gather_rows(): moved = lax.ppermute(taps, 'head', [(k, k ^ bit) for k in range(4)])  7.83 us
    pallas_call x1, Pallas kernels, local(): pl.pallas_call(functools.partial(pair_kernel, variants), out_shape=jax.Sh...  6.76 us
    ppermute x3, starting transfers between devices, gather_rows(): lax.ppermute(array, 'head', [(k, (k + s) % 4) for k in range(4)])  5.84 us
    ppermute x4, starting transfers between devices, gather_rows(): lax.ppermute(array, 'ctx', [(k, k ^ bit) for k in range(4)])  4.12 us
  transfers between devices with their start and end apart: 25, of which 11 were waited for; matrix products, arithmetic and copies ran while one was open for 3% of the time, Pallas kernels for 18%

profile of v4, /device:TPU:0, one launch (start us, length us, event | category | flops | bytes accessed | tf_op | source)
XLA Modules:
  0.0 113.7 jit_solution(16267673387061503101)
XLA Ops:
  0.0 1.0 copy-done
  1.0 5.1 %collective-permute-start.1 = (bf16[256,384]{1,0:T(8,128)(2,1)S(1)}, bf16[256,384]{1,0:T(8,128)(2,1)S(1)}, u32[]{:S(2)}, u32[]{:S(2)}) collective-permute-start(bf16[256,384]{1,0:T(8,128)(2,1)S(1)} %constant_dynamic-slice_fusion), channel_id=1, source_target_pairs={{0,6},{2,0},{4,2},{6,4},{1,7},{3,1},{5,3},{7,5},{8,14},{10,8},{12,... | collective-permute-start | bytes 589832 | tf_op jit(solution)/shard_map/ppermute | solution.py:331
  6.2 0.0 copy-start.7
  6.2 5.2 %collective-permute-done.1 = bf16[256,384]{1,0:T(8,128)(2,1)S(1)} collective-permute-done((bf16[256,384]{1,0:T(8,128)(2,1)S(1)}, bf16[256,384]{1,0:T(8,128)(2,1)S(1)}, u32[]{:S(2)}, u32[]{:S(2)}) %collective-permute-start.1) | collective-permute-done | bytes 196640 | tf_op jit(solution)/shard_map/ppermute | solution.py:331
  11.4 4.0 %collective-permute-done = bf16[256,384]{1,0:T(8,128)(2,1)S(1)} collective-permute-done((bf16[256,384]{1,0:T(8,128)(2,1)S(1)}, bf16[256,384]{1,0:T(8,128)(2,1)S(1)}, u32[]{:S(2)}, u32[]{:S(2)}) %collective-permute-start) | collective-permute-done | bytes 196640 | tf_op jit(solution)/shard_map/ppermute | solution.py:331
  15.4 0.1 pad_maximum_fusion.1
  15.5 1.6 %collective-permute-start.5 = (bf16[3,256,384]{2,1,0:T(8,128)(2,1)S(1)}, bf16[3,256,384]{2,1,0:T(8,128)(2,1)}, u32[]{:S(2)}, u32[]{:S(2)}) collective-permute-start(bf16[3,256,384]{2,1,0:T(8,128)(2,1)S(1)} %pad_maximum_fusion.1), channel_id=1, source_target_pairs={{0,8},{8,0},{16,24},{24,16},{1,9},{9,1},{17,25},{25,17},{2,10},{10... | collective-permute-start | bytes 1769480 | tf_op jit(solution)/shard_map/ppermute | solution.py:332
  17.0 1.5 %collective-permute-start.2 = (bf16[3,256,384]{2,1,0:T(8,128)(2,1)S(1)}, bf16[3,256,384]{2,1,0:T(8,128)(2,1)S(1)}, u32[]{:S(2)}, u32[]{:S(2)}) collective-permute-start(bf16[3,256,384]{2,1,0:T(8,128)(2,1)S(1)} %pad_maximum_fusion.1), channel_id=1, source_target_pairs={{0,16},{8,24},{16,0},{24,8},{1,17},{9,25},{17,1},{25,9},{2,18},{10... | collective-permute-start | bytes 1769480 | tf_op jit(solution)/shard_map/ppermute | solution.py:332
  18.6 0.7 collective-permute-start.3
  19.3 9.8 %collective-permute-done.3 = bf16[256,384]{1,0:T(8,128)(2,1)} collective-permute-done((bf16[256,384]{1,0:T(8,128)(2,1)S(1)}, bf16[256,384]{1,0:T(8,128)(2,1)}, u32[]{:S(2)}, u32[]{:S(2)}) %collective-permute-start.3) | collective-permute-done | bytes 196640 | tf_op jit(solution)/shard_map/ppermute | solution.py:331
  29.1 0.5 collective-permute-start.6
  29.6 0.5 collective-permute-start.4
  30.1 1.1 pad_maximum_fusion.refs_1_
  31.2 0.1 collective-permute-start.8
  31.3 1.3 %constant_dynamic-update-slice_fusion.3 = bf16[4,256,384]{2,1,0:T(8,128)(2,1)S(1)} fusion(bf16[3,256,384]{2,1,0:T(8,128)(2,1)} %collective-permute-done.5), kind=kLoop, calls=%fused_computation.20 | loop fusion | bytes 1179648
  32.6 2.4 %collective-permute-done.6 = bf16[1,256,384]{2,1,0:T(8,128)(2,1)S(1)} collective-permute-done((bf16[1,256,384]{2,1,0:T(8,128)(2,1)}, bf16[1,256,384]{2,1,0:T(8,128)(2,1)S(1)}, u32[]{:S(2)}, u32[]{:S(2)}) %collective-permute-start.6) | collective-permute-done | bytes 196640 | tf_op jit(solution)/shard_map/ppermute | solution.py:332
  35.1 0.1 constant_dynamic-update-slice_fusion.1
  35.2 0.3 collective-permute-done.4
  35.6 0.1 broadcast_select_fusion
  35.7 1.6 %collective-permute-start.7 = (bf16[4,256,384]{2,1,0:T(8,128)(2,1)S(1)}, bf16[4,256,384]{2,1,0:T(8,128)(2,1)}, u32[]{:S(2)}, u32[]{:S(2)}) collective-permute-start(bf16[4,256,384]{2,1,0:T(8,128)(2,1)S(1)} %broadcast_select_fusion), channel_id=1, source_target_pairs={{0,8},{1,17},{8,0},{9,25},{16,24},{17,1},{24,16},{25,9},{2,10},{3,... | collective-permute-start | bytes 2359304 | tf_op jit(solution)/shard_map/ppermute | solution.py:342
  37.2 0.5 collective-permute-start.9
  37.7 0.4 collective-permute-start.11
  38.2 3.3 %collective-permute-done.11 = f32[4,384]{1,0:T(4,128)S(1)} collective-permute-done((f32[4,384]{1,0:T(4,128)S(1)}, f32[4,384]{1,0:T(4,128)S(1)}, u32[]{:S(2)}, u32[]{:S(2)}) %collective-permute-start.11) | collective-permute-done | bytes 6176 | tf_op jit(solution)/shard_map/ppermute | solution.py:345
  41.5 0.1 collective-permute-start.12
  41.5 4.6 %collective-permute-done.12 = f32[8,384]{1,0:T(8,128)S(1)} collective-permute-done((f32[8,384]{1,0:T(8,128)S(1)}, f32[8,384]{1,0:T(8,128)S(1)}, u32[]{:S(2)}, u32[]{:S(2)}) %collective-permute-start.12) | collective-permute-done | bytes 12320 | tf_op jit(solution)/shard_map/ppermute | solution.py:345
  46.1 1.7 %collective-permute-done.7.refs_4_ = bf16[4,256,384]{2,1,0:T(8,128)(2,1)} collective-permute-done((bf16[4,256,384]{2,1,0:T(8,128)(2,1)S(1)}, bf16[4,256,384]{2,1,0:T(8,128)(2,1)}, u32[]{:S(2)}, u32[]{:S(2)}) %collective-permute-start.7) | collective-permute-done | bytes 786464 | tf_op jit(solution)/shard_map/ppermute | solution.py:342
  47.8 0.1 collective-permute-start.13
  47.9 1.2 %collective-permute-start.16 = (bf16[384,256]{1,0:T(8,128)(2,1)S(1)}, bf16[384,256]{1,0:T(8,128)(2,1)S(1)}, u32[]{:S(2)}, u32[]{:S(2)}) collective-permute-start(bf16[384,256]{1,0:T(8,128)(2,1)S(1)} %copy-done.3), channel_id=1, source_target_pairs={{0,6},{2,0},{4,2},{6,4},{1,7},{3,1},{5,3},{7,5},{8,14},{10,8},{12,... | collective-permute-start | bytes 589832 | tf_op jit(solution)/shard_map/ppermute | solution.py:311
  49.2 1.6 %collective-permute-start.15 = (bf16[384,256]{1,0:T(8,128)(2,1)S(1)}, bf16[384,256]{1,0:T(8,128)(2,1)S(1)}, u32[]{:S(2)}, u32[]{:S(2)}) collective-permute-start(bf16[384,256]{1,0:T(8,128)(2,1)S(1)} %copy-done.3), channel_id=1, source_target_pairs={{0,4},{2,6},{4,0},{6,2},{1,5},{3,7},{5,1},{7,3},{8,12},{10,14},{12... | collective-permute-start | bytes 589832 | tf_op jit(solution)/shard_map/ppermute | solution.py:311
  50.8 0.1 collective-permute-start.14
  50.9 0.2 dynamic-slice_reduce_fusion
  51.1 0.1 concatenate.48.order
  51.2 0.1 concatenate.41.scalars
  51.3 16.2 %project.1 = (bf16[2048,1024]{1,0:T(8,128)(2,1)S(1)}, f32[512,384]{1,0:T(8,128)S(1)}) custom-call(s32[8]{0:T(128)S(1)} %concatenate.41.scalars, bf16[1536,896]{1,0:T(8,128)(2,1)} %w_proj.1, f32[4,4,384]{2,1,0:T(4,128)S(1)} %reshape.3.refs_0_, bf16[4,256,384]{2,1,0:T(8,128)(2,1)} %copy-done.6, bf16[4,256,384]{2,1,0:T(8,128)(2,1)} %copy-done.5, ...), custom_call_target="tpu_custom_call" | custom-call | flops 7952400384 | bytes 12582912 | tf_op jit(solution)/shard_map/project/pallas_call | solution.py:384
  67.6 1.0 collective-permute-done.15.refs_3_
  68.6 12.2 %attend.2 = (bf16[3,128,256]{2,1,0:T(8,128)(2,1)S(1)}, bf16[2,256,256]{2,1,0:T(8,128)(2,1)S(1)}) custom-call(s32[7]{0:T(128)S(1)} %concatenate.48.order, bf16[2048,1024]{1,0:T(8,128)(2,1)S(1)} %get-tuple-element.19.kvq, f32[512,384]{1,0:T(8,128)S(1)} %get-tuple-element.20.pooled, bf16[384,1536]{1,0:T(8,128)(2,1)S(1)} %copy-done.2, ...), custom_call_target="tpu_custom_call" | custom-call | flops 6442450944 | bytes 4194304 | tf_op jit(solution)/shard_map/attend/pallas_call | solution.py:430
  80.9 0.8 collective-permute-start.17
  81.7 3.0 %collective-permute-start.19 = (bf16[128,256]{1,0:T(8,128)(2,1)S(1)}, bf16[128,256]{1,0:T(8,128)(2,1)S(1)}, u32[]{:S(2)}, u32[]{:S(2)}) collective-permute-start(bf16[128,256]{1,0:T(8,128)(2,1)S(1)} %get-tuple-element.24), channel_id=1, source_target_pairs={{0,6},{2,0},{4,2},{6,4},{1,7},{3,1},{5,3},{7,5},{8,14},{10,8},{12,... | collective-permute-start | bytes 196616 | tf_op jit(solution)/shard_map/ppermute | solution.py:459
  84.7 4.4 %attend.3 = f32[1,128,256]{2,1,0:T(8,128)S(1)} custom-call(s32[1]{0:T(128)} %bitcast.order, bf16[2048,1024]{1,0:T(8,128)(2,1)S(1)} %get-tuple-element.19.kvq, f32[512,384]{1,0:T(8,128)S(1)} %get-tuple-element.20.pooled, bf16[2,256,256]{2,1,0:T(8,128)(2,1)S(1)} %get-tuple-element.21.refs_0_, bf16[384,256]{1,0:T(8,128)(2,1)S(1)} %copy-done.3), custom_call_target="tpu_custom_call" | custom-call | flops 2147483648 | bytes 4194304 | tf_op jit(solution)/shard_map/attend/pallas_call | solution.py:430
  89.2 0.8 collective-permute-done.18
  90.1 0.7 collective-permute-start.20
  90.8 3.5 %collective-permute-start.23 = (bf16[1,128,128]{2,1,0:T(8,128)(2,1)S(1)}, bf16[1,128,128]{2,1,0:T(8,128)(2,1)S(1)}, u32[]{:S(2)}, u32[]{:S(2)}) collective-permute-start(bf16[1,128,128]{2,1,0:T(8,128)(2,1)S(1)} %get-tuple-element.26), channel_id=1, source_target_pairs={{0,8},{8,0},{16,24},{24,16},{1,9},{9,1},{17,25},{25,17},{2,10},{10... | collective-permute-start | bytes 98312 | tf_op jit(solution)/shard_map/ppermute | solution.py:319
  94.2 0.1 stack.71.order
  94.3 3.2 %collective-permute-start.21 = (bf16[1,128,128]{2,1,0:T(8,128)(2,1)S(1)}, bf16[1,128,128]{2,1,0:T(8,128)(2,1)S(1)}, u32[]{:S(2)}, u32[]{:S(2)}) collective-permute-start(bf16[1,128,128]{2,1,0:T(8,128)(2,1)S(1)} %bitcast.40), channel_id=1, source_target_pairs={{0,2},{2,0},{4,6},{6,4},{1,3},{3,1},{5,7},{7,5},{8,10},{10,8},{12,... | collective-permute-start | bytes 98312 | tf_op jit(solution)/shard_map/ppermute | solution.py:319
  97.5 2.9 %collective-permute-start.24 = (bf16[2,128,128]{2,1,0:T(8,128)(2,1)S(1)}, bf16[2,128,128]{2,1,0:T(8,128)(2,1)S(1)}, u32[]{:S(2)}, u32[]{:S(2)}) collective-permute-start(bf16[2,128,128]{2,1,0:T(8,128)(2,1)S(1)} %pad_maximum_fusion.5), channel_id=1, source_target_pairs={{0,16},{8,24},{16,0},{24,8},{1,17},{9,25},{17,1},{25,9},{2,18},{10... | collective-permute-start | bytes 196616 | tf_op jit(solution)/shard_map/ppermute | solution.py:319
  100.4 4.0 %collective-permute-start.22 = (bf16[2,128,128]{2,1,0:T(8,128)(2,1)S(1)}, bf16[2,128,128]{2,1,0:T(8,128)(2,1)S(1)}, u32[]{:S(2)}, u32[]{:S(2)}) collective-permute-start(bf16[2,128,128]{2,1,0:T(8,128)(2,1)S(1)} %pad_maximum_fusion.4), channel_id=1, source_target_pairs={{0,4},{2,6},{4,0},{6,2},{1,5},{3,7},{5,1},{7,3},{8,12},{10,14},{12... | collective-permute-start | bytes 196616 | tf_op jit(solution)/shard_map/ppermute | solution.py:319
  104.5 2.2 %collective-permute-done.22 = bf16[2,128,128]{2,1,0:T(8,128)(2,1)S(1)} collective-permute-done((bf16[2,128,128]{2,1,0:T(8,128)(2,1)S(1)}, bf16[2,128,128]{2,1,0:T(8,128)(2,1)S(1)}, u32[]{:S(2)}, u32[]{:S(2)}) %collective-permute-start.22) | collective-permute-done | bytes 65568 | tf_op jit(solution)/shard_map/ppermute | solution.py:319
  106.7 6.8 %pair_map.1 = bf16[4,128,128,128]{3,2,1,0:T(8,128)(2,1)} custom-call(s32[9]{0:T(128)S(1)} %stack.71.order, f32[16,128]{1,0:T(8,128)S(1)} %copy-done.1, bf16[4,128,128]{2,1,0:T(8,128)(2,1)S(1)} %pad_maximum_fusion.2.row_feats, bf16[4,128,128]{2,1,0:T(8,128)(2,1)S(1)} %pad_maximum_fusion.3.col_feats), custom_call_target="tpu_custom_call" | custom-call | tf_op jit(solution)/shard_map/pair_map/pallas_call | solution.py:478
  (58 shorter events, 0.4 us)
Async XLA Ops:
  0.0 1.0 copy-start
  1.0 10.4 %collective-permute-start.1 = (bf16[256,384]{1,0:T(8,128)(2,1)S(1)}, bf16[256,384]{1,0:T(8,128)(2,1)S(1)}, u32[]{:S(2)}, u32[]{:S(2)}) collective-permute-start(bf16[256,384]{1,0:T(8,128)(2,1)S(1)} %constant_dynamic-slice_fusion), channel_id=1, source_target_pairs={{0,6},{2,0},{4,2},{6,4},{1,7},{3,1},{5,3},{7,5},{8,14},{10,8},{12,... | collective-permute-start | bytes 589832 | tf_op jit(solution)/shard_map/ppermute | solution.py:331
  6.1 9.3 %collective-permute-start = (bf16[256,384]{1,0:T(8,128)(2,1)S(1)}, bf16[256,384]{1,0:T(8,128)(2,1)S(1)}, u32[]{:S(2)}, u32[]{:S(2)}) collective-permute-start(bf16[256,384]{1,0:T(8,128)(2,1)S(1)} %constant_dynamic-slice_fusion), channel_id=1, source_target_pairs={{0,2},{2,4},{4,6},{6,0},{1,3},{3,5},{5,7},{7,1},{8,10},{10,12},{12... | collective-permute-start | bytes 589832 | tf_op jit(solution)/shard_map/ppermute | solution.py:331
  6.2 31.6 %copy-start.8 = (f32[384]{0:T(512)S(1)}, f32[384]{0:T(512)}, u32[]{:S(2)}) copy-start(f32[384]{0:T(512)} %param.11) | copy-start | bytes 4612
  6.2 31.6 %copy-start.7 = (f32[3,384]{1,0:T(4,128)S(1)}, f32[3,384]{1,0:T(4,128)}, u32[]{:S(2)}) copy-start(f32[3,384]{1,0:T(4,128)} %param.10) | copy-start | bytes 13828
  6.2 41.7 %copy-start.3 = (bf16[384,256]{1,0:T(8,128)(2,1)S(1)}, bf16[384,256]{1,0:T(8,128)(2,1)}, u32[]{:S(2)}) copy-start(bf16[384,256]{1,0:T(8,128)(2,1)} %refs_1_.3) | copy-start | bytes 589828
  15.4 35.5 %copy-start.9 = (s32[4,2]{0,1:T(2,128)S(1)}, s32[4,2]{0,1:T(2,128)}, u32[]{:S(2)}) copy-start(s32[4,2]{0,1:T(2,128)} %param.9) | copy-start | bytes 100
  15.5 15.8 %collective-permute-start.5 = (bf16[3,256,384]{2,1,0:T(8,128)(2,1)S(1)}, bf16[3,256,384]{2,1,0:T(8,128)(2,1)}, u32[]{:S(2)}, u32[]{:S(2)}) collective-permute-start(bf16[3,256,384]{2,1,0:T(8,128)(2,1)S(1)} %pad_maximum_fusion.1), channel_id=1, source_target_pairs={{0,8},{8,0},{16,24},{24,16},{1,9},{9,1},{17,25},{25,17},{2,10},{10... | collective-permute-start | bytes 1769480 | tf_op jit(solution)/shard_map/ppermute | solution.py:332
  17.0 18.1 %collective-permute-start.2 = (bf16[3,256,384]{2,1,0:T(8,128)(2,1)S(1)}, bf16[3,256,384]{2,1,0:T(8,128)(2,1)S(1)}, u32[]{:S(2)}, u32[]{:S(2)}) collective-permute-start(bf16[3,256,384]{2,1,0:T(8,128)(2,1)S(1)} %pad_maximum_fusion.1), channel_id=1, source_target_pairs={{0,16},{8,24},{16,0},{24,8},{1,17},{9,25},{17,1},{25,9},{2,18},{10... | collective-permute-start | bytes 1769480 | tf_op jit(solution)/shard_map/ppermute | solution.py:332
  18.6 10.5 %collective-permute-start.3 = (bf16[256,384]{1,0:T(8,128)(2,1)S(1)}, bf16[256,384]{1,0:T(8,128)(2,1)}, u32[]{:S(2)}, u32[]{:S(2)}) collective-permute-start(bf16[256,384]{1,0:T(8,128)(2,1)S(1)} %constant_dynamic-slice_fusion), channel_id=1, source_target_pairs={{0,4},{2,6},{4,0},{6,2},{1,5},{3,7},{5,1},{7,3},{8,12},{10,14},{12... | collective-permute-start | bytes 589832 | tf_op jit(solution)/shard_map/ppermute | solution.py:331
  29.1 6.0 %collective-permute-start.6 = (bf16[1,256,384]{2,1,0:T(8,128)(2,1)}, bf16[1,256,384]{2,1,0:T(8,128)(2,1)S(1)}, u32[]{:S(2)}, u32[]{:S(2)}) collective-permute-start(bf16[1,256,384]{2,1,0:T(8,128)(2,1)} %bitcast.13), channel_id=1, source_target_pairs={{0,8},{8,0},{16,24},{24,16},{1,9},{9,1},{17,25},{25,17},{2,10},{10... | collective-permute-start | bytes 589832 | tf_op jit(solution)/shard_map/ppermute | solution.py:332
  29.6 5.9 %collective-permute-start.4 = (bf16[1,256,384]{2,1,0:T(8,128)(2,1)}, bf16[1,256,384]{2,1,0:T(8,128)(2,1)S(1)}, u32[]{:S(2)}, u32[]{:S(2)}) collective-permute-start(bf16[1,256,384]{2,1,0:T(8,128)(2,1)} %bitcast.13), channel_id=1, source_target_pairs={{0,16},{8,24},{16,0},{24,8},{1,17},{9,25},{17,1},{25,9},{2,18},{10... | collective-permute-start | bytes 589832 | tf_op jit(solution)/shard_map/ppermute | solution.py:332
  31.2 17.9 %copy-start.6 = (bf16[4,256,384]{2,1,0:T(8,128)(2,1)}, bf16[4,256,384]{2,1,0:T(8,128)(2,1)S(1)}, u32[]{:S(2)}) copy-start(bf16[4,256,384]{2,1,0:T(8,128)(2,1)S(1)} %pad_maximum_fusion.refs_1_) | copy-start | bytes 2359300
  31.2 14.9 %collective-permute-start.8 = (bf16[4,256,384]{2,1,0:T(8,128)(2,1)S(1)}, bf16[4,256,384]{2,1,0:T(8,128)(2,1)S(1)}, u32[]{:S(2)}, u32[]{:S(2)}) collective-permute-start(bf16[4,256,384]{2,1,0:T(8,128)(2,1)S(1)} %pad_maximum_fusion.refs_1_), channel_id=1, source_target_pairs={{0,1},{1,0},{2,3},{3,2},{4,5},{5,4},{6,7},{7,6},{8,9},{9,8},{10,11... | collective-permute-start | bytes 2359304 | tf_op jit(solution)/shard_map/ppermute | solution.py:329
  35.1 16.2 %copy-start.5 = (bf16[4,256,384]{2,1,0:T(8,128)(2,1)}, bf16[4,256,384]{2,1,0:T(8,128)(2,1)S(1)}, u32[]{:S(2)}) copy-start(bf16[4,256,384]{2,1,0:T(8,128)(2,1)S(1)} %constant_dynamic-update-slice_fusion.2.refs_2_) | copy-start | bytes 2359300
  35.5 15.8 %copy-start.4 = (bf16[4,256,384]{2,1,0:T(8,128)(2,1)}, bf16[4,256,384]{2,1,0:T(8,128)(2,1)S(1)}, u32[]{:S(2)}) copy-start(bf16[4,256,384]{2,1,0:T(8,128)(2,1)S(1)} %constant_dynamic-update-slice_fusion.refs_3_) | copy-start | bytes 2359300
  35.7 12.2 %collective-permute-start.7 = (bf16[4,256,384]{2,1,0:T(8,128)(2,1)S(1)}, bf16[4,256,384]{2,1,0:T(8,128)(2,1)}, u32[]{:S(2)}, u32[]{:S(2)}) collective-permute-start(bf16[4,256,384]{2,1,0:T(8,128)(2,1)S(1)} %broadcast_select_fusion), channel_id=1, source_target_pairs={{0,8},{1,17},{8,0},{9,25},{16,24},{17,1},{24,16},{25,9},{2,10},{3,... | collective-permute-start | bytes 2359304 | tf_op jit(solution)/shard_map/ppermute | solution.py:342
  37.2 10.6 %collective-permute-start.10 = (bf16[4,256,384]{2,1,0:T(8,128)(2,1)S(1)}, bf16[4,256,384]{2,1,0:T(8,128)(2,1)S(1)}, u32[]{:S(2)}, u32[]{:S(2)}) collective-permute-start(bf16[4,256,384]{2,1,0:T(8,128)(2,1)S(1)} %constant_dynamic-update-slice_fusion.refs_3_), channel_id=1, source_target_pairs={{0,1},{1,0},{2,3},{3,2},{4,5},{5,4},{6,7},{7,6},{8,9},{9,8},{10,11... | collective-permute-start | bytes 2359304 | tf_op jit(solution)/shard_map/ppermute | solution.py:329
  37.2 10.6 %collective-permute-start.9 = (bf16[4,256,384]{2,1,0:T(8,128)(2,1)S(1)}, bf16[4,256,384]{2,1,0:T(8,128)(2,1)S(1)}, u32[]{:S(2)}, u32[]{:S(2)}) collective-permute-start(bf16[4,256,384]{2,1,0:T(8,128)(2,1)S(1)} %constant_dynamic-update-slice_fusion.2.refs_2_), channel_id=1, source_target_pairs={{0,1},{1,0},{2,3},{3,2},{4,5},{5,4},{6,7},{7,6},{8,9},{9,8},{10,11... | collective-permute-start | bytes 2359304 | tf_op jit(solution)/shard_map/ppermute | solution.py:329
  37.7 3.7 %collective-permute-start.11 = (f32[4,384]{1,0:T(4,128)S(1)}, f32[4,384]{1,0:T(4,128)S(1)}, u32[]{:S(2)}, u32[]{:S(2)}) collective-permute-start(f32[4,384]{1,0:T(4,128)S(1)} %pad_maximum_fusion.8), channel_id=1, source_target_pairs={{0,2},{2,0},{4,6},{6,4},{1,3},{3,1},{5,7},{7,5},{8,10},{10,8},{12,... | collective-permute-start | bytes 18440 | tf_op jit(solution)/shard_map/ppermute | solution.py:345
  41.5 4.7 %collective-permute-start.12 = (f32[8,384]{1,0:T(8,128)S(1)}, f32[8,384]{1,0:T(8,128)S(1)}, u32[]{:S(2)}, u32[]{:S(2)}) collective-permute-start(f32[8,384]{1,0:T(8,128)S(1)} %pad_maximum_fusion.7), channel_id=1, source_target_pairs={{0,4},{2,6},{4,0},{6,2},{1,5},{3,7},{5,1},{7,3},{8,12},{10,14},{12... | collective-permute-start | bytes 36872 | tf_op jit(solution)/shard_map/ppermute | solution.py:345
  46.1 4.6 %copy-start.10 = (bf16[4,256,384]{2,1,0:T(8,128)(2,1)}, bf16[4,256,384]{2,1,0:T(8,128)(2,1)S(1)}, u32[]{:S(2)}) copy-start(bf16[4,256,384]{2,1,0:T(8,128)(2,1)S(1)} %collective-permute-done.8.refs_5_) | copy-start | bytes 2359300
  47.8 3.0 %copy-start.11 = (bf16[4,256,384]{2,1,0:T(8,128)(2,1)}, bf16[4,256,384]{2,1,0:T(8,128)(2,1)S(1)}, u32[]{:S(2)}) copy-start(bf16[4,256,384]{2,1,0:T(8,128)(2,1)S(1)} %collective-permute-done.10.refs_7_) | copy-start | bytes 2359300
  47.8 3.0 %copy-start.12 = (bf16[4,256,384]{2,1,0:T(8,128)(2,1)}, bf16[4,256,384]{2,1,0:T(8,128)(2,1)S(1)}, u32[]{:S(2)}) copy-start(bf16[4,256,384]{2,1,0:T(8,128)(2,1)S(1)} %collective-permute-done.9.refs_6_) | copy-start | bytes 2359300
  47.8 3.5 %collective-permute-start.13 = (bf16[4,256,384]{2,1,0:T(8,128)(2,1)}, bf16[4,256,384]{2,1,0:T(8,128)(2,1)}, u32[]{:S(2)}, u32[]{:S(2)}) collective-permute-start(bf16[4,256,384]{2,1,0:T(8,128)(2,1)} %collective-permute-done.7.refs_4_), channel_id=1, source_target_pairs={{0,1},{1,0},{2,3},{3,2},{4,5},{5,4},{6,7},{7,6},{8,9},{9,8},{10,11... | collective-permute-start | bytes 2359304 | tf_op jit(solution)/shard_map/ppermute | solution.py:329
  47.9 19.6 %collective-permute-start.16 = (bf16[384,256]{1,0:T(8,128)(2,1)S(1)}, bf16[384,256]{1,0:T(8,128)(2,1)S(1)}, u32[]{:S(2)}, u32[]{:S(2)}) collective-permute-start(bf16[384,256]{1,0:T(8,128)(2,1)S(1)} %copy-done.3), channel_id=1, source_target_pairs={{0,6},{2,0},{4,2},{6,4},{1,7},{3,1},{5,3},{7,5},{8,14},{10,8},{12,... | collective-permute-start | bytes 589832 | tf_op jit(solution)/shard_map/ppermute | solution.py:311
  49.2 19.5 %collective-permute-start.15 = (bf16[384,256]{1,0:T(8,128)(2,1)S(1)}, bf16[384,256]{1,0:T(8,128)(2,1)S(1)}, u32[]{:S(2)}, u32[]{:S(2)}) collective-permute-start(bf16[384,256]{1,0:T(8,128)(2,1)S(1)} %copy-done.3), channel_id=1, source_target_pairs={{0,4},{2,6},{4,0},{6,2},{1,5},{3,7},{5,1},{7,3},{8,12},{10,14},{12... | collective-permute-start | bytes 589832 | tf_op jit(solution)/shard_map/ppermute | solution.py:311
  50.8 17.8 %collective-permute-start.14 = (bf16[384,256]{1,0:T(8,128)(2,1)S(1)}, bf16[384,256]{1,0:T(8,128)(2,1)S(1)}, u32[]{:S(2)}, u32[]{:S(2)}) collective-permute-start(bf16[384,256]{1,0:T(8,128)(2,1)S(1)} %copy-done.3), channel_id=1, source_target_pairs={{0,2},{2,4},{4,6},{6,0},{1,3},{3,5},{5,7},{7,1},{8,10},{10,12},{12... | collective-permute-start | bytes 589832 | tf_op jit(solution)/shard_map/ppermute | solution.py:311
  51.3 17.3 %copy-start.2 = (bf16[384,1536]{1,0:T(8,128)(2,1)S(1)}, bf16[384,1536]{1,0:T(8,128)(2,1)}, u32[]{:S(2)}) copy-start(bf16[384,1536]{1,0:T(8,128)(2,1)} %refs_0_.1) | copy-start | bytes 3538948
  80.9 8.3 %collective-permute-start.17 = (bf16[128,256]{1,0:T(8,128)(2,1)S(1)}, bf16[128,256]{1,0:T(8,128)(2,1)S(1)}, u32[]{:S(2)}, u32[]{:S(2)}) collective-permute-start(bf16[128,256]{1,0:T(8,128)(2,1)S(1)} %get-tuple-element.23), channel_id=1, source_target_pairs={{0,2},{2,4},{4,6},{6,0},{1,3},{3,5},{5,7},{7,1},{8,10},{10,12},{12... | collective-permute-start | bytes 196616 | tf_op jit(solution)/shard_map/ppermute | solution.py:459
  81.7 7.5 %collective-permute-start.19 = (bf16[128,256]{1,0:T(8,128)(2,1)S(1)}, bf16[128,256]{1,0:T(8,128)(2,1)S(1)}, u32[]{:S(2)}, u32[]{:S(2)}) collective-permute-start(bf16[128,256]{1,0:T(8,128)(2,1)S(1)} %get-tuple-element.24), channel_id=1, source_target_pairs={{0,6},{2,0},{4,2},{6,4},{1,7},{3,1},{5,3},{7,5},{8,14},{10,8},{12,... | collective-permute-start | bytes 196616 | tf_op jit(solution)/shard_map/ppermute | solution.py:459
  84.7 5.3 %collective-permute-start.18 = (bf16[128,256]{1,0:T(8,128)(2,1)S(1)}, bf16[128,256]{1,0:T(8,128)(2,1)S(1)}, u32[]{:S(2)}, u32[]{:S(2)}) collective-permute-start(bf16[128,256]{1,0:T(8,128)(2,1)S(1)} %get-tuple-element.25), channel_id=1, source_target_pairs={{0,4},{2,6},{4,0},{6,2},{1,5},{3,7},{5,1},{7,3},{8,12},{10,14},{12... | collective-permute-start | bytes 196616 | tf_op jit(solution)/shard_map/ppermute | solution.py:459
  84.7 22.0 %copy-start.1 = (f32[16,128]{1,0:T(8,128)S(1)}, f32[16,128]{1,0:T(8,128)}, u32[]{:S(2)}) copy-start(f32[16,128]{1,0:T(8,128)} %dist_table.1) | copy-start | bytes 24580
  90.1 4.2 %collective-permute-start.20 = (bf16[128,128]{1,0:T(8,128)(2,1)S(1)}, bf16[128,128]{1,0:T(8,128)(2,1)S(1)}, u32[]{:S(2)}, u32[]{:S(2)}) collective-permute-start(bf16[128,128]{1,0:T(8,128)(2,1)S(1)} %get-tuple-element.27), channel_id=1, source_target_pairs={{0,0},{2,8},{4,16},{6,24},{8,2},{10,10},{12,18},{14,26},{16,4},{18... | collective-permute-start | bytes 98312 | tf_op jit(solution)/shard_map/ppermute | solution.py:460
  90.8 6.7 %collective-permute-start.23 = (bf16[1,128,128]{2,1,0:T(8,128)(2,1)S(1)}, bf16[1,128,128]{2,1,0:T(8,128)(2,1)S(1)}, u32[]{:S(2)}, u32[]{:S(2)}) collective-permute-start(bf16[1,128,128]{2,1,0:T(8,128)(2,1)S(1)} %get-tuple-element.26), channel_id=1, source_target_pairs={{0,8},{8,0},{16,24},{24,16},{1,9},{9,1},{17,25},{25,17},{2,10},{10... | collective-permute-start | bytes 98312 | tf_op jit(solution)/shard_map/ppermute | solution.py:319
  94.3 6.1 %collective-permute-start.21 = (bf16[1,128,128]{2,1,0:T(8,128)(2,1)S(1)}, bf16[1,128,128]{2,1,0:T(8,128)(2,1)S(1)}, u32[]{:S(2)}, u32[]{:S(2)}) collective-permute-start(bf16[1,128,128]{2,1,0:T(8,128)(2,1)S(1)} %bitcast.40), channel_id=1, source_target_pairs={{0,2},{2,0},{4,6},{6,4},{1,3},{3,1},{5,7},{7,5},{8,10},{10,8},{12,... | collective-permute-start | bytes 98312 | tf_op jit(solution)/shard_map/ppermute | solution.py:319
  97.5 7.0 %collective-permute-start.24 = (bf16[2,128,128]{2,1,0:T(8,128)(2,1)S(1)}, bf16[2,128,128]{2,1,0:T(8,128)(2,1)S(1)}, u32[]{:S(2)}, u32[]{:S(2)}) collective-permute-start(bf16[2,128,128]{2,1,0:T(8,128)(2,1)S(1)} %pad_maximum_fusion.5), channel_id=1, source_target_pairs={{0,16},{8,24},{16,0},{24,8},{1,17},{9,25},{17,1},{25,9},{2,18},{10... | collective-permute-start | bytes 196616 | tf_op jit(solution)/shard_map/ppermute | solution.py:319
  100.4 6.3 %collective-permute-start.22 = (bf16[2,128,128]{2,1,0:T(8,128)(2,1)S(1)}, bf16[2,128,128]{2,1,0:T(8,128)(2,1)S(1)}, u32[]{:S(2)}, u32[]{:S(2)}) collective-permute-start(bf16[2,128,128]{2,1,0:T(8,128)(2,1)S(1)} %pad_maximum_fusion.4), channel_id=1, source_target_pairs={{0,4},{2,6},{4,0},{6,2},{1,5},{3,7},{5,1},{7,3},{8,12},{10,14},{12... | collective-permute-start | bytes 196616 | tf_op jit(solution)/shard_map/ppermute | solution.py:319

commit v5 on v4

--- a/solution.py
+++ b/solution.py
@@ -415,8 +415,8 @@
 
     chunk = min(tokens, CHUNK)
 
-    pair_parts = shifts(w_pair, "head")
-    order_of_parts = [(ours + n_head - s) % n_head for s in range(n_head)]
+    pair_parts = list(doubled(w_pair, "head"))
+    order_of_parts = [ours ^ s for s in range(n_head)]
 
     def attend(order, dtype, w_mix):
         count = order.shape[0]

time: 114 us -> 131 us (1.15)
  waiting for transfers between devices: 35.4 us -> 53.6 us
  starting transfers between devices: 33.7 us -> 30.8 us
    ppermute x4 -> x6, waiting for transfers between devices: 2.23 us -> 22 us  [doubled(): moved = lax.ppermute(found, axis, [(k, k ^ bit) for k in range(size)])]
    ppermute x3 -> x0, starting transfers between devices: 2.9 us -> none  [shifts(): lax.ppermute(array, axis, [(k, (k + s) % size) for k in range(size)])]
    ppermute x4 -> x6, starting transfers between devices: 13.6 us -> 13.6 us  [doubled(): moved = lax.ppermute(found, axis, [(k, k ^ bit) for k in range(size)])]
  transfers between devices with their start and end apart: 25 -> 24, of which waited for: 11 -> 12; matrix products, arithmetic and copies ran while one was open for 3% -> 2% of each run, Pallas kernels for 18% -> 3%
where the time goes in v5:
time: 131 us; the launch traced here: 130 us
  waiting for transfers between devices  53.6 us (41%)
  Pallas kernels  39.6 us (30%)
  starting transfers between devices  30.8 us (24%)
  local copies, waits for them, and re-layouts  4.08 us (3%)
  other arithmetic  1.42 us (1%)
    ppermute x6, waiting for transfers between devices, doubled(): moved = lax.ppermute(found, axis, [(k, k ^ bit) for k in range(size)])  22 us
    ppermute x3, waiting for transfers between devices, gather_rows(): lax.ppermute(array, 'head', [(k, (k + s) % 4) for k in range(4)])  19 us
    pallas_call x2, Pallas kernels, attend(): pl.pallas_call(functools.partial(attend_kernel, heads, own, len(mixing)),...  16.4 us
    pallas_call x1, Pallas kernels, local(): pl.pallas_call(functools.partial(project_kernel, heads, n_var, n_head, le...  16.4 us
    ppermute x6, starting transfers between devices, doubled(): moved = lax.ppermute(found, axis, [(k, k ^ bit) for k in range(size)])  13.6 us
    ppermute x2, waiting for transfers between devices, gather_rows(): moved = lax.ppermute(taps, 'head', [(k, k ^ bit) for k in range(4)])  7.83 us
    pallas_call x1, Pallas kernels, local(): pl.pallas_call(functools.partial(pair_kernel, variants), out_shape=jax.Sh...  6.76 us
    ppermute x3, starting transfers between devices, gather_rows(): lax.ppermute(array, 'head', [(k, (k + s) % 4) for k in range(4)])  5.84 us
  transfers between devices with their start and end apart: 24, of which 12 were waited for; matrix products, arithmetic and copies ran while one was open for 2% of the time, Pallas kernels for 3%

profile of v5, /device:TPU:0, one launch (start us, length us, event | category | flops | bytes accessed | tf_op | source)
XLA Modules:
  0.0 130.0 jit_solution(6494202362745156344)
XLA Ops:
  0.0 1.0 copy-done
  1.0 5.1 %collective-permute-start.1 = (bf16[256,384]{1,0:T(8,128)(2,1)S(1)}, bf16[256,384]{1,0:T(8,128)(2,1)S(1)}, u32[]{:S(2)}, u32[]{:S(2)}) collective-permute-start(bf16[256,384]{1,0:T(8,128)(2,1)S(1)} %constant_dynamic-slice_fusion), channel_id=1, source_target_pairs={{0,6},{2,0},{4,2},{6,4},{1,7},{3,1},{5,3},{7,5},{8,14},{10,8},{12,... | collective-permute-start | bytes 589832 | tf_op jit(solution)/shard_map/ppermute | solution.py:331
  6.2 5.2 %collective-permute-done.1 = bf16[256,384]{1,0:T(8,128)(2,1)S(1)} collective-permute-done((bf16[256,384]{1,0:T(8,128)(2,1)S(1)}, bf16[256,384]{1,0:T(8,128)(2,1)S(1)}, u32[]{:S(2)}, u32[]{:S(2)}) %collective-permute-start.1) | collective-permute-done | bytes 196640 | tf_op jit(solution)/shard_map/ppermute | solution.py:331
  11.4 4.0 %collective-permute-done = bf16[256,384]{1,0:T(8,128)(2,1)S(1)} collective-permute-done((bf16[256,384]{1,0:T(8,128)(2,1)S(1)}, bf16[256,384]{1,0:T(8,128)(2,1)S(1)}, u32[]{:S(2)}, u32[]{:S(2)}) %collective-permute-start) | collective-permute-done | bytes 196640 | tf_op jit(solution)/shard_map/ppermute | solution.py:331
  15.4 0.1 pad_maximum_fusion.1
  15.5 1.6 %collective-permute-start.5 = (bf16[3,256,384]{2,1,0:T(8,128)(2,1)S(1)}, bf16[3,256,384]{2,1,0:T(8,128)(2,1)}, u32[]{:S(2)}, u32[]{:S(2)}) collective-permute-start(bf16[3,256,384]{2,1,0:T(8,128)(2,1)S(1)} %pad_maximum_fusion.1), channel_id=1, source_target_pairs={{0,8},{8,0},{16,24},{24,16},{1,9},{9,1},{17,25},{25,17},{2,10},{10... | collective-permute-start | bytes 1769480 | tf_op jit(solution)/shard_map/ppermute | solution.py:332
  17.1 1.5 %collective-permute-start.2 = (bf16[3,256,384]{2,1,0:T(8,128)(2,1)S(1)}, bf16[3,256,384]{2,1,0:T(8,128)(2,1)S(1)}, u32[]{:S(2)}, u32[]{:S(2)}) collective-permute-start(bf16[3,256,384]{2,1,0:T(8,128)(2,1)S(1)} %pad_maximum_fusion.1), channel_id=1, source_target_pairs={{0,16},{8,24},{16,0},{24,8},{1,17},{9,25},{17,1},{25,9},{2,18},{10... | collective-permute-start | bytes 1769480 | tf_op jit(solution)/shard_map/ppermute | solution.py:332
  18.6 0.7 collective-permute-start.3
  19.3 9.8 %collective-permute-done.3 = bf16[256,384]{1,0:T(8,128)(2,1)} collective-permute-done((bf16[256,384]{1,0:T(8,128)(2,1)S(1)}, bf16[256,384]{1,0:T(8,128)(2,1)}, u32[]{:S(2)}, u32[]{:S(2)}) %collective-permute-start.3) | collective-permute-done | bytes 196640 | tf_op jit(solution)/shard_map/ppermute | solution.py:331
  29.1 0.5 collective-permute-start.6
  29.6 0.5 collective-permute-start.4
  30.1 1.1 pad_maximum_fusion.refs_1_
  31.2 0.1 collective-permute-start.8
  31.3 1.3 %constant_dynamic-update-slice_fusion.3 = bf16[4,256,384]{2,1,0:T(8,128)(2,1)S(1)} fusion(bf16[3,256,384]{2,1,0:T(8,128)(2,1)} %collective-permute-done.5), kind=kLoop, calls=%fused_computation.23 | loop fusion | bytes 1179648
  32.7 2.4 %collective-permute-done.6 = bf16[1,256,384]{2,1,0:T(8,128)(2,1)S(1)} collective-permute-done((bf16[1,256,384]{2,1,0:T(8,128)(2,1)}, bf16[1,256,384]{2,1,0:T(8,128)(2,1)S(1)}, u32[]{:S(2)}, u32[]{:S(2)}) %collective-permute-start.6) | collective-permute-done | bytes 196640 | tf_op jit(solution)/shard_map/ppermute | solution.py:332
  35.1 0.1 constant_dynamic-update-slice_fusion.1
  35.2 0.3 collective-permute-done.4
  35.6 0.1 broadcast_select_fusion
  35.7 1.6 %collective-permute-start.7 = (bf16[4,256,384]{2,1,0:T(8,128)(2,1)S(1)}, bf16[4,256,384]{2,1,0:T(8,128)(2,1)}, u32[]{:S(2)}, u32[]{:S(2)}) collective-permute-start(bf16[4,256,384]{2,1,0:T(8,128)(2,1)S(1)} %broadcast_select_fusion), channel_id=1, source_target_pairs={{0,8},{1,17},{8,0},{9,25},{16,24},{17,1},{24,16},{25,9},{2,10},{3,... | collective-permute-start | bytes 2359304 | tf_op jit(solution)/shard_map/ppermute | solution.py:342
  37.2 0.5 collective-permute-start.9
  37.8 0.4 collective-permute-start.11
  38.2 3.3 %collective-permute-done.11 = f32[4,384]{1,0:T(4,128)S(1)} collective-permute-done((f32[4,384]{1,0:T(4,128)S(1)}, f32[4,384]{1,0:T(4,128)S(1)}, u32[]{:S(2)}, u32[]{:S(2)}) %collective-permute-start.11) | collective-permute-done | bytes 6176 | tf_op jit(solution)/shard_map/ppermute | solution.py:345
  41.5 0.1 collective-permute-start.12
  41.5 4.6 %collective-permute-done.12 = f32[8,384]{1,0:T(8,128)S(1)} collective-permute-done((f32[8,384]{1,0:T(8,128)S(1)}, f32[8,384]{1,0:T(8,128)S(1)}, u32[]{:S(2)}, u32[]{:S(2)}) %collective-permute-start.12) | collective-permute-done | bytes 12320 | tf_op jit(solution)/shard_map/ppermute | solution.py:345
  46.1 0.4 collective-permute-start.14
  46.5 1.3 collective-permute-done.7.refs_4_
  47.8 0.1 collective-permute-start.13
  47.9 0.8 copy-done.11
  48.7 0.3 copy-done.12
  49.0 2.8 %collective-permute-done.14 = bf16[1,384,256]{2,1,0:T(8,128)(2,1)S(1)} collective-permute-done((bf16[1,384,256]{2,1,0:T(8,128)(2,1)S(1)}, bf16[1,384,256]{2,1,0:T(8,128)(2,1)S(1)}, u32[]{:S(2)}, u32[]{:S(2)}) %collective-permute-start.14) | collective-permute-done | bytes 196640 | tf_op jit(solution)/shard_map/ppermute | solution.py:319
  51.9 0.1 collective-permute-start.15
  51.9 0.2 dynamic-slice_reduce_fusion
  52.1 0.1 concatenate.51.order
  52.2 0.1 concatenate.44.scalars
  52.3 16.9 %collective-permute-done.15 = bf16[2,384,256]{2,1,0:T(8,128)(2,1)S(1)} collective-permute-done((bf16[2,384,256]{2,1,0:T(8,128)(2,1)S(1)}, bf16[2,384,256]{2,1,0:T(8,128)(2,1)S(1)}, u32[]{:S(2)}, u32[]{:S(2)}) %collective-permute-start.15) | collective-permute-done | bytes 393248 | tf_op jit(solution)/shard_map/ppermute | solution.py:319
  69.3 16.4 %project.1 = (bf16[2048,1024]{1,0:T(8,128)(2,1)S(1)}, f32[512,384]{1,0:T(8,128)S(1)}) custom-call(s32[8]{0:T(128)S(1)} %concatenate.44.scalars, bf16[1536,896]{1,0:T(8,128)(2,1)} %w_proj.1, f32[4,4,384]{2,1,0:T(4,128)S(1)} %reshape.3.refs_0_, bf16[4,256,384]{2,1,0:T(8,128)(2,1)} %copy-done.6, bf16[4,256,384]{2,1,0:T(8,128)(2,1)} %copy-done.5, ...), custom_call_target="tpu_custom_call" | custom-call | flops 7952400384 | bytes 12582912 | tf_op jit(solution)/shard_map/project/pallas_call | solution.py:384
  85.8 12.0 %attend.2 = (bf16[3,128,256]{2,1,0:T(8,128)(2,1)S(1)}, bf16[2,256,256]{2,1,0:T(8,128)(2,1)S(1)}) custom-call(s32[7]{0:T(128)S(1)} %concatenate.51.order, bf16[2048,1024]{1,0:T(8,128)(2,1)S(1)} %get-tuple-element.19.kvq, f32[512,384]{1,0:T(8,128)S(1)} %get-tuple-element.20.pooled, bf16[384,1536]{1,0:T(8,128)(2,1)S(1)} %copy-done.3, ...), custom_call_target="tpu_custom_call" | custom-call | flops 6442450944 | bytes 4194304 | tf_op jit(solution)/shard_map/attend/pallas_call | solution.py:430
  97.9 3.8 %collective-permute-start.18 = (bf16[128,256]{1,0:T(8,128)(2,1)S(1)}, bf16[128,256]{1,0:T(8,128)(2,1)S(1)}, u32[]{:S(2)}, u32[]{:S(2)}) collective-permute-start(bf16[128,256]{1,0:T(8,128)(2,1)S(1)} %get-tuple-element.26), channel_id=1, source_target_pairs={{0,6},{2,0},{4,2},{6,4},{1,7},{3,1},{5,3},{7,5},{8,14},{10,8},{12,... | collective-permute-start | bytes 196616 | tf_op jit(solution)/shard_map/ppermute | solution.py:459
  101.7 4.4 %attend.3 = f32[1,128,256]{2,1,0:T(8,128)S(1)} custom-call(s32[1]{0:T(128)} %bitcast.order, bf16[2048,1024]{1,0:T(8,128)(2,1)S(1)} %get-tuple-element.19.kvq, f32[512,384]{1,0:T(8,128)S(1)} %get-tuple-element.20.pooled, bf16[2,256,256]{2,1,0:T(8,128)(2,1)S(1)} %get-tuple-element.21.refs_0_, bf16[384,256]{1,0:T(8,128)(2,1)S(1)} %copy-done.1), custom_call_target="tpu_custom_call" | custom-call | flops 2147483648 | bytes 4194304 | tf_op jit(solution)/shard_map/attend/pallas_call | solution.py:430
  106.1 0.7 collective-permute-done.17
  106.9 0.7 collective-permute-start.19
  107.6 2.7 %collective-permute-start.22 = (bf16[1,128,128]{2,1,0:T(8,128)(2,1)S(1)}, bf16[1,128,128]{2,1,0:T(8,128)(2,1)S(1)}, u32[]{:S(2)}, u32[]{:S(2)}) collective-permute-start(bf16[1,128,128]{2,1,0:T(8,128)(2,1)S(1)} %get-tuple-element.28), channel_id=1, source_target_pairs={{0,8},{8,0},{16,24},{24,16},{1,9},{9,1},{17,25},{25,17},{2,10},{10... | collective-permute-start | bytes 98312 | tf_op jit(solution)/shard_map/ppermute | solution.py:319
  110.3 0.1 stack.63.order
  110.4 3.2 %collective-permute-start.20 = (bf16[1,128,128]{2,1,0:T(8,128)(2,1)S(1)}, bf16[1,128,128]{2,1,0:T(8,128)(2,1)S(1)}, u32[]{:S(2)}, u32[]{:S(2)}) collective-permute-start(bf16[1,128,128]{2,1,0:T(8,128)(2,1)S(1)} %bitcast.45), channel_id=1, source_target_pairs={{0,2},{2,0},{4,6},{6,4},{1,3},{3,1},{5,7},{7,5},{8,10},{10,8},{12,... | collective-permute-start | bytes 98312 | tf_op jit(solution)/shard_map/ppermute | solution.py:319
  113.6 3.0 %collective-permute-start.23 = (bf16[2,128,128]{2,1,0:T(8,128)(2,1)S(1)}, bf16[2,128,128]{2,1,0:T(8,128)(2,1)S(1)}, u32[]{:S(2)}, u32[]{:S(2)}) collective-permute-start(bf16[2,128,128]{2,1,0:T(8,128)(2,1)S(1)} %pad_maximum_fusion.6), channel_id=1, source_target_pairs={{0,16},{8,24},{16,0},{24,8},{1,17},{9,25},{17,1},{25,9},{2,18},{10... | collective-permute-start | bytes 196616 | tf_op jit(solution)/shard_map/ppermute | solution.py:319
  116.6 4.2 %collective-permute-start.21 = (bf16[2,128,128]{2,1,0:T(8,128)(2,1)S(1)}, bf16[2,128,128]{2,1,0:T(8,128)(2,1)S(1)}, u32[]{:S(2)}, u32[]{:S(2)}) collective-permute-start(bf16[2,128,128]{2,1,0:T(8,128)(2,1)S(1)} %pad_maximum_fusion.5), channel_id=1, source_target_pairs={{0,4},{2,6},{4,0},{6,2},{1,5},{3,7},{5,1},{7,3},{8,12},{10,14},{12... | collective-permute-start | bytes 196616 | tf_op jit(solution)/shard_map/ppermute | solution.py:319
  120.8 2.2 %collective-permute-done.21 = bf16[2,128,128]{2,1,0:T(8,128)(2,1)S(1)} collective-permute-done((bf16[2,128,128]{2,1,0:T(8,128)(2,1)S(1)}, bf16[2,128,128]{2,1,0:T(8,128)(2,1)S(1)}, u32[]{:S(2)}, u32[]{:S(2)}) %collective-permute-start.21) | collective-permute-done | bytes 65568 | tf_op jit(solution)/shard_map/ppermute | solution.py:319
  123.1 6.8 %pair_map.1 = bf16[4,128,128,128]{3,2,1,0:T(8,128)(2,1)} custom-call(s32[9]{0:T(128)S(1)} %stack.63.order, f32[16,128]{1,0:T(8,128)S(1)} %copy-done.2, bf16[4,128,128]{2,1,0:T(8,128)(2,1)S(1)} %pad_maximum_fusion.3.row_feats, bf16[4,128,128]{2,1,0:T(8,128)(2,1)S(1)} %pad_maximum_fusion.4.col_feats), custom_call_target="tpu_custom_call" | custom-call | tf_op jit(solution)/shard_map/pair_map/pallas_call | solution.py:478
  (58 shorter events, 0.5 us)
Async XLA Ops:
  0.0 1.0 copy-start
  1.0 10.4 %collective-permute-start.1 = (bf16[256,384]{1,0:T(8,128)(2,1)S(1)}, bf16[256,384]{1,0:T(8,128)(2,1)S(1)}, u32[]{:S(2)}, u32[]{:S(2)}) collective-permute-start(bf16[256,384]{1,0:T(8,128)(2,1)S(1)} %constant_dynamic-slice_fusion), channel_id=1, source_target_pairs={{0,6},{2,0},{4,2},{6,4},{1,7},{3,1},{5,3},{7,5},{8,14},{10,8},{12,... | collective-permute-start | bytes 589832 | tf_op jit(solution)/shard_map/ppermute | solution.py:331
  6.1 9.3 %collective-permute-start = (bf16[256,384]{1,0:T(8,128)(2,1)S(1)}, bf16[256,384]{1,0:T(8,128)(2,1)S(1)}, u32[]{:S(2)}, u32[]{:S(2)}) collective-permute-start(bf16[256,384]{1,0:T(8,128)(2,1)S(1)} %constant_dynamic-slice_fusion), channel_id=1, source_target_pairs={{0,2},{2,4},{4,6},{6,0},{1,3},{3,5},{5,7},{7,1},{8,10},{10,12},{12... | collective-permute-start | bytes 589832 | tf_op jit(solution)/shard_map/ppermute | solution.py:331
  6.2 31.6 %copy-start.8 = (f32[384]{0:T(512)S(1)}, f32[384]{0:T(512)}, u32[]{:S(2)}) copy-start(f32[384]{0:T(512)} %param.11) | copy-start | bytes 4612
  6.2 31.6 %copy-start.7 = (f32[3,384]{1,0:T(4,128)S(1)}, f32[3,384]{1,0:T(4,128)}, u32[]{:S(2)}) copy-start(f32[3,384]{1,0:T(4,128)} %param.10) | copy-start | bytes 13828
  6.2 40.0 %copy-start.1 = (bf16[384,256]{1,0:T(8,128)(2,1)S(1)}, bf16[384,256]{1,0:T(8,128)(2,1)}, u32[]{:S(2)}) copy-start(bf16[384,256]{1,0:T(8,128)(2,1)} %refs_1_.3) | copy-start | bytes 589828
  15.5 36.5 %copy-start.9 = (s32[4,2]{0,1:T(2,128)S(1)}, s32[4,2]{0,1:T(2,128)}, u32[]{:S(2)}) copy-start(s32[4,2]{0,1:T(2,128)} %param.9) | copy-start | bytes 100
  15.5 15.8 %collective-permute-start.5 = (bf16[3,256,384]{2,1,0:T(8,128)(2,1)S(1)}, bf16[3,256,384]{2,1,0:T(8,128)(2,1)}, u32[]{:S(2)}, u32[]{:S(2)}) collective-permute-start(bf16[3,256,384]{2,1,0:T(8,128)(2,1)S(1)} %pad_maximum_fusion.1), channel_id=1, source_target_pairs={{0,8},{8,0},{16,24},{24,16},{1,9},{9,1},{17,25},{25,17},{2,10},{10... | collective-permute-start | bytes 1769480 | tf_op jit(solution)/shard_map/ppermute | solution.py:332
  17.1 18.1 %collective-permute-start.2 = (bf16[3,256,384]{2,1,0:T(8,128)(2,1)S(1)}, bf16[3,256,384]{2,1,0:T(8,128)(2,1)S(1)}, u32[]{:S(2)}, u32[]{:S(2)}) collective-permute-start(bf16[3,256,384]{2,1,0:T(8,128)(2,1)S(1)} %pad_maximum_fusion.1), channel_id=1, source_target_pairs={{0,16},{8,24},{16,0},{24,8},{1,17},{9,25},{17,1},{25,9},{2,18},{10... | collective-permute-start | bytes 1769480 | tf_op jit(solution)/shard_map/ppermute | solution.py:332
  18.6 10.5 %collective-permute-start.3 = (bf16[256,384]{1,0:T(8,128)(2,1)S(1)}, bf16[256,384]{1,0:T(8,128)(2,1)}, u32[]{:S(2)}, u32[]{:S(2)}) collective-permute-start(bf16[256,384]{1,0:T(8,128)(2,1)S(1)} %constant_dynamic-slice_fusion), channel_id=1, source_target_pairs={{0,4},{2,6},{4,0},{6,2},{1,5},{3,7},{5,1},{7,3},{8,12},{10,14},{12... | collective-permute-start | bytes 589832 | tf_op jit(solution)/shard_map/ppermute | solution.py:331
  29.1 6.0 %collective-permute-start.6 = (bf16[1,256,384]{2,1,0:T(8,128)(2,1)}, bf16[1,256,384]{2,1,0:T(8,128)(2,1)S(1)}, u32[]{:S(2)}, u32[]{:S(2)}) collective-permute-start(bf16[1,256,384]{2,1,0:T(8,128)(2,1)} %bitcast.13), channel_id=1, source_target_pairs={{0,8},{8,0},{16,24},{24,16},{1,9},{9,1},{17,25},{25,17},{2,10},{10... | collective-permute-start | bytes 589832 | tf_op jit(solution)/shard_map/ppermute | solution.py:332
  29.6 5.9 %collective-permute-start.4 = (bf16[1,256,384]{2,1,0:T(8,128)(2,1)}, bf16[1,256,384]{2,1,0:T(8,128)(2,1)S(1)}, u32[]{:S(2)}, u32[]{:S(2)}) collective-permute-start(bf16[1,256,384]{2,1,0:T(8,128)(2,1)} %bitcast.13), channel_id=1, source_target_pairs={{0,16},{8,24},{16,0},{24,8},{1,17},{9,25},{17,1},{25,9},{2,18},{10... | collective-permute-start | bytes 589832 | tf_op jit(solution)/shard_map/ppermute | solution.py:332
  31.2 20.6 %copy-start.6 = (bf16[4,256,384]{2,1,0:T(8,128)(2,1)}, bf16[4,256,384]{2,1,0:T(8,128)(2,1)S(1)}, u32[]{:S(2)}) copy-start(bf16[4,256,384]{2,1,0:T(8,128)(2,1)S(1)} %pad_maximum_fusion.refs_1_) | copy-start | bytes 2359300
  31.2 15.3 %collective-permute-start.8 = (bf16[4,256,384]{2,1,0:T(8,128)(2,1)S(1)}, bf16[4,256,384]{2,1,0:T(8,128)(2,1)S(1)}, u32[]{:S(2)}, u32[]{:S(2)}) collective-permute-start(bf16[4,256,384]{2,1,0:T(8,128)(2,1)S(1)} %pad_maximum_fusion.refs_1_), channel_id=1, source_target_pairs={{0,1},{1,0},{2,3},{3,2},{4,5},{5,4},{6,7},{7,6},{8,9},{9,8},{10,11... | collective-permute-start | bytes 2359304 | tf_op jit(solution)/shard_map/ppermute | solution.py:329
  35.1 34.2 %copy-start.5 = (bf16[4,256,384]{2,1,0:T(8,128)(2,1)}, bf16[4,256,384]{2,1,0:T(8,128)(2,1)S(1)}, u32[]{:S(2)}) copy-start(bf16[4,256,384]{2,1,0:T(8,128)(2,1)S(1)} %constant_dynamic-update-slice_fusion.2.refs_2_) | copy-start | bytes 2359300
  35.6 33.8 %copy-start.4 = (bf16[4,256,384]{2,1,0:T(8,128)(2,1)}, bf16[4,256,384]{2,1,0:T(8,128)(2,1)S(1)}, u32[]{:S(2)}) copy-start(bf16[4,256,384]{2,1,0:T(8,128)(2,1)S(1)} %constant_dynamic-update-slice_fusion.refs_3_) | copy-start | bytes 2359300
  35.7 12.2 %collective-permute-start.7 = (bf16[4,256,384]{2,1,0:T(8,128)(2,1)S(1)}, bf16[4,256,384]{2,1,0:T(8,128)(2,1)}, u32[]{:S(2)}, u32[]{:S(2)}) collective-permute-start(bf16[4,256,384]{2,1,0:T(8,128)(2,1)S(1)} %broadcast_select_fusion), channel_id=1, source_target_pairs={{0,8},{1,17},{8,0},{9,25},{16,24},{17,1},{24,16},{25,9},{2,10},{3,... | collective-permute-start | bytes 2359304 | tf_op jit(solution)/shard_map/ppermute | solution.py:342
  37.2 10.6 %collective-permute-start.10 = (bf16[4,256,384]{2,1,0:T(8,128)(2,1)S(1)}, bf16[4,256,384]{2,1,0:T(8,128)(2,1)S(1)}, u32[]{:S(2)}, u32[]{:S(2)}) collective-permute-start(bf16[4,256,384]{2,1,0:T(8,128)(2,1)S(1)} %constant_dynamic-update-slice_fusion.refs_3_), channel_id=1, source_target_pairs={{0,1},{1,0},{2,3},{3,2},{4,5},{5,4},{6,7},{7,6},{8,9},{9,8},{10,11... | collective-permute-start | bytes 2359304 | tf_op jit(solution)/shard_map/ppermute | solution.py:329
  37.2 10.6 %collective-permute-start.9 = (bf16[4,256,384]{2,1,0:T(8,128)(2,1)S(1)}, bf16[4,256,384]{2,1,0:T(8,128)(2,1)S(1)}, u32[]{:S(2)}, u32[]{:S(2)}) collective-permute-start(bf16[4,256,384]{2,1,0:T(8,128)(2,1)S(1)} %constant_dynamic-update-slice_fusion.2.refs_2_), channel_id=1, source_target_pairs={{0,1},{1,0},{2,3},{3,2},{4,5},{5,4},{6,7},{7,6},{8,9},{9,8},{10,11... | collective-permute-start | bytes 2359304 | tf_op jit(solution)/shard_map/ppermute | solution.py:329
  37.8 3.7 %collective-permute-start.11 = (f32[4,384]{1,0:T(4,128)S(1)}, f32[4,384]{1,0:T(4,128)S(1)}, u32[]{:S(2)}, u32[]{:S(2)}) collective-permute-start(f32[4,384]{1,0:T(4,128)S(1)} %pad_maximum_fusion.9), channel_id=1, source_target_pairs={{0,2},{2,0},{4,6},{6,4},{1,3},{3,1},{5,7},{7,5},{8,10},{10,8},{12,... | collective-permute-start | bytes 18440 | tf_op jit(solution)/shard_map/ppermute | solution.py:345
  41.5 4.7 %collective-permute-start.12 = (f32[8,384]{1,0:T(8,128)S(1)}, f32[8,384]{1,0:T(8,128)S(1)}, u32[]{:S(2)}, u32[]{:S(2)}) collective-permute-start(f32[8,384]{1,0:T(8,128)S(1)} %pad_maximum_fusion.8), channel_id=1, source_target_pairs={{0,4},{2,6},{4,0},{6,2},{1,5},{3,7},{5,1},{7,3},{8,12},{10,14},{12... | collective-permute-start | bytes 36872 | tf_op jit(solution)/shard_map/ppermute | solution.py:345
  46.1 5.7 %collective-permute-start.14 = (bf16[1,384,256]{2,1,0:T(8,128)(2,1)S(1)}, bf16[1,384,256]{2,1,0:T(8,128)(2,1)S(1)}, u32[]{:S(2)}, u32[]{:S(2)}) collective-permute-start(bf16[1,384,256]{2,1,0:T(8,128)(2,1)S(1)} %bitcast.38), channel_id=1, source_target_pairs={{0,2},{2,0},{4,6},{6,4},{1,3},{3,1},{5,7},{7,5},{8,10},{10,8},{12,... | collective-permute-start | bytes 589832 | tf_op jit(solution)/shard_map/ppermute | solution.py:319
  46.5 5.3 %copy-start.10 = (bf16[4,256,384]{2,1,0:T(8,128)(2,1)}, bf16[4,256,384]{2,1,0:T(8,128)(2,1)S(1)}, u32[]{:S(2)}) copy-start(bf16[4,256,384]{2,1,0:T(8,128)(2,1)S(1)} %collective-permute-done.8.refs_5_) | copy-start | bytes 2359300
  47.8 0.9 copy-start.11
  47.8 1.1 copy-start.12
  47.8 21.4 %collective-permute-start.13 = (bf16[4,256,384]{2,1,0:T(8,128)(2,1)}, bf16[4,256,384]{2,1,0:T(8,128)(2,1)}, u32[]{:S(2)}, u32[]{:S(2)}) collective-permute-start(bf16[4,256,384]{2,1,0:T(8,128)(2,1)} %collective-permute-done.7.refs_4_), channel_id=1, source_target_pairs={{0,1},{1,0},{2,3},{3,2},{4,5},{5,4},{6,7},{7,6},{8,9},{9,8},{10,11... | collective-permute-start | bytes 2359304 | tf_op jit(solution)/shard_map/ppermute | solution.py:329
  51.9 17.4 %collective-permute-start.15 = (bf16[2,384,256]{2,1,0:T(8,128)(2,1)S(1)}, bf16[2,384,256]{2,1,0:T(8,128)(2,1)S(1)}, u32[]{:S(2)}, u32[]{:S(2)}) collective-permute-start(bf16[2,384,256]{2,1,0:T(8,128)(2,1)S(1)} %pad_maximum_fusion.2), channel_id=1, source_target_pairs={{0,4},{2,6},{4,0},{6,2},{1,5},{3,7},{5,1},{7,3},{8,12},{10,14},{12... | collective-permute-start | bytes 1179656 | tf_op jit(solution)/shard_map/ppermute | solution.py:319
  69.3 16.5 %copy-start.3 = (bf16[384,1536]{1,0:T(8,128)(2,1)S(1)}, bf16[384,1536]{1,0:T(8,128)(2,1)}, u32[]{:S(2)}) copy-start(bf16[384,1536]{1,0:T(8,128)(2,1)} %refs_0_.1) | copy-start | bytes 3538948
  97.8 8.3 %collective-permute-start.16 = (bf16[128,256]{1,0:T(8,128)(2,1)S(1)}, bf16[128,256]{1,0:T(8,128)(2,1)S(1)}, u32[]{:S(2)}, u32[]{:S(2)}) collective-permute-start(bf16[128,256]{1,0:T(8,128)(2,1)S(1)} %get-tuple-element.25), channel_id=1, source_target_pairs={{0,2},{2,4},{4,6},{6,0},{1,3},{3,5},{5,7},{7,1},{8,10},{10,12},{12... | collective-permute-start | bytes 196616 | tf_op jit(solution)/shard_map/ppermute | solution.py:459
  97.9 8.3 %collective-permute-start.18 = (bf16[128,256]{1,0:T(8,128)(2,1)S(1)}, bf16[128,256]{1,0:T(8,128)(2,1)S(1)}, u32[]{:S(2)}, u32[]{:S(2)}) collective-permute-start(bf16[128,256]{1,0:T(8,128)(2,1)S(1)} %get-tuple-element.26), channel_id=1, source_target_pairs={{0,6},{2,0},{4,2},{6,4},{1,7},{3,1},{5,3},{7,5},{8,14},{10,8},{12,... | collective-permute-start | bytes 196616 | tf_op jit(solution)/shard_map/ppermute | solution.py:459
  101.7 5.2 %collective-permute-start.17 = (bf16[128,256]{1,0:T(8,128)(2,1)S(1)}, bf16[128,256]{1,0:T(8,128)(2,1)S(1)}, u32[]{:S(2)}, u32[]{:S(2)}) collective-permute-start(bf16[128,256]{1,0:T(8,128)(2,1)S(1)} %get-tuple-element.27), channel_id=1, source_target_pairs={{0,4},{2,6},{4,0},{6,2},{1,5},{3,7},{5,1},{7,3},{8,12},{10,14},{12... | collective-permute-start | bytes 196616 | tf_op jit(solution)/shard_map/ppermute | solution.py:459
  101.7 21.4 %copy-start.2 = (f32[16,128]{1,0:T(8,128)S(1)}, f32[16,128]{1,0:T(8,128)}, u32[]{:S(2)}) copy-start(f32[16,128]{1,0:T(8,128)} %dist_table.1) | copy-start | bytes 24580
  106.9 3.5 %collective-permute-start.19 = (bf16[128,128]{1,0:T(8,128)(2,1)S(1)}, bf16[128,128]{1,0:T(8,128)(2,1)S(1)}, u32[]{:S(2)}, u32[]{:S(2)}) collective-permute-start(bf16[128,128]{1,0:T(8,128)(2,1)S(1)} %get-tuple-element.29), channel_id=1, source_target_pairs={{0,0},{2,8},{4,16},{6,24},{8,2},{10,10},{12,18},{14,26},{16,4},{18... | collective-permute-start | bytes 98312 | tf_op jit(solution)/shard_map/ppermute | solution.py:460
  107.6 6.0 %collective-permute-start.22 = (bf16[1,128,128]{2,1,0:T(8,128)(2,1)S(1)}, bf16[1,128,128]{2,1,0:T(8,128)(2,1)S(1)}, u32[]{:S(2)}, u32[]{:S(2)}) collective-permute-start(bf16[1,128,128]{2,1,0:T(8,128)(2,1)S(1)} %get-tuple-element.28), channel_id=1, source_target_pairs={{0,8},{8,0},{16,24},{24,16},{1,9},{9,1},{17,25},{25,17},{2,10},{10... | collective-permute-start | bytes 98312 | tf_op jit(solution)/shard_map/ppermute | solution.py:319
  110.4 6.2 %collective-permute-start.20 = (bf16[1,128,128]{2,1,0:T(8,128)(2,1)S(1)}, bf16[1,128,128]{2,1,0:T(8,128)(2,1)S(1)}, u32[]{:S(2)}, u32[]{:S(2)}) collective-permute-start(bf16[1,128,128]{2,1,0:T(8,128)(2,1)S(1)} %bitcast.45), channel_id=1, source_target_pairs={{0,2},{2,0},{4,6},{6,4},{1,3},{3,1},{5,7},{7,5},{8,10},{10,8},{12,... | collective-permute-start | bytes 98312 | tf_op jit(solution)/shard_map/ppermute | solution.py:319
  113.6 7.2 %collective-permute-start.23 = (bf16[2,128,128]{2,1,0:T(8,128)(2,1)S(1)}, bf16[2,128,128]{2,1,0:T(8,128)(2,1)S(1)}, u32[]{:S(2)}, u32[]{:S(2)}) collective-permute-start(bf16[2,128,128]{2,1,0:T(8,128)(2,1)S(1)} %pad_maximum_fusion.6), channel_id=1, source_target_pairs={{0,16},{8,24},{16,0},{24,8},{1,17},{9,25},{17,1},{25,9},{2,18},{10... | collective-permute-start | bytes 196616 | tf_op jit(solution)/shard_map/ppermute | solution.py:319
  116.6 6.5 %collective-permute-start.21 = (bf16[2,128,128]{2,1,0:T(8,128)(2,1)S(1)}, bf16[2,128,128]{2,1,0:T(8,128)(2,1)S(1)}, u32[]{:S(2)}, u32[]{:S(2)}) collective-permute-start(bf16[2,128,128]{2,1,0:T(8,128)(2,1)S(1)} %pad_maximum_fusion.5), channel_id=1, source_target_pairs={{0,4},{2,6},{4,0},{6,2},{1,5},{3,7},{5,1},{7,3},{8,12},{10,14},{12... | collective-permute-start | bytes 196616 | tf_op jit(solution)/shard_map/ppermute | solution.py:319
